TPU v7x, 512 devices: a whole 4x4x16 slice. The times are simulated.
512 devices in a mesh: fsdp: 64 (over x, z_lo, core), col: 8 (over z_hi, y).
Axes of the slice: x: 4, y: 4, z: 16 (z_hi: 2, z_lo: 8; z = z_hi * 8 + z_lo), core: 2. Of those that a mesh axis runs over, the one named last changes fastest.
Arguments:
- codes: bfloat16 [8192, 26624], P('fsdp', 'col'), may hold values from -96 to 96
- scales: float32 [64, 208], P('fsdp', 'col'), may hold values from 0.01 to 0.1
- factors: float32 [7, 8192, 64], P(None, 'fsdp'), may hold values from -0.225 to 0.225
- upstream: bfloat16 [8192, 26624], P('fsdp', 'col'), may hold values from -0.036621094 to 0.036621094
Outputs:
- factor_grads: float32 [7, 8192, 64], P(None, 'fsdp')
All inputs are finite; a program needn't handle non-finite values.
Results may differ from a plain program's by a relative error of at most 0.02.
Values may be sent and summed in bfloat16 or wider, within the bound.
No kernel may reach another device: no remote copies, remote signals or barrier semaphores. Data moves between devices by JAX's collectives and lax.ppermute only.
A program may use at most 64 MiB of HBM per device.

v0:
```python
import jax
import jax.numpy as jnp
from jax import lax
from jax.sharding import PartitionSpec as P


def partner(block, axis, bit):
    count = lax.axis_size(axis)
    route = []
    for low in range(count):
        high = low | 1 << bit
        if high != low and high < count:
            route += [(low, high), (high, low)]
    return lax.ppermute(block, axis, route)


def rows_eye(first, count, distance, block):
    half = block // 2
    rows = first + jnp.arange(count, dtype=jnp.int32)
    pick = rows // distance % 2 * half + rows % half
    return (jnp.arange(block, dtype=jnp.int32)[None, :] == pick[:, None]).astype(jnp.float32)


def source_rows(first, count, distance, block):
    half = block // 2
    rows = first + jnp.arange(count, dtype=jnp.int32)
    inputs = jnp.arange(block, dtype=jnp.int32)
    group = rows // (2 * distance)
    part = rows % distance // half
    return (
        2 * distance * group[:, None]
        + distance * (inputs // half)[None, :]
        + half * part[:, None]
        + (inputs % half)[None, :]
    )


def dense_mixing(mixing, columns, width):
    onehot = columns[:, :, None] == jnp.arange(width, dtype=jnp.int32)[None, None, :]
    spread = jnp.where(onehot, mixing[:, :, None], jnp.zeros((), jnp.bfloat16))
    return jnp.sum(spread.astype(jnp.float32), axis=1).astype(jnp.bfloat16)


def left_product(matrix, grad):
    return lax.dot_general(
        matrix, grad, (((0,), (0,)), ((), ())), preferred_element_type=jnp.float32
    )


def local_scores(grad, values, distance, half):
    rows, wide = grad.shape
    groups = rows // (2 * distance)
    parts = distance // half
    grads = grad.reshape(groups, 2, parts, half, wide)
    vecs = values.reshape(groups, 2, parts, half, wide)
    out = jnp.einsum("ghqtc,gHqsc->ghqtHs", grads, vecs, preferred_element_type=jnp.float32)
    return out.reshape(rows, 2 * half)


def half_scores(grad, values, half):
    rows, wide = grad.shape
    grads = grad.reshape(rows // half, half, wide)
    vecs = values.reshape(rows // half, half, wide)
    out = jnp.einsum("qtc,qsc->qts", grads, vecs, preferred_element_type=jnp.float32)
    return out.reshape(rows, half)


def per_device(codes, scales, factors, upstream):
    rows, wide = codes.shape
    levels = factors.shape[0]
    block = factors.shape[2]
    half = block // 2
    scale_side = rows // scales.shape[0]
    index = lax.axis_index("fsdp")
    first = index * rows
    base = codes.astype(jnp.float32).reshape(
        rows // scale_side, scale_side, wide // scale_side, scale_side
    )
    base = (base * scales[:, None, :, None]).reshape(rows, wide).astype(jnp.bfloat16)
    row_ids = first + jnp.arange(rows, dtype=jnp.int32)
    plans = []
    for level in range(levels):
        distance = half * 2**level
        mixing = (rows_eye(first, rows, distance, block) + factors[level]).astype(jnp.bfloat16)
        sources = source_rows(first, rows, distance, block)
        if distance < rows:
            columns = sources - first
            matrix = dense_mixing(mixing, columns, rows)
            plans.append((matrix, None, None, None))
        else:
            stride = distance // rows
            bit = stride.bit_length() - 1
            side = index // stride % 2
            partner_first = first + distance * (1 - 2 * side)
            inside = (sources >= first) & (sources < first + rows)
            columns = jnp.where(inside, sources - first, sources - partner_first + rows)
            matrix = dense_mixing(mixing, columns, 2 * rows)
            plans.append((matrix[:, :rows], matrix[:, rows:], bit, side))
    values = base
    saved = []
    partners = []
    for level in range(levels):
        distance = half * 2**level
        matrix, far_matrix, bit, side = plans[level]
        saved.append(values)
        if distance < rows:
            partners.append(None)
            values = jnp.dot(matrix, values, preferred_element_type=jnp.float32).astype(
                jnp.bfloat16
            )
        else:
            other = partner(values, "fsdp", bit)
            partners.append(other)
            total = jnp.dot(matrix, values, preferred_element_type=jnp.float32)
            total = total + jnp.dot(far_matrix, other, preferred_element_type=jnp.float32)
            values = total.astype(jnp.bfloat16)
    grad = upstream
    results = [None] * levels
    for level in reversed(range(levels)):
        distance = half * 2**level
        matrix, far_matrix, bit, side = plans[level]
        if distance < rows:
            dmix = local_scores(grad, saved[level], distance, half)
            if level > 0:
                upper_rows = (row_ids // distance % 2 == 1)[:, None]
                low_matrix = jnp.where(upper_rows, jnp.zeros((), jnp.bfloat16), matrix)
                high_matrix = jnp.where(upper_rows, matrix, jnp.zeros((), jnp.bfloat16))
                lower = left_product(low_matrix, grad).astype(jnp.bfloat16)
                upper = left_product(high_matrix, grad).astype(jnp.bfloat16)
                grad = (lower.astype(jnp.float32) + upper.astype(jnp.float32)).astype(jnp.bfloat16)
        else:
            own_part = half_scores(grad, saved[level], half)
            far_part = half_scores(grad, partners[level], half)
            first_half = jnp.where(side == 0, own_part, far_part)
            second_half = jnp.where(side == 0, far_part, own_part)
            dmix = jnp.concatenate([first_half, second_half], axis=1)
            near_term = left_product(matrix, grad).astype(jnp.bfloat16)
            got_grad, got_matrix = partner((grad, far_matrix), "fsdp", bit)
            far_term = left_product(got_matrix, got_grad).astype(jnp.bfloat16)
            grad = (near_term.astype(jnp.float32) + far_term.astype(jnp.float32)).astype(
                jnp.bfloat16
            )
        results[level] = dmix
    stacked = jnp.stack(results)
    stacked = lax.psum(stacked, "col")
    return stacked


def solution(mesh):
    return jax.shard_map(
        per_device,
        mesh=mesh,
        in_specs=(P("fsdp", "col"), P("fsdp", "col"), P(None, "fsdp", None), P("fsdp", "col")),
        out_specs=P(None, "fsdp", None),
        check_vma=False,
    )
```

profile of v0, /device:TPU:24, one launch (start us, length us, event | category | flops | bytes accessed | tf_op | source)
XLA Modules:
  0.0 487.3 jit_solution(10612959449377692866)
XLA Ops:
  8.1 2.8 fusion.33
  11.0 3.4 collective-permute-start
  14.4 2.4 collective-permute-start.1
  17.3 2.8 fusion.34
  20.8 9.1 %collective-permute-start.2 = (bf16[128,128]{1,0:T(8,128)(2,1)}, bf16[128,128]{1,0:T(8,128)(2,1)}, u32[]{:S(2)}, u32[]{:S(2)}) collective-permute-start(bf16[128,128]{1,0:T(8,128)(2,1)} %slice.74), channel_id=1, source_target_pairs={{0,64},{64,0},{8,72},{72,8},{16,80},{80,16},{24,88},{88,24},{32,96... | collective-permute-start | bytes 98312 | tf_op jit(solution)/shard_map/ppermute | solution.py:14
  30.1 2.8 fusion.35
  33.6 5.2 %collective-permute-start.4 = (bf16[128,128]{1,0:T(8,128)(2,1)}, bf16[128,128]{1,0:T(8,128)(2,1)}, u32[]{:S(2)}, u32[]{:S(2)}) collective-permute-start(bf16[128,128]{1,0:T(8,128)(2,1)} %slice.75), channel_id=1, source_target_pairs={{0,32},{32,0},{8,40},{40,8},{16,48},{48,16},{24,56},{56,24},{64,96... | collective-permute-start | bytes 98312 | tf_op jit(solution)/shard_map/ppermute | solution.py:14
  39.4 2.8 fusion.41
  42.2 2.8 fusion.40
  48.0 2.8 fusion.37
  54.3 2.8 fusion.36
  58.4 3.9 collective-permute-start.6
  62.4 2.2 fusion.31
  64.5 1.9 collective-permute-start.3
  67.4 2.1 collective-permute-start.11
  70.4 2.1 collective-permute-start.8
  72.4 73.0 %collective-permute-done.3 = bf16[128,3328]{1,0:T(8,128)(2,1)S(1)} collective-permute-done((bf16[128,3328]{1,0:T(8,128)(2,1)S(1)}, bf16[128,3328]{1,0:T(8,128)(2,1)S(1)}, u32[]{:S(2)}, u32[]{:S(2)}) %collective-permute-start.3) | collective-permute-done | bytes 852000 | tf_op jit(solution)/shard_map/ppermute | solution.py:14
  146.7 2.1 collective-permute-start.5
  149.1 4.8 collective-permute-start.12
  155.1 45.1 %collective-permute-done.5 = bf16[128,3328]{1,0:T(8,128)(2,1)S(1)} collective-permute-done((bf16[128,3328]{1,0:T(8,128)(2,1)S(1)}, bf16[128,3328]{1,0:T(8,128)(2,1)S(1)}, u32[]{:S(2)}, u32[]{:S(2)}) %collective-permute-start.5) | collective-permute-done | bytes 852000 | tf_op jit(solution)/shard_map/ppermute | solution.py:14
  201.4 1.9 collective-permute-start.7
  205.0 13.5 %collective-permute-done.12 = bf16[128,3328]{1,0:T(8,128)(2,1)S(1)} collective-permute-done((bf16[128,3328]{1,0:T(8,128)(2,1)S(1)}, bf16[128,3328]{1,0:T(8,128)(2,1)S(1)}, u32[]{:S(2)}, u32[]{:S(2)}) %collective-permute-start.12) | collective-permute-done | bytes 852000 | tf_op jit(solution)/shard_map/ppermute | solution.py:14
  219.8 6.7 %collective-permute-start.13 = (bf16[128,3328]{1,0:T(8,128)(2,1)}, bf16[128,3328]{1,0:T(8,128)(2,1)}, u32[]{:S(2)}, u32[]{:S(2)}) collective-permute-start(bf16[128,3328]{1,0:T(8,128)(2,1)} %fusion.7), channel_id=1, source_target_pairs={{0,64},{64,0},{8,72},{72,8},{16,80},{80,16},{24,88},{88,24},{32,96... | collective-permute-start | bytes 2555912 | tf_op jit(solution)/shard_map/ppermute | solution.py:14
  227.9 2.7 fusion.76
  231.6 2.1 fusion.127
  239.8 2.3 fusion.19
  244.0 56.6 %collective-permute-done.13 = bf16[128,3328]{1,0:T(8,128)(2,1)} collective-permute-done((bf16[128,3328]{1,0:T(8,128)(2,1)}, bf16[128,3328]{1,0:T(8,128)(2,1)}, u32[]{:S(2)}, u32[]{:S(2)}) %collective-permute-start.13) | collective-permute-done | bytes 852000 | tf_op jit(solution)/shard_map/ppermute | solution.py:14
  300.6 2.5 fusion.8
  303.0 3.7 collective-permute-start.14
  312.6 2.2 fusion.15
  318.6 7.6 %collective-permute-done.14 = bf16[128,3328]{1,0:T(8,128)(2,1)} collective-permute-done((bf16[128,3328]{1,0:T(8,128)(2,1)}, bf16[128,3328]{1,0:T(8,128)(2,1)}, u32[]{:S(2)}, u32[]{:S(2)}) %collective-permute-start.14) | collective-permute-done | bytes 852000 | tf_op jit(solution)/shard_map/ppermute | solution.py:14
  328.9 149.9 %all-reduce.2.cloned.1.call-done = f32[7,128,64]{1,2,0:T(8,128)} async-done(((f32[7,128,64]{1,2,0:T(8,128)}), f32[7,128,64]{1,2,0:T(8,128)}) %all-reduce.2.cloned.1.call-update) | async-done | bytes 229392 | tf_op jit(solution)/shard_map/psum | solution.py:145
  (155 shorter events, 44.1 us)
Async XLA Ops:
  6.5 32.2 %copy-start = (f32[1,26]{1,0:T(1,128)S(1)}, f32[1,26]{1,0:T(1,128)}, u32[]{:S(2)}) copy-start(f32[1,26]{1,0:T(1,128)} %param.5) | copy-start | bytes 316
  6.5 32.7 %copy-start.10 = (bf16[128,3328]{1,0:T(8,128)(2,1)S(1)}, bf16[128,3328]{1,0:T(8,128)(2,1)}, u32[]{:S(2)}) copy-start(bf16[128,3328]{1,0:T(8,128)(2,1)} %param.4) | copy-start | bytes 2555908
  6.5 472.3 %all-reduce.2.cloned.1.call-start = ((), (), s32[]{:S(2)}) async-start(), calls=%async_computation | async-start | bytes 458752 | tf_op jit(solution)/shard_map/psum | solution.py:145
  11.0 47.4 %collective-permute-start = (bf16[128,128]{1,0:T(8,128)(2,1)S(1)}, bf16[128,128]{1,0:T(8,128)(2,1)S(1)}, u32[]{:S(2)}, u32[]{:S(2)}) collective-permute-start(bf16[128,128]{1,0:T(8,128)(2,1)S(1)} %slice.73), channel_id=1, source_target_pairs={{0,128},{128,0},{8,136},{136,8},{16,144},{144,16},{24,152},{152,24... | collective-permute-start | bytes 98312 | tf_op jit(solution)/shard_map/ppermute | solution.py:14
  14.4 48.0 %collective-permute-start.1 = (bf16[128,3328]{1,0:T(8,128)(2,1)}, bf16[128,3328]{1,0:T(8,128)(2,1)}, u32[]{:S(2)}, u32[]{:S(2)}) collective-permute-start(bf16[128,3328]{1,0:T(8,128)(2,1)} %param.7), channel_id=1, source_target_pairs={{0,128},{128,0},{8,136},{136,8},{16,144},{144,16},{24,152},{152,24... | collective-permute-start | bytes 2555912 | tf_op jit(solution)/shard_map/ppermute | solution.py:14
  20.8 49.6 %collective-permute-start.2 = (bf16[128,128]{1,0:T(8,128)(2,1)}, bf16[128,128]{1,0:T(8,128)(2,1)}, u32[]{:S(2)}, u32[]{:S(2)}) collective-permute-start(bf16[128,128]{1,0:T(8,128)(2,1)} %slice.74), channel_id=1, source_target_pairs={{0,64},{64,0},{8,72},{72,8},{16,80},{80,16},{24,88},{88,24},{32,96... | collective-permute-start | bytes 98312 | tf_op jit(solution)/shard_map/ppermute | solution.py:14
  32.9 12.1 %copy-start.11 = (bf16[128,256]{1,0:T(8,128)(2,1)}, bf16[128,256]{1,0:T(8,128)(2,1)S(1)}, u32[]{:S(2)}) copy-start(bf16[128,256]{1,0:T(8,128)(2,1)S(1)} %fusion.35) | copy-start | bytes 196612
  33.6 121.6 %collective-permute-start.4 = (bf16[128,128]{1,0:T(8,128)(2,1)}, bf16[128,128]{1,0:T(8,128)(2,1)}, u32[]{:S(2)}, u32[]{:S(2)}) collective-permute-start(bf16[128,128]{1,0:T(8,128)(2,1)} %slice.75), channel_id=1, source_target_pairs={{0,32},{32,0},{8,40},{40,8},{16,48},{48,16},{24,56},{56,24},{64,96... | collective-permute-start | bytes 98312 | tf_op jit(solution)/shard_map/ppermute | solution.py:14
  39.4 6.4 %copy-start.2 = (bf16[128,3328]{1,0:T(8,128)(2,1)}, bf16[128,3328]{1,0:T(8,128)(2,1)S(1)}, u32[]{:S(2)}) copy-start(bf16[128,3328]{1,0:T(8,128)(2,1)S(1)} %multiply_convert_fusion) | copy-start | bytes 2555908
  42.2 3.6 copy-start.15
  45.0 5.8 %copy-start.1 = (bf16[128,3328]{1,0:T(8,128)(2,1)S(1)}, bf16[128,3328]{1,0:T(8,128)(2,1)}, u32[]{:S(2)}) copy-start(bf16[128,3328]{1,0:T(8,128)(2,1)} %param.7) | copy-start | bytes 2555908
  45.9 20.6 %collective-permute-start.10 = (bf16[128,3328]{1,0:T(8,128)(2,1)S(1)}, bf16[128,3328]{1,0:T(8,128)(2,1)S(1)}, u32[]{:S(2)}, u32[]{:S(2)}) collective-permute-start(bf16[128,3328]{1,0:T(8,128)(2,1)S(1)} %convolution_convert_fusion), channel_id=1, source_target_pairs={{0,8},{8,0},{16,24},{24,16},{32,40},{40,32},{48,56},{56,48},{64,72... | collective-permute-start | bytes 2555912 | tf_op jit(solution)/shard_map/ppermute | solution.py:14
  57.1 5.2 %copy-start.13 = (bf16[128,256]{1,0:T(8,128)(2,1)}, bf16[128,256]{1,0:T(8,128)(2,1)S(1)}, u32[]{:S(2)}) copy-start(bf16[128,256]{1,0:T(8,128)(2,1)S(1)} %fusion.36) | copy-start | bytes 196612
  58.4 8.1 %copy-start.4 = (f32[128,3328]{1,0:T(8,128)S(1)}, f32[128,3328]{1,0:T(8,128)}, u32[]{:S(2)}) copy-start(f32[128,3328]{1,0:T(8,128)} %fusion.85) | copy-start | bytes 5111812
  58.4 4.0 copy-start.23
  58.4 181.4 %collective-permute-start.6 = (bf16[128,128]{1,0:T(8,128)(2,1)}, bf16[128,128]{1,0:T(8,128)(2,1)}, u32[]{:S(2)}, u32[]{:S(2)}) collective-permute-start(bf16[128,128]{1,0:T(8,128)(2,1)} %slice.76), channel_id=1, source_target_pairs={{0,16},{16,0},{8,24},{24,8},{32,48},{48,32},{40,56},{56,40},{64,80... | collective-permute-start | bytes 98312 | tf_op jit(solution)/shard_map/ppermute | solution.py:14
  64.5 81.0 %collective-permute-start.3 = (bf16[128,3328]{1,0:T(8,128)(2,1)S(1)}, bf16[128,3328]{1,0:T(8,128)(2,1)S(1)}, u32[]{:S(2)}, u32[]{:S(2)}) collective-permute-start(bf16[128,3328]{1,0:T(8,128)(2,1)S(1)} %fusion.31), channel_id=1, source_target_pairs={{0,64},{64,0},{8,72},{72,8},{16,80},{80,16},{24,88},{88,24},{32,96... | collective-permute-start | bytes 2555912 | tf_op jit(solution)/shard_map/ppermute | solution.py:14
  67.4 81.3 %collective-permute-start.11 = (bf16[128,3328]{1,0:T(8,128)(2,1)S(1)}, bf16[128,3328]{1,0:T(8,128)(2,1)S(1)}, u32[]{:S(2)}, u32[]{:S(2)}) collective-permute-start(bf16[128,3328]{1,0:T(8,128)(2,1)S(1)} %fusion.5), channel_id=1, source_target_pairs={{0,16},{16,0},{8,24},{24,8},{32,48},{48,32},{40,56},{56,40},{64,80... | collective-permute-start | bytes 2555912 | tf_op jit(solution)/shard_map/ppermute | solution.py:14
  70.4 242.2 %collective-permute-start.8 = (bf16[128,128]{1,0:T(8,128)(2,1)}, bf16[128,128]{1,0:T(8,128)(2,1)}, u32[]{:S(2)}, u32[]{:S(2)}) collective-permute-start(bf16[128,128]{1,0:T(8,128)(2,1)} %slice.77), channel_id=1, source_target_pairs={{0,8},{8,0},{16,24},{24,16},{32,40},{40,32},{48,56},{56,48},{64,72... | collective-permute-start | bytes 98312 | tf_op jit(solution)/shard_map/ppermute | solution.py:14
  146.7 7.3 %copy-start.12 = (bf16[128,256]{1,0:T(8,128)(2,1)S(1)}, bf16[128,256]{1,0:T(8,128)(2,1)}, u32[]{:S(2)}) copy-start(bf16[128,256]{1,0:T(8,128)(2,1)} %copy-done.11) | copy-start | bytes 196612
  146.7 53.6 %collective-permute-start.5 = (bf16[128,3328]{1,0:T(8,128)(2,1)S(1)}, bf16[128,3328]{1,0:T(8,128)(2,1)S(1)}, u32[]{:S(2)}, u32[]{:S(2)}) collective-permute-start(bf16[128,3328]{1,0:T(8,128)(2,1)S(1)} %fusion.27), channel_id=1, source_target_pairs={{0,32},{32,0},{8,40},{40,8},{16,48},{48,16},{24,56},{56,24},{64,96... | collective-permute-start | bytes 2555912 | tf_op jit(solution)/shard_map/ppermute | solution.py:14
  149.1 69.4 %collective-permute-start.12 = (bf16[128,3328]{1,0:T(8,128)(2,1)S(1)}, bf16[128,3328]{1,0:T(8,128)(2,1)S(1)}, u32[]{:S(2)}, u32[]{:S(2)}) collective-permute-start(bf16[128,3328]{1,0:T(8,128)(2,1)S(1)} %fusion.6), channel_id=1, source_target_pairs={{0,32},{32,0},{8,40},{40,8},{16,48},{48,16},{24,56},{56,24},{64,96... | collective-permute-start | bytes 2555912 | tf_op jit(solution)/shard_map/ppermute | solution.py:14
  201.4 38.4 %collective-permute-start.7 = (bf16[128,3328]{1,0:T(8,128)(2,1)S(1)}, bf16[128,3328]{1,0:T(8,128)(2,1)}, u32[]{:S(2)}, u32[]{:S(2)}) collective-permute-start(bf16[128,3328]{1,0:T(8,128)(2,1)S(1)} %fusion.23), channel_id=1, source_target_pairs={{0,16},{16,0},{8,24},{24,8},{32,48},{48,32},{40,56},{56,40},{64,80... | collective-permute-start | bytes 2555912 | tf_op jit(solution)/shard_map/ppermute | solution.py:14
  219.8 80.8 %collective-permute-start.13 = (bf16[128,3328]{1,0:T(8,128)(2,1)}, bf16[128,3328]{1,0:T(8,128)(2,1)}, u32[]{:S(2)}, u32[]{:S(2)}) collective-permute-start(bf16[128,3328]{1,0:T(8,128)(2,1)} %fusion.7), channel_id=1, source_target_pairs={{0,64},{64,0},{8,72},{72,8},{16,80},{80,16},{24,88},{88,24},{32,96... | collective-permute-start | bytes 2555912 | tf_op jit(solution)/shard_map/ppermute | solution.py:14
  239.8 60.8 %copy-start.5 = (f32[128,3328]{1,0:T(8,128)S(1)}, f32[128,3328]{1,0:T(8,128)}, u32[]{:S(2)}) copy-start(f32[128,3328]{1,0:T(8,128)} %fusion.76) | copy-start | bytes 5111812
  242.1 70.5 %collective-permute-start.9 = (bf16[128,3328]{1,0:T(8,128)(2,1)S(1)}, bf16[128,3328]{1,0:T(8,128)(2,1)}, u32[]{:S(2)}, u32[]{:S(2)}) collective-permute-start(bf16[128,3328]{1,0:T(8,128)(2,1)S(1)} %fusion.19), channel_id=1, source_target_pairs={{0,8},{8,0},{16,24},{24,16},{32,40},{40,32},{48,56},{56,48},{64,72... | collective-permute-start | bytes 2555912 | tf_op jit(solution)/shard_map/ppermute | solution.py:14
  303.0 4.1 copy-start.9
  303.0 23.2 %collective-permute-start.14 = (bf16[128,3328]{1,0:T(8,128)(2,1)}, bf16[128,3328]{1,0:T(8,128)(2,1)}, u32[]{:S(2)}, u32[]{:S(2)}) collective-permute-start(bf16[128,3328]{1,0:T(8,128)(2,1)} %fusion.8), channel_id=1, source_target_pairs={{0,128},{128,0},{8,136},{136,8},{16,144},{144,16},{24,152},{152,24... | collective-permute-start | bytes 2555912 | tf_op jit(solution)/shard_map/ppermute | solution.py:14
  318.3 9.8 %copy-start.19 = (f32[128,32]{0,1:T(8,128)S(1)}, f32[128,32]{0,1:T(8,128)}, u32[]{:S(2)}) copy-start(f32[128,32]{0,1:T(8,128)} %copy.85) | copy-start | bytes 49156
  318.3 9.8 %copy-start.21 = (f32[128,32]{0,1:T(8,128)S(1)}, f32[128,32]{0,1:T(8,128)}, u32[]{:S(2)}) copy-start(f32[128,32]{0,1:T(8,128)} %copy.84) | copy-start | bytes 49156
  318.3 9.8 %copy-start.20 = (f32[128,32]{0,1:T(8,128)S(1)}, f32[128,32]{0,1:T(8,128)}, u32[]{:S(2)}) copy-start(f32[128,32]{0,1:T(8,128)} %copy.87) | copy-start | bytes 49156
  318.3 9.8 %copy-start.22 = (f32[128,32]{0,1:T(8,128)S(1)}, f32[128,32]{0,1:T(8,128)}, u32[]{:S(2)}) copy-start(f32[128,32]{0,1:T(8,128)} %copy.86) | copy-start | bytes 49156
  (8 other events, 12.5 us)
Sparse Core Ops, SparseCore 0:
  329.0 149.7 all-reduce.1
where the time goes:
time: 489 us; the launch traced here: 487 us
  waiting for transfers between devices  346 us (71%)
  starting transfers between devices  53.2 us (11%)
  matrix products  37.7 us (8%)
  other arithmetic  21.3 us (4%)
  local copies, waits for them, and re-layouts  14.8 us (3%)
  between operations  14.4 us (3%)
    ppermute x15, waiting for transfers between devices, partner(): return lax.ppermute(block, axis, route)  196 us
    psum x1, waiting for transfers between devices, per_device(): stacked = lax.psum(stacked, 'col')  150 us
    ppermute x15, starting transfers between devices, partner(): return lax.ppermute(block, axis, route)  53.2 us
    reduce_sum x7, other arithmetic, dense_mixing(): return jnp.sum(spread.astype(jnp.float32), axis=1).astype(jnp.bfloat16)  19.8 us
    dot_general x12, matrix products, left_product(): lax.dot_general(matrix, grad, (((0,), (0,)), ((), ())), preferred_element...  15.7 us
    dot_general x10, matrix products, half_scores(): jnp.einsum('qtc,qsc->qts', grads, vecs, preferred_element_type=jnp.float32)  10.1 us
  transfers between devices with their start and end apart: 16, of which 6 were waited for; matrix products, arithmetic and copies ran while one was open for 13% of the time, Pallas kernels for 0%

commit v1 on v0

v1 whole, which is shorter than its diff:
```python
import functools

import jax
import jax.numpy as jnp
from jax import lax
from jax.experimental import pallas as pl
from jax.experimental.pallas import tpu as pltpu
from jax.sharding import Mesh
from jax.sharding import PartitionSpec as P

BF = jnp.bfloat16
F32 = jnp.float32
HALF = 32
ROWS = 128
LEVELS = 7


def dot(a, b):
    return lax.dot_general(a, b, (((1,), (0,)), ((), ())), preferred_element_type=F32)


def dot_nt(a, b):
    return lax.dot_general(a, b, (((1,), (1,)), ((), ())), preferred_element_type=F32)


def pair(p, bit):
    low = (p >> bit << (bit + 1)) | (p & ((1 << bit) - 1))
    return low, low | (1 << bit)


def iota(shape, dim):
    return lax.broadcasted_iota(jnp.int32, shape, dim)


def spread(m, level):
    width = ROWS if level < 2 else 2 * ROWS
    src, col = iota((2 * HALF, width), 0), iota((2 * HALF, width), 1)
    r, c = iota((ROWS, width), 0), iota((ROWS, width), 1)
    if level == 0:
        pick = src == col % 64
        keep = r // 64 == c // 64
    elif level == 1:
        pick = src == col // 64 * HALF + col % HALF
        keep = (r // HALF) % 2 == (c // HALF) % 2
    else:
        pick = src == col // ROWS * HALF + col % HALF
        keep = r // HALF == (c // HALF) % 4
    dense = dot(m, pick.astype(F32).astype(BF))
    return jnp.where(keep, dense, 0.0).astype(BF)


def grad_kernel(blocks, mix, far_mix, mine, theirs, grads, dense, state):
    step = pl.program_id(0)

    def top():
        r, c = iota((ROWS, ROWS), 0), iota((ROWS, ROWS), 1)
        keep = r // HALF == c // HALF
        pick = (iota((HALF, ROWS), 0) == iota((HALF, ROWS), 1) % HALF).astype(F32).astype(BF)

        def body(b, carry):
            near = jnp.where(keep, dot(far_mix[0, b], pick), 0.0).astype(BF)
            far = jnp.where(keep, dot(far_mix[1, b], pick), 0.0).astype(BF)
            both = jnp.concatenate([mine[b], theirs[b]], axis=1)
            out = dot(both, jnp.concatenate([near, far], axis=0)).astype(BF)
            state[b] = out
            grads[0, b] = out
            return carry

        lax.fori_loop(0, blocks, body, 0)

    def wide(level):
        def body(p, carry):
            lo, hi = pair(p, level - 2)
            dlo, dhi = spread(mix[0, lo], level), spread(mix[0, hi], level)
            dense[0, lo], dense[0, hi] = dlo, dhi
            both = jnp.concatenate([state[lo], state[hi]], axis=1)
            out = dot(both, jnp.concatenate([dlo, dhi], axis=0)).astype(BF)
            state[lo], state[hi] = out[:, :ROWS], out[:, ROWS:]
            grads[0, lo], grads[0, hi] = out[:, :ROWS], out[:, ROWS:]
            return carry

        lax.fori_loop(0, blocks // 2, body, 0)

    def narrow(level):
        def body(b, carry):
            d = spread(mix[0, b], level)
            dense[0, b, :, :ROWS] = d
            if level:
                out = dot(state[b], d).astype(BF)
                grads[0, b] = out
            return carry

        lax.fori_loop(0, blocks, body, 0)

    for s in range(LEVELS):
        level = LEVELS - 1 - s
        pl.when(step == s)(top if s == 0 else functools.partial(wide if level > 1 else narrow, level))


def grad_chain(mix, top_mix, mine, theirs):
    blocks, wide, rows = mine.shape
    last = LEVELS - 1
    return pl.pallas_call(
        functools.partial(grad_kernel, blocks),
        grid=(LEVELS,),
        in_specs=[
            pl.BlockSpec((1, blocks, rows, 2 * HALF), lambda s: (jnp.minimum(last - s, last - 1), 0, 0, 0)),
            pl.BlockSpec(memory_space=pltpu.VMEM),
            pl.BlockSpec(memory_space=pltpu.VMEM),
            pl.BlockSpec(memory_space=pltpu.VMEM),
        ],
        out_specs=[
            pl.BlockSpec((1, blocks, wide, rows), lambda s: (jnp.maximum(last - 1 - s, 0), 0, 0, 0)),
            pl.BlockSpec((1, blocks, rows, 2 * rows), lambda s: (jnp.minimum(last - s, last - 1), 0, 0, 0)),
        ],
        out_shape=[
            jax.ShapeDtypeStruct((last, blocks, wide, rows), BF),
            jax.ShapeDtypeStruct((last, blocks, rows, 2 * rows), BF),
        ],
        scratch_shapes=[pltpu.VMEM((blocks, wide, rows), BF)],
        compiler_params=pltpu.CompilerParams(vmem_limit_bytes=40 * 2**20),
        name="grad_chain",
    )(mix, top_mix, mine, theirs)


def fold(quad):
    lane = iota((HALF, ROWS), 1) // HALF
    out = quad[:HALF]
    for q in range(1, 4):
        out = jnp.where(lane == q, quad[q * HALF : (q + 1) * HALF], out)
    return out


def score_kernel(blocks, base, dense, grads, mine, theirs, out, state):
    level = pl.program_id(0)
    rows = ROWS

    def first():
        eye = (iota((rows, rows), 0) == iota((rows, rows), 1)).astype(F32).astype(BF)

        def body(b, carry):
            x = dot_nt(eye, base[b]).astype(BF)
            quad = dot(x, grads[0, b])
            lane = iota((64, rows), 1) // 64
            out[b, 0] = jnp.where(lane == 0, quad[:64], quad[64:]).astype(BF)
            state[b] = dot(dense[0, b, :, :rows], x).astype(BF)
            return carry

        lax.fori_loop(0, blocks, body, 0)

    def second():
        def body(b, carry):
            x = state[b]
            quad = dot(x, grads[0, b])
            lane = (iota((HALF, rows), 1) // HALF) % 2
            out[b, 0, :HALF] = jnp.where(lane == 0, quad[:HALF], quad[HALF : 2 * HALF]).astype(BF)
            out[b, 0, HALF:] = jnp.where(lane == 0, quad[2 * HALF : 3 * HALF], quad[3 * HALF :]).astype(BF)
            state[b] = dot(dense[0, b, :, :rows], x).astype(BF)
            return carry

        lax.fori_loop(0, blocks, body, 0)

    def wide(lev):
        def body(p, carry):
            lo, hi = pair(p, lev - 2)
            x = jnp.concatenate([state[lo], state[hi]], axis=0)
            g = jnp.concatenate([grads[0, lo], grads[0, hi]], axis=1)
            quad = dot(x, g)
            for k, b in enumerate((lo, hi)):
                for h in range(2):
                    part = fold(quad[h * rows : (h + 1) * rows, k * rows : (k + 1) * rows])
                    out[b, 0, h * HALF : (h + 1) * HALF] = part.astype(BF)
            y = dot(jnp.concatenate([dense[0, lo], dense[0, hi]], axis=0), x).astype(BF)
            state[lo], state[hi] = y[:rows], y[rows:]
            return carry

        lax.fori_loop(0, blocks // 2, body, 0)

    def top():
        def body(b, carry):
            quad = dot(state[b], jnp.concatenate([mine[b], theirs[b]], axis=1))
            out[b, 0, :HALF] = fold(quad[:, :rows]).astype(BF)
            out[b, 0, HALF:] = fold(quad[:, rows:]).astype(BF)
            return carry

        lax.fori_loop(0, blocks, body, 0)

    for lev in range(LEVELS):
        body = first if lev == 0 else second if lev == 1 else top if lev == LEVELS - 1 else functools.partial(wide, lev)
        pl.when(level == lev)(body)


def scores(base, dense, grads, mine, theirs):
    blocks, wide, rows = base.shape
    last = LEVELS - 1
    return pl.pallas_call(
        functools.partial(score_kernel, blocks),
        grid=(LEVELS,),
        in_specs=[
            pl.BlockSpec(memory_space=pltpu.VMEM),
            pl.BlockSpec((1, blocks, rows, 2 * rows), lambda s: (jnp.minimum(s, last - 1), 0, 0, 0)),
            pl.BlockSpec((1, blocks, wide, rows), lambda s: (jnp.minimum(s, last - 1), 0, 0, 0)),
            pl.BlockSpec(memory_space=pltpu.VMEM),
            pl.BlockSpec(memory_space=pltpu.VMEM),
        ],
        out_specs=pl.BlockSpec((blocks, 1, 2 * HALF, rows), lambda s: (0, s, 0, 0)),
        out_shape=jax.ShapeDtypeStruct((blocks, LEVELS, 2 * HALF, rows), BF),
        scratch_shapes=[pltpu.VMEM((blocks, rows, wide), BF)],
        compiler_params=pltpu.CompilerParams(vmem_limit_bytes=40 * 2**20),
        name="scores",
    )(base, dense, grads, mine, theirs)


def flips(count, distance=1):
    return [(i, i ^ distance) for i in range(count)]


def per_device(codes, scales, factors, upstream):
    rows, wide = codes.shape
    nz, ny = lax.axis_size("z"), lax.axis_size("y")
    blocks = 2 * nz
    chunk = wide // blocks
    side = lax.axis_index("x0")
    core = lax.axis_index("core")
    me_y = lax.axis_index("y")
    first = ((lax.axis_index("x1") * 2 + side) * nz + lax.axis_index("z")) * 2 * rows + core * rows

    mine = lax.all_to_all(upstream.T.reshape(blocks, chunk, rows), ("z", "core"), 0, 0)
    base = (
        codes.astype(F32).reshape(rows, wide // rows, rows) * scales[0][None, :, None]
    ).reshape(rows, wide).astype(BF)
    base = lax.all_to_all(base.T.reshape(blocks, chunk, rows), ("z", "core"), 0, 0)
    theirs = lax.ppermute(mine, "x0", flips(2))

    row = first + jnp.arange(rows, dtype=jnp.int32)
    mixing = []
    for level in range(LEVELS):
        pick = row // (HALF * 2**level) % 2 * HALF + row % HALF
        eye = (jnp.arange(2 * HALF, dtype=jnp.int32)[None, :] == pick[:, None]).astype(F32)
        mixing.append((eye + factors[level]).astype(BF))
    mix = lax.all_gather(jnp.stack(mixing), ("z", "core"), axis=1)
    last = mix[LEVELS - 1]
    send = jnp.where(side == 0, last[..., HALF:], last[..., :HALF])
    keep = jnp.where(side == 0, last[..., :HALF], last[..., HALF:])
    top_mix = jnp.stack([keep, lax.ppermute(send, "x0", flips(2))])

    grads, dense = grad_chain(mix[: LEVELS - 1], top_mix, mine, theirs)
    parts = scores(base, dense, grads, mine, theirs)

    far = lax.ppermute(parts[:, LEVELS - 1, HALF:], "x0", flips(2))
    near = parts[:, LEVELS - 1, :HALF]
    top = jnp.concatenate([jnp.where(side == 0, near, far), jnp.where(side == 0, far, near)], axis=1)
    parts = jnp.concatenate([parts[:, : LEVELS - 1], top[:, None]], axis=1)

    parts = parts.reshape(nz, 2, LEVELS, 2 * HALF, rows)
    own = lax.dynamic_index_in_dim(parts, core, 1, keepdims=False)
    away = lax.dynamic_index_in_dim(parts, 1 - core, 1, keepdims=False)
    total = own.astype(F32) + lax.ppermute(away, "core", flips(2)).astype(F32)
    total = total.astype(BF).reshape(nz, LEVELS, ny, 2 * HALF // ny, rows).transpose(2, 0, 1, 3, 4)
    total = jnp.sum(lax.all_to_all(total, "y", 0, 0).astype(F32), axis=0).astype(BF)
    total = jnp.sum(lax.all_to_all(total, "z", 0, 0).astype(F32), axis=0)
    total = total + lax.ppermute(total, "zh", flips(2))
    total = lax.all_gather(total, "y", axis=1)
    return total.reshape(LEVELS, 2 * HALF, rows).transpose(0, 2, 1)


def solution(mesh):
    fsdp, col = mesh.devices.shape
    nz = 8
    names = ("x1", "x0", "z", "core", "zh", "y")
    fine = Mesh(mesh.devices.reshape(fsdp // (4 * nz), 2, nz, 2, 2, col // 2), names)
    rows, cols = ("x1", "x0", "z", "core"), ("zh", "y")
    return jax.shard_map(
        per_device,
        mesh=fine,
        in_specs=(P(rows, cols), P(rows, cols), P(None, rows, None), P(rows, cols)),
        out_specs=P(None, rows, None),
        check_vma=False,
    )
```

time: 489 us -> 285 us (0.58)
  waiting for transfers between devices: 346 us -> 96.9 us
  blocking collectives: 0 us -> 57.5 us
  Pallas kernels: 0 us -> 47.1 us
  matrix products: 37.7 us -> 0 us
  other arithmetic: 21.3 us -> 3.56 us
  starting transfers between devices: 53.2 us -> 47.3 us
    ppermute x15 -> x5, waiting for transfers between devices: 196 us -> 17.9 us  [the longest x1 6.83 us: per_device(): total = total + lax.ppermute(total, 'zh', flips(2))]
    psum x1 -> x0, waiting for transfers between devices: 150 us -> none  [per_device(): stacked = lax.psum(stacked, 'col')]
    pallas_call x0 -> x2, Pallas kernels: none -> 47.1 us  [the longest x1 25.8 us: grad_chain(): pl.pallas_call(functools.partial(grad_kernel, blocks), grid=(LEVELS,), in...]
    all_to_all x0 -> x2, blocking collectives: none -> 45.3 us  [the longest x1 27.8 us: per_device(): total = jnp.sum(lax.all_to_all(total, 'z', 0, 0).astype(F32), axis=0)]
    all_gather x0 -> x1, waiting for transfers between devices: none -> 41 us  [per_device(): mix = lax.all_gather(jnp.stack(mixing), ('z', 'core'), axis=1)]
    all_to_all x0 -> x2, waiting for transfers between devices: none -> 37.9 us  [the longest x1 37.9 us: per_device(): lax.all_to_all(upstream.T.reshape(blocks, chunk, rows), ('z', 'core'), 0, 0)]
    dot_general x34 -> x0, matrix products: 37.7 us -> none  [the longest x12 15.7 us: left_product(): lax.dot_general(matrix, grad, (((0,), (0,)), ((), ())), preferred_element...]
    ppermute x15 -> x5, starting transfers between devices: 53.2 us -> 23.1 us  [the longest x1 8.58 us: per_device(): total = total + lax.ppermute(total, 'zh', flips(2))]
  transfers between devices with their start and end apart: 16 -> 8, of which waited for: 6 -> 6; matrix products, arithmetic and copies ran while one was open for 13% -> 4% of each run, Pallas kernels for 0% -> 9%
where the time goes in v1:
time: 285 us; the launch traced here: 283 us
  waiting for transfers between devices  96.9 us (34%)
  blocking collectives  57.5 us (20%)
  starting transfers between devices  47.3 us (17%)
  Pallas kernels  47.1 us (17%)
  local copies, waits for them, and re-layouts  17 us (6%)
  between operations  13.7 us (5%)
  other arithmetic  3.56 us (1%)
    all_gather x1, waiting for transfers between devices, per_device(): mix = lax.all_gather(jnp.stack(mixing), ('z', 'core'), axis=1)  41 us
    all_to_all x1, waiting for transfers between devices, per_device(): lax.all_to_all(upstream.T.reshape(blocks, chunk, rows), ('z', 'core'), 0, 0)  37.9 us
    all_to_all x1, blocking collectives, per_device(): total = jnp.sum(lax.all_to_all(total, 'z', 0, 0).astype(F32), axis=0)  27.8 us
    pallas_call x1, Pallas kernels, grad_chain(): pl.pallas_call(functools.partial(grad_kernel, blocks), grid=(LEVELS,), in...  25.8 us
    pallas_call x1, Pallas kernels, scores(): pl.pallas_call(functools.partial(score_kernel, blocks), grid=(LEVELS,), i...  21.3 us
    all_to_all x1, blocking collectives, per_device(): lax.all_to_all(total, 'y', 0, 0).astype(F32)  17.6 us
    all_to_all x1, starting transfers between devices, per_device(): lax.all_to_all(upstream.T.reshape(blocks, chunk, rows), ('z', 'core'), 0, 0)  12.7 us
    all_gather x1, blocking collectives, per_device(): total = lax.all_gather(total, 'y', axis=1)  12.2 us
  transfers between devices with their start and end apart: 8, of which 6 were waited for; matrix products, arithmetic and copies ran while one was open for 4% of the time, Pallas kernels for 9%

profile of v1, /device:TPU:24, one launch (start us, length us, event | category | flops | bytes accessed | tf_op | source)
XLA Modules:
  0.0 283.0 jit_solution(15135979786935959874)
XLA Ops:
  6.5 2.3 copy.31
  8.9 12.7 %all-to-all-start.1 = ((bf16[16,208,128]{2,1,0:T(8,128)(2,1)}), bf16[16,208,128]{2,1,0:T(8,128)(2,1)}, u32[]{:S(2)}, u32[]{:S(2)}) async-start(bf16[16,208,128]{2,1,0:T(8,128)(2,1)} %bitcast.9), calls=%async_computation.1 | async-start | bytes 1703936 | tf_op jit(solution)/shard_map/all_to_all | solution.py:228
  21.9 0.6 copy-done.6
  22.8 1.3 copy.27
  24.0 37.9 %all-to-all-done.1.mine = bf16[16,208,128]{2,1,0:T(8,128)(2,1)} async-done(((bf16[16,208,128]{2,1,0:T(8,128)(2,1)}), bf16[16,208,128]{2,1,0:T(8,128)(2,1)}, u32[]{:S(2)}, u32[]{:S(2)}) %all-to-all-start.1) | async-done | bytes 852000 | tf_op jit(solution)/shard_map/all_to_all | solution.py:228
  62.0 11.5 %all-to-all-start = ((bf16[16,208,128]{2,1,0:T(8,128)(2,1)}), bf16[16,208,128]{2,1,0:T(8,128)(2,1)}, u32[]{:S(2)}, u32[]{:S(2)}) async-start(bf16[16,208,128]{2,1,0:T(8,128)(2,1)} %bitcast.3), calls=%async_computation | async-start | bytes 1703936 | tf_op jit(solution)/shard_map/all_to_all | solution.py:232
  73.5 3.4 %collective-permute-start.1 = (bf16[16,208,128]{2,1,0:T(8,128)(2,1)}, bf16[16,208,128]{2,1,0:T(8,128)(2,1)}, u32[]{:S(2)}, u32[]{:S(2)}) collective-permute-start(bf16[16,208,128]{2,1,0:T(8,128)(2,1)} %all-to-all-done.1.mine), channel_id=1, source_target_pairs={{0,128},{128,0},{1,129},{129,1},{2,130},{130,2},{3,131},{131,3},{4... | collective-permute-start | bytes 2555912 | tf_op jit(solution)/shard_map/ppermute | solution.py:233
  76.9 41.0 %all-gather.4.cloned.1.call-done = bf16[7,2048,64]{1,2,0:T(8,128)(2,1)} async-done(((bf16[7,128,64]{1,2,0:T(8,128)(2,1)}), bf16[7,2048,64]{1,2,0:T(8,128)(2,1)}) %all-gather.4.cloned.1.call-update) | async-done | bytes 1835024 | tf_op jit(solution)/shard_map/all_gather | solution.py:241
  117.9 1.1 slice.61
  119.0 0.3 copy.36
  119.3 1.2 select_bitcast_fusion
  120.5 3.4 %collective-permute-start = (bf16[16,128,32]{2,1,0:T(8,128)(2,1)}, bf16[16,128,32]{2,1,0:T(8,128)(2,1)}, u32[]{:S(2)}, u32[]{:S(2)}) collective-permute-start(bf16[16,128,32]{2,1,0:T(8,128)(2,1)} %get-tuple-element.12), channel_id=1, source_target_pairs={{0,128},{128,0},{1,129},{129,1},{2,130},{130,2},{3,131},{131,3},{4... | collective-permute-start | bytes 393224 | tf_op jit(solution)/shard_map/ppermute | solution.py:245
  123.9 1.3 slice.60
  125.2 3.1 %copy.28 = bf16[6,2048,64]{2,1,0:T(8,128)(2,1)S(1)} copy(bf16[6,2048,64]{1,2,0:T(8,128)(2,1)} %slice.60) | data formatting | bytes 3145728 | tf_op jit(solution)/shard_map/slice | solution.py:247
  128.2 5.5 %collective-permute-done = bf16[16,128,32]{2,1,0:T(8,128)(2,1)} collective-permute-done((bf16[16,128,32]{2,1,0:T(8,128)(2,1)}, bf16[16,128,32]{2,1,0:T(8,128)(2,1)}, u32[]{:S(2)}, u32[]{:S(2)}) %collective-permute-start) | collective-permute-done | bytes 131104 | tf_op jit(solution)/shard_map/ppermute | solution.py:245
  133.7 1.4 pad_maximum_fusion.far_mix
  135.2 25.8 %grad_chain.1 = (bf16[6,16,208,128]{3,2,1,0:T(8,128)(2,1)S(1)}, bf16[6,16,128,256]{3,2,1,0:T(8,128)(2,1)}) custom-call(bf16[6,16,128,64]{3,2,1,0:T(8,128)(2,1)S(1)} %bitcast.35, bf16[2,16,128,32]{3,2,1,0:T(8,128)(2,1)S(1)} %pad_maximum_fusion.far_mix, bf16[16,208,128]{2,1,0:T(8,128)(2,1)} %all-to-all-done.1.mine, ...), custom_call_target="tpu_custom_call" | custom-call | tf_op jit(solution)/shard_map/grad_chain/pallas_call | solution.py:103
  161.0 2.3 copy-done.1
  163.3 2.4 copy-done.2
  165.8 21.3 %scores.1 = bf16[16,7,64,128]{3,2,1,0:T(8,128)(2,1)S(1)} custom-call(bf16[16,208,128]{2,1,0:T(8,128)(2,1)} %all-to-all-done.base, bf16[6,16,128,256]{3,2,1,0:T(8,128)(2,1)} %get-tuple-element.7.dense, bf16[6,16,208,128]{3,2,1,0:T(8,128)(2,1)S(1)} %copy-done.2, bf16[16,208,128]{2,1,0:T(8,128)(2,1)} %all-to-all-done.1.mine, ...), custom_call_target="tpu_custom_call" | custom-call | tf_op jit(solution)/shard_map/scores/pallas_call | solution.py:196
  187.2 3.4 %collective-permute-start.2 = (bf16[16,32,128]{2,1,0:T(8,128)(2,1)S(1)}, bf16[16,32,128]{2,1,0:T(8,128)(2,1)S(1)}, u32[]{:S(2)}, u32[]{:S(2)}) collective-permute-start(bf16[16,32,128]{2,1,0:T(8,128)(2,1)S(1)} %slice_bitcast_fusion), channel_id=1, source_target_pairs={{0,128},{128,0},{1,129},{129,1},{2,130},{130,2},{3,131},{131,3},{4... | collective-permute-start | bytes 393224 | tf_op jit(solution)/shard_map/ppermute | solution.py:250
  190.8 3.3 %collective-permute-done.2 = bf16[16,32,128]{2,1,0:T(8,128)(2,1)S(1)} collective-permute-done((bf16[16,32,128]{2,1,0:T(8,128)(2,1)S(1)}, bf16[16,32,128]{2,1,0:T(8,128)(2,1)S(1)}, u32[]{:S(2)}, u32[]{:S(2)}) %collective-permute-start.2) | collective-permute-done | bytes 131104 | tf_op jit(solution)/shard_map/ppermute | solution.py:250
  194.2 1.0 dynamic-slice_bitcast_fusion
  195.2 4.3 %collective-permute-start.3 = (bf16[8,7,64,128]{3,2,1,0:T(8,128)(2,1)}, bf16[8,7,64,128]{3,2,1,0:T(8,128)(2,1)S(1)}, u32[]{:S(2)}, u32[]{:S(2)}) collective-permute-start(bf16[8,7,64,128]{3,2,1,0:T(8,128)(2,1)} %dynamic-slice_bitcast_fusion), channel_id=1, source_target_pairs={{0,8},{8,0},{1,9},{9,1},{2,10},{10,2},{3,11},{11,3},{4,12},{12,4},... | collective-permute-start | bytes 2752520 | tf_op jit(solution)/shard_map/ppermute | solution.py:258
  199.5 2.3 collective-permute-done.3
  201.8 0.3 fusion
  202.3 17.6 %all_to_all.20 = bf16[4,8,7,16,128]{4,3,2,1,0:T(8,128)(2,1)S(1)} all-to-all(bf16[4,8,7,16,128]{4,3,2,1,0:T(8,128)(2,1)S(1)} %copy.35), channel_id=1, replica_groups=mesh['x1'=2,'x0'=2,'z'=8,'core'=2,'zh'=2,'y'=4] {'y'}, dimensions={0} | all-to-all | bytes 1835008 | tf_op jit(solution)/shard_map/all_to_all | solution.py:260
  220.0 27.8 %all_to_all.21 = bf16[8,7,16,128]{3,2,1,0:T(8,128)(2,1)S(1)} all-to-all(bf16[8,7,16,128]{3,2,1,0:T(8,128)(2,1)S(1)} %reduce_sum.21), channel_id=1, replica_groups=mesh['x1'=2,'x0'=2,'z'=8,'core'=2,'zh'=2,'y'=4] {'z'}, dimensions={0} | all-to-all | bytes 458752 | tf_op jit(solution)/shard_map/all_to_all | solution.py:261
  247.8 8.6 %collective-permute-start.4 = (f32[7,16,128]{2,1,0:T(8,128)S(1)}, f32[7,16,128]{2,1,0:T(8,128)S(1)}, u32[]{:S(2)}, u32[]{:S(2)}) collective-permute-start(f32[7,16,128]{2,1,0:T(8,128)S(1)} %convert_reduce_fusion), channel_id=1, source_target_pairs={{0,4},{4,0},{1,5},{5,1},{2,6},{6,2},{3,7},{7,3},{8,12},{12,8},{9,1... | collective-permute-start | bytes 172040 | tf_op jit(solution)/shard_map/ppermute | solution.py:262
  256.4 6.8 %collective-permute-done.4 = f32[7,16,128]{2,1,0:T(8,128)S(1)} collective-permute-done((f32[7,16,128]{2,1,0:T(8,128)S(1)}, f32[7,16,128]{2,1,0:T(8,128)S(1)}, u32[]{:S(2)}, u32[]{:S(2)}) %collective-permute-start.4) | collective-permute-done | bytes 57376 | tf_op jit(solution)/shard_map/ppermute | solution.py:262
  263.3 12.2 %all-gather.1 = f32[7,64,128]{2,1,0:T(8,128)S(1)} all-gather(f32[7,16,128]{2,1,0:T(8,128)S(1)} %add.289), channel_id=3, replica_groups=mesh['x1'=2,'x0'=2,'z'=8,'core'=2,'zh'=2,'y'=4] {'y'}, dimensions={1}, use_global_device_ids=true | all-gather | bytes 286720 | tf_op jit(solution)/shard_map/all_gather | solution.py:263
  275.4 0.7 copy.48
  (38 shorter events, 1.3 us)
Async XLA Ops:
  6.5 16.0 %copy-start = (f32[1,26]{1,0:T(1,128)S(1)}, f32[1,26]{1,0:T(1,128)}, u32[]{:S(2)}) copy-start(f32[1,26]{1,0:T(1,128)} %param.5) | copy-start | bytes 316
  6.5 15.2 %copy-start.5 = (f32[7,128,64]{1,2,0:T(8,128)S(1)}, f32[7,128,64]{1,2,0:T(8,128)}, u32[]{:S(2)}) copy-start(f32[7,128,64]{1,2,0:T(8,128)} %param.6) | copy-start | bytes 688132
  6.5 16.1 %copy-start.4 = (bf16[128,3328]{1,0:T(8,128)(2,1)S(1)}, bf16[128,3328]{1,0:T(8,128)(2,1)}, u32[]{:S(2)}) copy-start(bf16[128,3328]{1,0:T(8,128)(2,1)} %param.4) | copy-start | bytes 2555908
  8.9 53.1 %all-to-all-start.1 = ((bf16[16,208,128]{2,1,0:T(8,128)(2,1)}), bf16[16,208,128]{2,1,0:T(8,128)(2,1)}, u32[]{:S(2)}, u32[]{:S(2)}) async-start(bf16[16,208,128]{2,1,0:T(8,128)(2,1)} %bitcast.9), calls=%async_computation.1 | async-start | bytes 1703936 | tf_op jit(solution)/shard_map/all_to_all | solution.py:228
  21.5 96.3 %all-gather.4.cloned.1.call-start = ((), (), s32[]{:S(2)}) async-start(), calls=%async_computation.4 | async-start | bytes 1949696 | tf_op jit(solution)/shard_map/all_gather | solution.py:241
  21.9 0.6 copy-start.6
  62.0 101.3 %all-to-all-start = ((bf16[16,208,128]{2,1,0:T(8,128)(2,1)}), bf16[16,208,128]{2,1,0:T(8,128)(2,1)}, u32[]{:S(2)}, u32[]{:S(2)}) async-start(bf16[16,208,128]{2,1,0:T(8,128)(2,1)} %bitcast.3), calls=%async_computation | async-start | bytes 1703936 | tf_op jit(solution)/shard_map/all_to_all | solution.py:232
  73.5 61.7 %collective-permute-start.1 = (bf16[16,208,128]{2,1,0:T(8,128)(2,1)}, bf16[16,208,128]{2,1,0:T(8,128)(2,1)}, u32[]{:S(2)}, u32[]{:S(2)}) collective-permute-start(bf16[16,208,128]{2,1,0:T(8,128)(2,1)} %all-to-all-done.1.mine), channel_id=1, source_target_pairs={{0,128},{128,0},{1,129},{129,1},{2,130},{130,2},{3,131},{131,3},{4... | collective-permute-start | bytes 2555912 | tf_op jit(solution)/shard_map/ppermute | solution.py:233
  117.9 6.0 %copy-start.3 = (bf16[7,2048,64]{1,2,0:T(8,128)(2,1)S(1)}, bf16[7,2048,64]{1,2,0:T(8,128)(2,1)}, u32[]{:S(2)}) copy-start(bf16[7,2048,64]{1,2,0:T(8,128)(2,1)} %all-gather.4.cloned.1.call-done) | copy-start | bytes 5505028
  120.5 13.3 %collective-permute-start = (bf16[16,128,32]{2,1,0:T(8,128)(2,1)}, bf16[16,128,32]{2,1,0:T(8,128)(2,1)}, u32[]{:S(2)}, u32[]{:S(2)}) collective-permute-start(bf16[16,128,32]{2,1,0:T(8,128)(2,1)} %get-tuple-element.12), channel_id=1, source_target_pairs={{0,128},{128,0},{1,129},{129,1},{2,130},{130,2},{3,131},{131,3},{4... | collective-permute-start | bytes 393224 | tf_op jit(solution)/shard_map/ppermute | solution.py:245
  161.0 2.3 copy-start.1
  163.3 2.5 copy-start.2
  187.2 6.9 %collective-permute-start.2 = (bf16[16,32,128]{2,1,0:T(8,128)(2,1)S(1)}, bf16[16,32,128]{2,1,0:T(8,128)(2,1)S(1)}, u32[]{:S(2)}, u32[]{:S(2)}) collective-permute-start(bf16[16,32,128]{2,1,0:T(8,128)(2,1)S(1)} %slice_bitcast_fusion), channel_id=1, source_target_pairs={{0,128},{128,0},{1,129},{129,1},{2,130},{130,2},{3,131},{131,3},{4... | collective-permute-start | bytes 393224 | tf_op jit(solution)/shard_map/ppermute | solution.py:250
  195.2 6.6 %collective-permute-start.3 = (bf16[8,7,64,128]{3,2,1,0:T(8,128)(2,1)}, bf16[8,7,64,128]{3,2,1,0:T(8,128)(2,1)S(1)}, u32[]{:S(2)}, u32[]{:S(2)}) collective-permute-start(bf16[8,7,64,128]{3,2,1,0:T(8,128)(2,1)} %dynamic-slice_bitcast_fusion), channel_id=1, source_target_pairs={{0,8},{8,0},{1,9},{9,1},{2,10},{10,2},{3,11},{11,3},{4,12},{12,4},... | collective-permute-start | bytes 2752520 | tf_op jit(solution)/shard_map/ppermute | solution.py:258
  247.8 15.4 %collective-permute-start.4 = (f32[7,16,128]{2,1,0:T(8,128)S(1)}, f32[7,16,128]{2,1,0:T(8,128)S(1)}, u32[]{:S(2)}, u32[]{:S(2)}) collective-permute-start(f32[7,16,128]{2,1,0:T(8,128)S(1)} %convert_reduce_fusion), channel_id=1, source_target_pairs={{0,4},{4,0},{1,5},{5,1},{2,6},{6,2},{3,7},{7,3},{8,12},{12,8},{9,1... | collective-permute-start | bytes 172040 | tf_op jit(solution)/shard_map/ppermute | solution.py:262
Sparse Core Ops, SparseCore 0:
  24.4 93.4 all-gather.3

commit v2 on v0

v2 whole, which is shorter than its diff:
```python
import functools

import jax
import jax.numpy as jnp
from jax import lax
from jax.experimental import pallas as pl
from jax.experimental.pallas import tpu as pltpu
from jax.sharding import Mesh
from jax.sharding import PartitionSpec as P

BF = jnp.bfloat16
F32 = jnp.float32
HALF = 32
BLOCK = 2 * HALF
ROWS = 128
LEVELS = 7
TOP = LEVELS - 1
NZ = 8
NY = 4
SLICE = BLOCK // NY
PARAMS = pltpu.CompilerParams(vmem_limit_bytes=58 * 2**20)
WHOLE = pl.BlockSpec(memory_space=pltpu.VMEM)
SCALARS = pl.BlockSpec(memory_space=pltpu.SMEM)


def dot(a, b):
    return lax.dot_general(a, b, (((1,), (0,)), ((), ())), preferred_element_type=F32)


def dot_nt(a, b):
    return lax.dot_general(a, b, (((1,), (1,)), ((), ())), preferred_element_type=F32)


def iota(shape, dim):
    return lax.broadcasted_iota(jnp.int32, shape, dim)


def flips(count, distance=1):
    return [(i, i ^ distance) for i in range(count)]


def units(level):
    if level == 2:
        return [[(2 * z, 2 * z + 1)] for z in range(NZ)]
    if level < 2 or level == TOP:
        return [[(2 * z, None), (2 * z + 1, None)] for z in range(NZ)]
    bit = level - 3
    lows = [z for z in range(NZ) if not z >> bit & 1]
    return [[(2 * z + c, 2 * (z | 1 << bit) + c) for c in range(2)] for z in lows]


def pack_kernel(me, upstream, factors, out):
    chunk = out.shape[1] - BLOCK
    for t in range(upstream.shape[1] // ROWS):
        turned = upstream[:, t * ROWS : (t + 1) * ROWS].T
        start, end = t * ROWS, (t + 1) * ROWS
        while start < end:
            block, at = start // chunk, start % chunk
            size = min(end - start, chunk - at)
            out[block, at : at + size] = turned[start - t * ROWS : start - t * ROWS + size]
            start += size
    row = me[4] + iota((ROWS, BLOCK), 0)
    tile = jnp.zeros((ROWS, ROWS), F32)
    for side in range(2):
        level = jnp.minimum(2 * me[0] + side, TOP)
        pick = lax.shift_right_logical(row, level + 5) % 2 * HALF + row % HALF
        eye = (iota((ROWS, BLOCK), 1) == pick).astype(F32)
        place = (iota((BLOCK, ROWS), 1) == iota((BLOCK, ROWS), 0) + side * BLOCK).astype(F32).astype(BF)
        tile = tile + dot((eye + factors[level]).astype(BF), place)
    tile = tile.astype(BF)
    for block in range(out.shape[0]):
        half = block % 2 * BLOCK
        out[block, chunk:] = tile[half : half + BLOCK]


def pack(me, upstream, factors):
    rows, wide = upstream.shape
    return pl.pallas_call(
        pack_kernel,
        in_specs=[SCALARS, WHOLE, WHOLE],
        out_specs=WHOLE,
        out_shape=jax.ShapeDtypeStruct((2 * NZ, wide // (2 * NZ) + BLOCK, rows), BF),
        compiler_params=PARAMS,
        name="pack",
    )(me, upstream, factors)


def expand_kernel(me, near, away, dense):
    my_y, my_core, my_x = me[0], me[2], me[3]

    def run(level):
        width = ROWS if level < 2 else 2 * ROWS
        src, col = iota((ROWS, width), 0), iota((ROWS, width), 1)
        lane = level % 2 * BLOCK
        if level == 0:
            pick = src == lane + col % BLOCK
        elif level == 1:
            pick = src == lane + col // BLOCK * HALF + col % HALF
        elif level < TOP:
            pick = src == lane + col // ROWS * HALF + col % HALF
        else:
            pick = src == HALF * my_x + col // ROWS * BLOCK + col % HALF
        pick = pick.astype(F32).astype(BF)
        which = jnp.bitwise_xor(my_y, level // 2)
        for c, ref in enumerate((near, away)):
            at = pl.multiple_of(jnp.bitwise_xor(my_core, c) * BLOCK, BLOCK)
            row, col = at + iota((BLOCK, width), 0), iota((BLOCK, width), 1)
            if level == 0:
                keep = row // BLOCK == col // BLOCK
            elif level == 1:
                keep = (row // HALF) % 2 == (col // HALF) % 2
            else:
                keep = row // HALF == (col // HALF) % 4
            for block in range(2 * NZ):
                full = jnp.where(keep, dot(ref[which, block], pick), 0.0).astype(BF)
                dense[0, block, pl.ds(at, BLOCK), :width] = full

    for level in range(LEVELS):
        pl.when(pl.program_id(0) == level)(functools.partial(run, level))


def expand(me, near, away):
    shape = (2 * NZ, ROWS, 2 * ROWS)
    return pl.pallas_call(
        expand_kernel,
        grid=(LEVELS,),
        in_specs=[SCALARS, WHOLE, WHOLE],
        out_specs=pl.BlockSpec((1,) + shape, lambda s: (s, 0, 0, 0)),
        out_shape=jax.ShapeDtypeStruct((LEVELS,) + shape, BF),
        compiler_params=PARAMS,
        name="expand",
    )(me, near, away)


def grad_kernel(dense, mine, theirs, grads, state):
    def run(level):
        for unit in units(level):
            for lo, hi in unit:
                if level == TOP:
                    both = jnp.concatenate([mine[lo], theirs[lo]], axis=1)
                    full = jnp.concatenate([dense[0, lo, :, :ROWS], dense[0, lo, :, ROWS:]], axis=0)
                elif level == 1:
                    both, full = state[lo], dense[0, lo, :, :ROWS]
                else:
                    both = jnp.concatenate([state[lo], state[hi]], axis=1)
                    full = jnp.concatenate([dense[0, lo], dense[0, hi]], axis=0)
                out = dot(both, full).astype(BF)
                grads[0, lo] = out[:, :ROWS]
                if level > 1:
                    state[lo] = out[:, :ROWS]
                if hi is not None:
                    grads[0, hi] = out[:, ROWS:]
                    state[hi] = out[:, ROWS:]

    for s in range(TOP):
        pl.when(pl.program_id(0) == s)(functools.partial(run, TOP - s))


def grad_chain(dense, mine, theirs):
    blocks, wide, rows = mine.shape
    return pl.pallas_call(
        grad_kernel,
        grid=(TOP,),
        in_specs=[pl.BlockSpec((1, blocks, rows, 2 * rows), lambda s: (TOP - s, 0, 0, 0)), WHOLE, WHOLE],
        out_specs=pl.BlockSpec((1, blocks, wide, rows), lambda s: (TOP - 1 - s, 0, 0, 0)),
        out_shape=jax.ShapeDtypeStruct((TOP, blocks, wide, rows), BF),
        scratch_shapes=[pltpu.VMEM((blocks, wide, rows), BF)],
        compiler_params=PARAMS,
        name="grad_chain",
    )(dense, mine, theirs)


def fold(quad):
    lane = iota((HALF, ROWS), 1) // HALF
    out = quad[:HALF]
    for q in range(1, 4):
        out = jnp.where(lane == q, quad[q * HALF : (q + 1) * HALF], out)
    return out


def score_kernel(me, base, dense, grads, mine, theirs, own, away, state):
    first_core = me[2] == 0

    def store(z, parts):
        zero, one = parts
        mine_, other = jnp.where(first_core, zero, one), jnp.where(first_core, one, zero)
        for y in range(NY):
            own[y, z, 0] = mine_[y * SLICE : (y + 1) * SLICE].astype(BF)
            away[y, z, 0] = other[y * SLICE : (y + 1) * SLICE].astype(BF)

    def run(level):
        if level == 0:
            eye = (iota((ROWS, ROWS), 0) == iota((ROWS, ROWS), 1)).astype(F32).astype(BF)
        for unit in units(level):
            parts = {}
            for lo, hi in unit:
                if level == 0:
                    x = dot_nt(eye, base[lo]).astype(BF)
                elif hi is None:
                    x = state[lo]
                else:
                    x = jnp.concatenate([state[lo], state[hi]], axis=0)
                if level == TOP:
                    g = jnp.concatenate([mine[lo], theirs[lo]], axis=1)
                elif hi is None:
                    g = grads[0, lo]
                else:
                    g = jnp.concatenate([grads[0, lo], grads[0, hi]], axis=1)
                quad = dot(x, g)
                if level == 0:
                    parts[lo] = jnp.where(iota((BLOCK, ROWS), 1) < BLOCK, quad[:BLOCK], quad[BLOCK:])
                elif level == 1:
                    even = (iota((HALF, ROWS), 1) // HALF) % 2 == 0
                    rows = [quad[q * HALF : (q + 1) * HALF] for q in range(4)]
                    parts[lo] = jnp.concatenate([jnp.where(even, rows[0], rows[1]), jnp.where(even, rows[2], rows[3])], axis=0)
                elif level == TOP:
                    parts[lo] = jnp.concatenate([fold(quad[:, :ROWS]), fold(quad[:, ROWS:])], axis=0)
                else:
                    for b, at in ((lo, slice(0, ROWS)), (hi, slice(ROWS, 2 * ROWS))):
                        parts[b] = jnp.concatenate([fold(quad[:ROWS, at]), fold(quad[ROWS:, at])], axis=0)
                if level < 2:
                    state[lo] = dot(dense[0, lo, :, :ROWS], x).astype(BF)
                elif level < TOP:
                    full = jnp.concatenate([dense[0, lo], dense[0, hi]], axis=0)
                    out = dot(full, x).astype(BF)
                    state[lo], state[hi] = out[:ROWS], out[ROWS:]
            for z in sorted({b // 2 for b in parts}):
                store(z, (parts[2 * z], parts[2 * z + 1]))

    for level in range(LEVELS):
        pl.when(pl.program_id(0) == level)(functools.partial(run, level))


def scores(me, base, dense, grads, mine, theirs):
    blocks, wide, rows = base.shape
    shape = (NY, NZ, LEVELS, SLICE, rows)
    out_spec = pl.BlockSpec((NY, NZ, 1, SLICE, rows), lambda s: (0, 0, s, 0, 0))
    return pl.pallas_call(
        score_kernel,
        grid=(LEVELS,),
        in_specs=[
            SCALARS,
            WHOLE,
            pl.BlockSpec((1, blocks, rows, 2 * rows), lambda s: (jnp.minimum(s, TOP - 1), 0, 0, 0)),
            pl.BlockSpec((1, blocks, wide, rows), lambda s: (jnp.minimum(s, TOP - 1), 0, 0, 0)),
            WHOLE,
            WHOLE,
        ],
        out_specs=[out_spec, out_spec],
        out_shape=[jax.ShapeDtypeStruct(shape, BF)] * 2,
        scratch_shapes=[pltpu.VMEM((blocks, rows, wide), BF)],
        compiler_params=PARAMS,
        name="scores",
    )(me, base, dense, grads, mine, theirs)


def core_sum_kernel(me, own, got, *outs):
    for k, out in enumerate(outs):
        y = jnp.bitwise_xor(me[0], k)
        out[...] = (own[y].astype(F32) + got[y].astype(F32)).astype(BF)


def core_sum(me, own, got):
    return pl.pallas_call(
        core_sum_kernel,
        in_specs=[SCALARS, WHOLE, WHOLE],
        out_specs=[WHOLE] * NY,
        out_shape=[jax.ShapeDtypeStruct(own.shape[1:], BF)] * NY,
        compiler_params=PARAMS,
        name="core_sum",
    )(me, own, got)


def finish_kernel(me, *refs):
    *pieces, out, rows = refs
    for k, piece in enumerate(pieces):
        y = jnp.bitwise_xor(me[0], k)
        rows[:, pl.ds(pl.multiple_of(y * SLICE, SLICE), SLICE), :] = piece[...]
    for level in range(TOP):
        out[level] = rows[level].T
    last = rows[TOP]
    swapped = jnp.concatenate([last[HALF:], last[:HALF]], axis=0)
    out[TOP] = jnp.where(me[3] == 0, last, swapped).T


def finish(me, pieces):
    return pl.pallas_call(
        finish_kernel,
        in_specs=[SCALARS] + [WHOLE] * NY,
        out_specs=WHOLE,
        out_shape=jax.ShapeDtypeStruct((LEVELS, ROWS, BLOCK), F32),
        scratch_shapes=[pltpu.VMEM((LEVELS, BLOCK, ROWS), F32)],
        compiler_params=PARAMS,
        name="finish",
    )(me, *pieces)


def per_device(codes, scales, factors, upstream):
    rows, wide = codes.shape
    blocks = 2 * NZ
    chunk = wide // blocks
    side, my_z, my_core, my_y = (lax.axis_index(name) for name in ("x0", "z", "core", "y"))
    first = (((lax.axis_index("x1") * 2 + side) * NZ + my_z) * 2 + my_core) * rows
    me = jnp.stack([my_y, my_z, my_core, side, first]).astype(jnp.int32)

    got = lax.all_to_all(pack(me, upstream, factors), ("z", "core"), 0, 0)
    mine, mixing = got[:, :chunk], got[:, chunk:]
    base = codes.astype(F32).reshape(rows, wide // rows, rows) * scales[0][None, :, None]
    base = base.reshape(rows, wide).astype(BF).T.reshape(blocks, chunk, rows)
    base = lax.all_to_all(base, ("z", "core"), 0, 0)
    theirs = lax.ppermute(mine, "x0", flips(2))

    partner = lax.ppermute(mixing[..., :BLOCK], "x0", flips(2))
    beside = jnp.where(my_y == NY - 1, partner, mixing[..., BLOCK:])
    mixing = jnp.concatenate([mixing[..., :BLOCK], beside], axis=2)
    near = jnp.stack([mixing] + [lax.ppermute(mixing, "y", flips(NY, k)) for k in range(1, NY)])
    dense = expand(me, near, lax.ppermute(near, "core", flips(2)))
    grads = grad_chain(dense, mine, theirs)
    own, away = scores(me, base, dense, grads, mine, theirs)

    pieces = core_sum(me, own, lax.ppermute(away, "core", flips(2)))
    total = pieces[0].astype(F32)
    for k in range(1, NY):
        total = total + lax.ppermute(pieces[k], "y", flips(NY, k)).astype(F32)
    total = total.astype(BF)
    far = lax.ppermute(total[:, TOP], "x0", flips(2))
    last = jnp.where(my_y < NY // 2, total[:, TOP], far)
    total = jnp.concatenate([total[:, :TOP], last[:, None]], axis=1)
    total = jnp.sum(lax.all_to_all(total, "z", 0, 0).astype(F32), axis=0)
    total = total + lax.ppermute(total, "zh", flips(2))
    return finish(me, [total] + [lax.ppermute(total, "y", flips(NY, k)) for k in range(1, NY)])


def solution(mesh):
    fsdp, col = mesh.devices.shape
    names = ("x1", "x0", "z", "core", "zh", "y")
    fine = Mesh(mesh.devices.reshape(fsdp // (4 * NZ), 2, NZ, 2, col // NY, NY), names)
    rows, cols = ("x1", "x0", "z", "core"), ("zh", "y")
    return jax.shard_map(
        per_device,
        mesh=fine,
        in_specs=(P(rows, cols), P(rows, cols), P(None, rows, None), P(rows, cols)),
        out_specs=P(None, rows, None),
        check_vma=False,
    )
```

time: 489 us -> 247 us (0.51)
  waiting for transfers between devices: 346 us -> 96.5 us
  matrix products: 37.7 us -> 0 us
  Pallas kernels: 0 us -> 34.7 us
  starting transfers between devices: 53.2 us -> 76.9 us
  blocking collectives: 0 us -> 22.9 us
  other arithmetic: 21.3 us -> 1.69 us
  between operations: 14.4 us -> 0.31 us
    psum x1 -> x0, waiting for transfers between devices: 150 us -> none  [per_device(): stacked = lax.psum(stacked, 'col')]
    ppermute x15, waiting for transfers between devices: 196 us -> 51.6 us  [the longest x1 11.4 us: per_device(): theirs = lax.ppermute(mine, 'x0', flips(2))]
    all_to_all x0 -> x2, waiting for transfers between devices: none -> 44.8 us  [the longest x1 44.8 us: per_device(): got = lax.all_to_all(pack(me, upstream, factors), ('z', 'core'), 0, 0)]
    dot_general x34 -> x0, matrix products: 37.7 us -> none  [the longest x12 15.7 us: left_product(): lax.dot_general(matrix, grad, (((0,), (0,)), ((), ())), preferred_element...]
    pallas_call x0 -> x6, Pallas kernels: none -> 34.7 us  [the longest x1 12 us: scores(): pl.pallas_call(score_kernel, grid=(LEVELS,), in_specs=[SCALARS, WHOLE, pl...]
    all_to_all x0 -> x2, starting transfers between devices: none -> 24.4 us  [the longest x1 12.8 us: per_device(): got = lax.all_to_all(pack(me, upstream, factors), ('z', 'core'), 0, 0)]
    all_to_all x0 -> x1, blocking collectives: none -> 22.9 us  [per_device(): total = jnp.sum(lax.all_to_all(total, 'z', 0, 0).astype(F32), axis=0)]
    reduce_sum x7 -> x1, other arithmetic: 19.8 us -> 0.03 us  [per_device(): total = jnp.sum(lax.all_to_all(total, 'z', 0, 0).astype(F32), axis=0)]
  transfers between devices with their start and end apart: 16 -> 17, of which waited for: 6 -> 13; matrix products, arithmetic and copies ran while one was open for 13% -> 1% of each run, Pallas kernels for 0% -> 6%
where the time goes in v2:
time: 247 us; the launch traced here: 244 us
  waiting for transfers between devices  96.5 us (39%)
  starting transfers between devices  76.9 us (31%)
  Pallas kernels  34.7 us (14%)
  blocking collectives  22.9 us (9%)
  local copies, waits for them, and re-layouts  10.6 us (4%)
    all_to_all x1, waiting for transfers between devices, per_device(): got = lax.all_to_all(pack(me, upstream, factors), ('z', 'core'), 0, 0)  44.8 us
    all_to_all x1, blocking collectives, per_device(): total = jnp.sum(lax.all_to_all(total, 'z', 0, 0).astype(F32), axis=0)  22.9 us
    all_to_all x1, starting transfers between devices, per_device(): got = lax.all_to_all(pack(me, upstream, factors), ('z', 'core'), 0, 0)  12.8 us
    pallas_call x1, Pallas kernels, scores(): pl.pallas_call(score_kernel, grid=(LEVELS,), in_specs=[SCALARS, WHOLE, pl...  12 us
    all_to_all x1, starting transfers between devices, per_device(): base = lax.all_to_all(base, ('z', 'core'), 0, 0)  11.6 us
    ppermute x1, waiting for transfers between devices, per_device(): theirs = lax.ppermute(mine, 'x0', flips(2))  11.4 us
    ppermute x3, starting transfers between devices, per_device(): total = total + lax.ppermute(pieces[k], 'y', flips(NY, k)).astype(F32)  10.4 us
    ppermute x3, starting transfers between devices, per_device(): lax.ppermute(mixing, 'y', flips(NY, k))  9.82 us
  transfers between devices with their start and end apart: 17, of which 13 were waited for; matrix products, arithmetic and copies ran while one was open for 1% of the time, Pallas kernels for 6%

profile of v2, /device:TPU:24, one launch (start us, length us, event | category | flops | bytes accessed | tf_op | source)
XLA Modules:
  0.0 243.6 jit_solution(15955213838966413346)
XLA Ops:
  0.0 2.0 copy.6.factors
  2.6 2.6 %pack.1 = bf16[16,272,128]{2,1,0:T(8,128)(2,1)} custom-call(s32[5]{0:T(128)} %stack.38.me, bf16[128,3328]{1,0:T(8,128)(2,1)} %upstream.1, f32[7,128,64]{2,1,0:T(8,128)} %copy.6.factors), custom_call_target="tpu_custom_call" | custom-call | tf_op jit(solution)/shard_map/pack/pallas_call | solution.py:78
  5.3 12.8 %all-to-all-start.1 = ((bf16[16,272,128]{2,1,0:T(8,128)(2,1)}), bf16[16,272,128]{2,1,0:T(8,128)(2,1)S(1)}, u32[]{:S(2)}, u32[]{:S(2)}) async-start(bf16[16,272,128]{2,1,0:T(8,128)(2,1)} %pack.1), calls=%async_computation.1 | async-start | bytes 2228224 | tf_op jit(solution)/shard_map/all_to_all | solution.py:306
  19.5 44.8 %all-to-all-done.1 = bf16[16,272,128]{2,1,0:T(8,128)(2,1)S(1)} async-done(((bf16[16,272,128]{2,1,0:T(8,128)(2,1)}), bf16[16,272,128]{2,1,0:T(8,128)(2,1)S(1)}, u32[]{:S(2)}, u32[]{:S(2)}) %all-to-all-start.1) | async-done | bytes 1114144 | tf_op jit(solution)/shard_map/all_to_all | solution.py:306
  64.4 11.6 %all-to-all-start = ((bf16[16,208,128]{2,1,0:T(8,128)(2,1)}), bf16[16,208,128]{2,1,0:T(8,128)(2,1)S(1)}, u32[]{:S(2)}, u32[]{:S(2)}) async-start(bf16[16,208,128]{2,1,0:T(8,128)(2,1)} %bitcast.8), calls=%async_computation | async-start | bytes 1703936 | tf_op jit(solution)/shard_map/all_to_all | solution.py:310
  76.0 3.4 %collective-permute-start = (bf16[16,64,64]{2,1,0:T(8,128)(2,1)S(1)}, bf16[16,64,64]{2,1,0:T(8,128)(2,1)S(1)}, u32[]{:S(2)}, u32[]{:S(2)}) collective-permute-start(bf16[16,64,64]{2,1,0:T(8,128)(2,1)S(1)} %slice.25), channel_id=1, source_target_pairs={{0,128},{128,0},{1,129},{129,1},{2,130},{130,2},{3,131},{131,3},{4... | collective-permute-start | bytes 393224 | tf_op jit(solution)/shard_map/ppermute | solution.py:313
  79.4 7.1 %collective-permute-done = bf16[16,64,64]{2,1,0:T(8,128)(2,1)S(1)} collective-permute-done((bf16[16,64,64]{2,1,0:T(8,128)(2,1)S(1)}, bf16[16,64,64]{2,1,0:T(8,128)(2,1)S(1)}, u32[]{:S(2)}, u32[]{:S(2)}) %collective-permute-start) | collective-permute-done | bytes 131104 | tf_op jit(solution)/shard_map/ppermute | solution.py:313
  86.9 2.1 collective-permute-start.3
  89.0 4.5 %collective-permute-start.2 = (bf16[16,64,128]{2,1,0:T(8,128)(2,1)S(1)}, bf16[16,64,128]{2,1,0:T(8,128)(2,1)S(1)}, u32[]{:S(2)}, u32[]{:S(2)}) collective-permute-start(bf16[16,64,128]{2,1,0:T(8,128)(2,1)S(1)} %pad_maximum_fusion.1), channel_id=1, source_target_pairs={{0,2},{1,3},{2,0},{3,1},{4,6},{5,7},{6,4},{7,5},{8,10},{9,11},{10,... | collective-permute-start | bytes 786440 | tf_op jit(solution)/shard_map/ppermute | solution.py:316
  93.5 3.2 %collective-permute-start.1 = (bf16[16,64,128]{2,1,0:T(8,128)(2,1)S(1)}, bf16[16,64,128]{2,1,0:T(8,128)(2,1)S(1)}, u32[]{:S(2)}, u32[]{:S(2)}) collective-permute-start(bf16[16,64,128]{2,1,0:T(8,128)(2,1)S(1)} %pad_maximum_fusion.1), channel_id=1, source_target_pairs={{0,1},{1,0},{2,3},{3,2},{4,5},{5,4},{6,7},{7,6},{8,9},{9,8},{10,11... | collective-permute-start | bytes 786440 | tf_op jit(solution)/shard_map/ppermute | solution.py:316
  96.7 6.7 %collective-permute-done.3 = bf16[16,64,128]{2,1,0:T(8,128)(2,1)S(1)} collective-permute-done((bf16[16,64,128]{2,1,0:T(8,128)(2,1)S(1)}, bf16[16,64,128]{2,1,0:T(8,128)(2,1)S(1)}, u32[]{:S(2)}, u32[]{:S(2)}) %collective-permute-start.3) | collective-permute-done | bytes 262176 | tf_op jit(solution)/shard_map/ppermute | solution.py:316
  103.4 2.5 %collective-permute-done.1 = bf16[16,64,128]{2,1,0:T(8,128)(2,1)S(1)} collective-permute-done((bf16[16,64,128]{2,1,0:T(8,128)(2,1)S(1)}, bf16[16,64,128]{2,1,0:T(8,128)(2,1)S(1)}, u32[]{:S(2)}, u32[]{:S(2)}) %collective-permute-start.1) | collective-permute-done | bytes 262176 | tf_op jit(solution)/shard_map/ppermute | solution.py:316
  108.1 3.6 %collective-permute-start.5 = (bf16[16,208,128]{2,1,0:T(8,128)(2,1)S(1)}, bf16[16,208,128]{2,1,0:T(8,128)(2,1)S(1)}, u32[]{:S(2)}, u32[]{:S(2)}) collective-permute-start(bf16[16,208,128]{2,1,0:T(8,128)(2,1)S(1)} %slice.27.mine), channel_id=1, source_target_pairs={{0,128},{128,0},{1,129},{129,1},{2,130},{130,2},{3,131},{131,3},{4... | collective-permute-start | bytes 2555912 | tf_op jit(solution)/shard_map/ppermute | solution.py:311
  112.8 7.2 %expand.1.dense = bf16[7,16,128,256]{3,2,1,0:T(8,128)(2,1)} custom-call(s32[5]{0:T(128)} %stack.38.me, bf16[4,16,64,128]{3,2,1,0:T(8,128)(2,1)} %copy-done.2, bf16[4,16,64,128]{3,2,1,0:T(8,128)(2,1)} %copy-done.5), custom_call_target="tpu_custom_call" | custom-call | tf_op jit(solution)/shard_map/expand/pallas_call | solution.py:124
  120.0 11.4 %collective-permute-done.5.theirs = bf16[16,208,128]{2,1,0:T(8,128)(2,1)S(1)} collective-permute-done((bf16[16,208,128]{2,1,0:T(8,128)(2,1)S(1)}, bf16[16,208,128]{2,1,0:T(8,128)(2,1)S(1)}, u32[]{:S(2)}, u32[]{:S(2)}) %collective-permute-start.5) | collective-permute-done | bytes 852000 | tf_op jit(solution)/shard_map/ppermute | solution.py:311
  132.3 8.5 %grad_chain.1.grads = bf16[6,16,208,128]{3,2,1,0:T(8,128)(2,1)} custom-call(bf16[7,16,128,256]{3,2,1,0:T(8,128)(2,1)} %expand.1.dense, bf16[16,208,128]{2,1,0:T(8,128)(2,1)} %copy-done.1, bf16[16,208,128]{2,1,0:T(8,128)(2,1)} %copy-done.3), custom_call_target="tpu_custom_call" | custom-call | tf_op jit(solution)/shard_map/grad_chain/pallas_call | solution.py:161
  141.7 12.0 %scores.1 = (bf16[4,8,7,16,128]{4,3,2,1,0:T(8,128)(2,1)}, bf16[4,8,7,16,128]{4,3,2,1,0:T(8,128)(2,1)}) custom-call(s32[5]{0:T(128)} %stack.38.me, bf16[16,208,128]{2,1,0:T(8,128)(2,1)} %copy-done.4, bf16[7,16,128,256]{3,2,1,0:T(8,128)(2,1)} %expand.1.dense, bf16[6,16,208,128]{3,2,1,0:T(8,128)(2,1)} %grad_chain.1.grads, bf16[16,208,128]{2,1,0:T(8,128)(2,1)} %copy-done.1, ...), custom_call_target="tpu_custom_call" | custom-call | tf_op jit(solution)/shard_map/scores/pallas_call | solution.py:238
  155.6 2.6 %collective-permute-done.6.got = bf16[4,8,7,16,128]{4,3,2,1,0:T(8,128)(2,1)S(1)} collective-permute-done((bf16[4,8,7,16,128]{4,3,2,1,0:T(8,128)(2,1)}, bf16[4,8,7,16,128]{4,3,2,1,0:T(8,128)(2,1)S(1)}, u32[]{:S(2)}, u32[]{:S(2)}) %collective-permute-start.6) | collective-permute-done | bytes 917536 | tf_op jit(solution)/shard_map/ppermute | solution.py:321
  159.2 2.4 %core_sum.1 = (bf16[8,7,16,128]{3,2,1,0:T(8,128)(2,1)}, bf16[8,7,16,128]{3,2,1,0:T(8,128)(2,1)}, bf16[8,7,16,128]{3,2,1,0:T(8,128)(2,1)}, bf16[8,7,16,128]{3,2,1,0:T(8,128)(2,1)}) custom-call(s32[5]{0:T(128)} %stack.38.me, bf16[4,8,7,16,128]{4,3,2,1,0:T(8,128)(2,1)} %get-tuple-element.11.own, bf16[4,8,7,16,128]{4,3,2,1,0:T(8,128)(2,1)} %copy-done.6), custom_call_target="tpu_custom_call" | custom-call | tf_op jit(solution)/shard_map/core_sum/pallas_call | solution.py:264
  161.7 2.6 %collective-permute-start.7 = (bf16[8,7,16,128]{3,2,1,0:T(8,128)(2,1)}, bf16[8,7,16,128]{3,2,1,0:T(8,128)(2,1)S(1)}, u32[]{:S(2)}, u32[]{:S(2)}) collective-permute-start(bf16[8,7,16,128]{3,2,1,0:T(8,128)(2,1)} %get-tuple-element.14), channel_id=1, source_target_pairs={{0,1},{1,0},{2,3},{3,2},{4,5},{5,4},{6,7},{7,6},{8,9},{9,8},{10,11... | collective-permute-start | bytes 688136 | tf_op jit(solution)/shard_map/ppermute | solution.py:324
  164.3 2.9 %collective-permute-start.8 = (bf16[8,7,16,128]{3,2,1,0:T(8,128)(2,1)}, bf16[8,7,16,128]{3,2,1,0:T(8,128)(2,1)S(1)}, u32[]{:S(2)}, u32[]{:S(2)}) collective-permute-start(bf16[8,7,16,128]{3,2,1,0:T(8,128)(2,1)} %get-tuple-element.15), channel_id=1, source_target_pairs={{0,2},{1,3},{2,0},{3,1},{4,6},{5,7},{6,4},{7,5},{8,10},{9,11},{10,... | collective-permute-start | bytes 688136 | tf_op jit(solution)/shard_map/ppermute | solution.py:324
  167.3 4.9 %collective-permute-start.9 = (bf16[8,7,16,128]{3,2,1,0:T(8,128)(2,1)}, bf16[8,7,16,128]{3,2,1,0:T(8,128)(2,1)S(1)}, u32[]{:S(2)}, u32[]{:S(2)}) collective-permute-start(bf16[8,7,16,128]{3,2,1,0:T(8,128)(2,1)} %get-tuple-element.16), channel_id=1, source_target_pairs={{0,3},{1,2},{2,1},{3,0},{4,7},{5,6},{6,5},{7,4},{8,11},{9,10},{10,... | collective-permute-start | bytes 688136 | tf_op jit(solution)/shard_map/ppermute | solution.py:324
  172.2 3.9 %collective-permute-done.8 = bf16[8,7,16,128]{3,2,1,0:T(8,128)(2,1)S(1)} collective-permute-done((bf16[8,7,16,128]{3,2,1,0:T(8,128)(2,1)}, bf16[8,7,16,128]{3,2,1,0:T(8,128)(2,1)S(1)}, u32[]{:S(2)}, u32[]{:S(2)}) %collective-permute-start.8) | collective-permute-done | bytes 229408 | tf_op jit(solution)/shard_map/ppermute | solution.py:324
  176.2 4.8 %collective-permute-done.9 = bf16[8,7,16,128]{3,2,1,0:T(8,128)(2,1)S(1)} collective-permute-done((bf16[8,7,16,128]{3,2,1,0:T(8,128)(2,1)}, bf16[8,7,16,128]{3,2,1,0:T(8,128)(2,1)S(1)}, u32[]{:S(2)}, u32[]{:S(2)}) %collective-permute-start.9) | collective-permute-done | bytes 229408 | tf_op jit(solution)/shard_map/ppermute | solution.py:324
  182.1 3.4 %collective-permute-start.10 = (bf16[8,16,128]{2,1,0:T(8,128)(2,1)S(1)}, bf16[8,16,128]{2,1,0:T(8,128)(2,1)S(1)}, u32[]{:S(2)}, u32[]{:S(2)}) collective-permute-start(bf16[8,16,128]{2,1,0:T(8,128)(2,1)S(1)} %slice_bitcast_fusion), channel_id=1, source_target_pairs={{0,128},{128,0},{1,129},{129,1},{2,130},{130,2},{3,131},{131,3},{4... | collective-permute-start | bytes 98312 | tf_op jit(solution)/shard_map/ppermute | solution.py:326
  185.5 2.4 collective-permute-done.10
  187.9 22.9 %all_to_all.15 = bf16[8,7,16,128]{3,2,1,0:T(8,128)(2,1)S(1)} all-to-all(bf16[8,7,16,128]{3,2,1,0:T(8,128)(2,1)S(1)} %pad_maximum_fusion.2), channel_id=1, replica_groups=mesh['x1'=2,'x0'=2,'z'=8,'core'=2,'zh'=2,'y'=4] {'z'}, dimensions={0} | all-to-all | bytes 458752 | tf_op jit(solution)/shard_map/all_to_all | solution.py:329
  210.8 8.2 %collective-permute-start.11 = (f32[7,16,128]{2,1,0:T(8,128)S(1)}, f32[7,16,128]{2,1,0:T(8,128)S(1)}, u32[]{:S(2)}, u32[]{:S(2)}) collective-permute-start(f32[7,16,128]{2,1,0:T(8,128)S(1)} %convert_reduce_fusion), channel_id=1, source_target_pairs={{0,4},{4,0},{1,5},{5,1},{2,6},{6,2},{3,7},{7,3},{8,12},{12,8},{9,1... | collective-permute-start | bytes 172040 | tf_op jit(solution)/shard_map/ppermute | solution.py:330
  219.1 7.0 %collective-permute-done.11 = f32[7,16,128]{2,1,0:T(8,128)S(1)} collective-permute-done((f32[7,16,128]{2,1,0:T(8,128)S(1)}, f32[7,16,128]{2,1,0:T(8,128)S(1)}, u32[]{:S(2)}, u32[]{:S(2)}) %collective-permute-start.11) | collective-permute-done | bytes 57376 | tf_op jit(solution)/shard_map/ppermute | solution.py:330
  226.1 4.8 %collective-permute-start.14 = (f32[7,16,128]{2,1,0:T(8,128)S(1)}, f32[7,16,128]{2,1,0:T(8,128)S(1)}, u32[]{:S(2)}, u32[]{:S(2)}) collective-permute-start(f32[7,16,128]{2,1,0:T(8,128)S(1)} %add.27.refs_0_), channel_id=1, source_target_pairs={{0,3},{1,2},{2,1},{3,0},{4,7},{5,6},{6,5},{7,4},{8,11},{9,10},{10,... | collective-permute-start | bytes 172040 | tf_op jit(solution)/shard_map/ppermute | solution.py:331
  232.9 3.0 %collective-permute-start.12 = (f32[7,16,128]{2,1,0:T(8,128)S(1)}, f32[7,16,128]{2,1,0:T(8,128)S(1)}, u32[]{:S(2)}, u32[]{:S(2)}) collective-permute-start(f32[7,16,128]{2,1,0:T(8,128)S(1)} %add.27.refs_0_), channel_id=1, source_target_pairs={{0,1},{1,0},{2,3},{3,2},{4,5},{5,4},{6,7},{7,6},{8,9},{9,8},{10,11... | collective-permute-start | bytes 172040 | tf_op jit(solution)/shard_map/ppermute | solution.py:331
  236.0 2.6 %collective-permute-done.13.refs_2_ = f32[7,16,128]{2,1,0:T(8,128)S(1)} collective-permute-done((f32[7,16,128]{2,1,0:T(8,128)S(1)}, f32[7,16,128]{2,1,0:T(8,128)S(1)}, u32[]{:S(2)}, u32[]{:S(2)}) %collective-permute-start.13) | collective-permute-done | bytes 57376 | tf_op jit(solution)/shard_map/ppermute | solution.py:331
  (51 shorter events, 18.6 us)
Async XLA Ops:
  0.0 18.0 %copy-start = (f32[1,26]{1,0:T(1,128)S(1)}, f32[1,26]{1,0:T(1,128)}, u32[]{:S(2)}) copy-start(f32[1,26]{1,0:T(1,128)} %param.5) | copy-start | bytes 316
  5.3 12.9 %copy-start.7 = (bf16[128,3328]{1,0:T(8,128)(2,1)S(1)}, bf16[128,3328]{1,0:T(8,128)(2,1)}, u32[]{:S(2)}) copy-start(bf16[128,3328]{1,0:T(8,128)(2,1)} %param.4) | copy-start | bytes 2555908
  5.3 59.1 %all-to-all-start.1 = ((bf16[16,272,128]{2,1,0:T(8,128)(2,1)}), bf16[16,272,128]{2,1,0:T(8,128)(2,1)S(1)}, u32[]{:S(2)}, u32[]{:S(2)}) async-start(bf16[16,272,128]{2,1,0:T(8,128)(2,1)} %pack.1), calls=%async_computation.1 | async-start | bytes 2228224 | tf_op jit(solution)/shard_map/all_to_all | solution.py:306
  64.4 76.4 %all-to-all-start = ((bf16[16,208,128]{2,1,0:T(8,128)(2,1)}), bf16[16,208,128]{2,1,0:T(8,128)(2,1)S(1)}, u32[]{:S(2)}, u32[]{:S(2)}) async-start(bf16[16,208,128]{2,1,0:T(8,128)(2,1)} %bitcast.8), calls=%async_computation | async-start | bytes 1703936 | tf_op jit(solution)/shard_map/all_to_all | solution.py:310
  76.0 10.5 %collective-permute-start = (bf16[16,64,64]{2,1,0:T(8,128)(2,1)S(1)}, bf16[16,64,64]{2,1,0:T(8,128)(2,1)S(1)}, u32[]{:S(2)}, u32[]{:S(2)}) collective-permute-start(bf16[16,64,64]{2,1,0:T(8,128)(2,1)S(1)} %slice.25), channel_id=1, source_target_pairs={{0,128},{128,0},{1,129},{129,1},{2,130},{130,2},{3,131},{131,3},{4... | collective-permute-start | bytes 393224 | tf_op jit(solution)/shard_map/ppermute | solution.py:313
  86.9 16.6 %collective-permute-start.3 = (bf16[16,64,128]{2,1,0:T(8,128)(2,1)S(1)}, bf16[16,64,128]{2,1,0:T(8,128)(2,1)S(1)}, u32[]{:S(2)}, u32[]{:S(2)}) collective-permute-start(bf16[16,64,128]{2,1,0:T(8,128)(2,1)S(1)} %pad_maximum_fusion.1), channel_id=1, source_target_pairs={{0,3},{1,2},{2,1},{3,0},{4,7},{5,6},{6,5},{7,4},{8,11},{9,10},{10,... | collective-permute-start | bytes 786440 | tf_op jit(solution)/shard_map/ppermute | solution.py:316
  89.0 14.4 %collective-permute-start.2 = (bf16[16,64,128]{2,1,0:T(8,128)(2,1)S(1)}, bf16[16,64,128]{2,1,0:T(8,128)(2,1)S(1)}, u32[]{:S(2)}, u32[]{:S(2)}) collective-permute-start(bf16[16,64,128]{2,1,0:T(8,128)(2,1)S(1)} %pad_maximum_fusion.1), channel_id=1, source_target_pairs={{0,2},{1,3},{2,0},{3,1},{4,6},{5,7},{6,4},{7,5},{8,10},{9,11},{10,... | collective-permute-start | bytes 786440 | tf_op jit(solution)/shard_map/ppermute | solution.py:316
  93.5 12.5 %collective-permute-start.1 = (bf16[16,64,128]{2,1,0:T(8,128)(2,1)S(1)}, bf16[16,64,128]{2,1,0:T(8,128)(2,1)S(1)}, u32[]{:S(2)}, u32[]{:S(2)}) collective-permute-start(bf16[16,64,128]{2,1,0:T(8,128)(2,1)S(1)} %pad_maximum_fusion.1), channel_id=1, source_target_pairs={{0,1},{1,0},{2,3},{3,2},{4,5},{5,4},{6,7},{7,6},{8,9},{9,8},{10,11... | collective-permute-start | bytes 786440 | tf_op jit(solution)/shard_map/ppermute | solution.py:316
  106.1 5.6 %copy-start.2 = (bf16[4,16,64,128]{3,2,1,0:T(8,128)(2,1)}, bf16[4,16,64,128]{3,2,1,0:T(8,128)(2,1)S(1)}, u32[]{:S(2)}) copy-start(bf16[4,16,64,128]{3,2,1,0:T(8,128)(2,1)S(1)} %pad_maximum_fusion.near) | copy-start | bytes 3145732
  106.1 5.6 %collective-permute-start.4 = (bf16[4,16,64,128]{3,2,1,0:T(8,128)(2,1)S(1)}, bf16[4,16,64,128]{3,2,1,0:T(8,128)(2,1)S(1)}, u32[]{:S(2)}, u32[]{:S(2)}) collective-permute-start(bf16[4,16,64,128]{3,2,1,0:T(8,128)(2,1)S(1)} %pad_maximum_fusion.near), channel_id=1, source_target_pairs={{0,8},{8,0},{1,9},{9,1},{2,10},{10,2},{3,11},{11,3},{4,12},{12,4},... | collective-permute-start | bytes 3145736 | tf_op jit(solution)/shard_map/ppermute | solution.py:317
  108.1 11.9 %copy-start.1 = (bf16[16,208,128]{2,1,0:T(8,128)(2,1)}, bf16[16,208,128]{2,1,0:T(8,128)(2,1)S(1)}, u32[]{:S(2)}) copy-start(bf16[16,208,128]{2,1,0:T(8,128)(2,1)S(1)} %slice.27.mine) | copy-start | bytes 2555908
  108.1 23.2 %collective-permute-start.5 = (bf16[16,208,128]{2,1,0:T(8,128)(2,1)S(1)}, bf16[16,208,128]{2,1,0:T(8,128)(2,1)S(1)}, u32[]{:S(2)}, u32[]{:S(2)}) collective-permute-start(bf16[16,208,128]{2,1,0:T(8,128)(2,1)S(1)} %slice.27.mine), channel_id=1, source_target_pairs={{0,128},{128,0},{1,129},{129,1},{2,130},{130,2},{3,131},{131,3},{4... | collective-permute-start | bytes 2555912 | tf_op jit(solution)/shard_map/ppermute | solution.py:311
  111.7 1.0 copy-start.5
  131.4 0.9 copy-start.3
  140.8 0.9 copy-start.4
  153.7 4.6 %collective-permute-start.6 = (bf16[4,8,7,16,128]{4,3,2,1,0:T(8,128)(2,1)}, bf16[4,8,7,16,128]{4,3,2,1,0:T(8,128)(2,1)S(1)}, u32[]{:S(2)}, u32[]{:S(2)}) collective-permute-start(bf16[4,8,7,16,128]{4,3,2,1,0:T(8,128)(2,1)} %get-tuple-element.12), channel_id=1, source_target_pairs={{0,8},{8,0},{1,9},{9,1},{2,10},{10,2},{3,11},{11,3},{4,12},{12,4},... | collective-permute-start | bytes 2752520 | tf_op jit(solution)/shard_map/ppermute | solution.py:321
  158.3 1.0 copy-start.6
  161.7 10.5 %collective-permute-start.7 = (bf16[8,7,16,128]{3,2,1,0:T(8,128)(2,1)}, bf16[8,7,16,128]{3,2,1,0:T(8,128)(2,1)S(1)}, u32[]{:S(2)}, u32[]{:S(2)}) collective-permute-start(bf16[8,7,16,128]{3,2,1,0:T(8,128)(2,1)} %get-tuple-element.14), channel_id=1, source_target_pairs={{0,1},{1,0},{2,3},{3,2},{4,5},{5,4},{6,7},{7,6},{8,9},{9,8},{10,11... | collective-permute-start | bytes 688136 | tf_op jit(solution)/shard_map/ppermute | solution.py:324
  164.3 11.8 %collective-permute-start.8 = (bf16[8,7,16,128]{3,2,1,0:T(8,128)(2,1)}, bf16[8,7,16,128]{3,2,1,0:T(8,128)(2,1)S(1)}, u32[]{:S(2)}, u32[]{:S(2)}) collective-permute-start(bf16[8,7,16,128]{3,2,1,0:T(8,128)(2,1)} %get-tuple-element.15), channel_id=1, source_target_pairs={{0,2},{1,3},{2,0},{3,1},{4,6},{5,7},{6,4},{7,5},{8,10},{9,11},{10,... | collective-permute-start | bytes 688136 | tf_op jit(solution)/shard_map/ppermute | solution.py:324
  167.3 13.7 %collective-permute-start.9 = (bf16[8,7,16,128]{3,2,1,0:T(8,128)(2,1)}, bf16[8,7,16,128]{3,2,1,0:T(8,128)(2,1)S(1)}, u32[]{:S(2)}, u32[]{:S(2)}) collective-permute-start(bf16[8,7,16,128]{3,2,1,0:T(8,128)(2,1)} %get-tuple-element.16), channel_id=1, source_target_pairs={{0,3},{1,2},{2,1},{3,0},{4,7},{5,6},{6,5},{7,4},{8,11},{9,10},{10,... | collective-permute-start | bytes 688136 | tf_op jit(solution)/shard_map/ppermute | solution.py:324
  182.1 5.8 %collective-permute-start.10 = (bf16[8,16,128]{2,1,0:T(8,128)(2,1)S(1)}, bf16[8,16,128]{2,1,0:T(8,128)(2,1)S(1)}, u32[]{:S(2)}, u32[]{:S(2)}) collective-permute-start(bf16[8,16,128]{2,1,0:T(8,128)(2,1)S(1)} %slice_bitcast_fusion), channel_id=1, source_target_pairs={{0,128},{128,0},{1,129},{129,1},{2,130},{130,2},{3,131},{131,3},{4... | collective-permute-start | bytes 98312 | tf_op jit(solution)/shard_map/ppermute | solution.py:326
  210.8 15.2 %collective-permute-start.11 = (f32[7,16,128]{2,1,0:T(8,128)S(1)}, f32[7,16,128]{2,1,0:T(8,128)S(1)}, u32[]{:S(2)}, u32[]{:S(2)}) collective-permute-start(f32[7,16,128]{2,1,0:T(8,128)S(1)} %convert_reduce_fusion), channel_id=1, source_target_pairs={{0,4},{4,0},{1,5},{5,1},{2,6},{6,2},{3,7},{7,3},{8,12},{12,8},{9,1... | collective-permute-start | bytes 172040 | tf_op jit(solution)/shard_map/ppermute | solution.py:330
  226.1 12.9 %copy-start.8 = (f32[7,16,128]{2,1,0:T(8,128)}, f32[7,16,128]{2,1,0:T(8,128)S(1)}, u32[]{:S(2)}) copy-start(f32[7,16,128]{2,1,0:T(8,128)S(1)} %add.27.refs_0_) | copy-start | bytes 172036
  226.1 9.8 %collective-permute-start.14 = (f32[7,16,128]{2,1,0:T(8,128)S(1)}, f32[7,16,128]{2,1,0:T(8,128)S(1)}, u32[]{:S(2)}, u32[]{:S(2)}) collective-permute-start(f32[7,16,128]{2,1,0:T(8,128)S(1)} %add.27.refs_0_), channel_id=1, source_target_pairs={{0,3},{1,2},{2,1},{3,0},{4,7},{5,6},{6,5},{7,4},{8,11},{9,10},{10,... | collective-permute-start | bytes 172040 | tf_op jit(solution)/shard_map/ppermute | solution.py:331
  230.9 7.6 %collective-permute-start.13 = (f32[7,16,128]{2,1,0:T(8,128)S(1)}, f32[7,16,128]{2,1,0:T(8,128)S(1)}, u32[]{:S(2)}, u32[]{:S(2)}) collective-permute-start(f32[7,16,128]{2,1,0:T(8,128)S(1)} %add.27.refs_0_), channel_id=1, source_target_pairs={{0,2},{1,3},{2,0},{3,1},{4,6},{5,7},{6,4},{7,5},{8,10},{9,11},{10,... | collective-permute-start | bytes 172040 | tf_op jit(solution)/shard_map/ppermute | solution.py:331
  232.9 6.1 %collective-permute-start.12 = (f32[7,16,128]{2,1,0:T(8,128)S(1)}, f32[7,16,128]{2,1,0:T(8,128)S(1)}, u32[]{:S(2)}, u32[]{:S(2)}) collective-permute-start(f32[7,16,128]{2,1,0:T(8,128)S(1)} %add.27.refs_0_), channel_id=1, source_target_pairs={{0,1},{1,0},{2,3},{3,2},{4,5},{5,4},{6,7},{7,6},{8,9},{9,8},{10,11... | collective-permute-start | bytes 172040 | tf_op jit(solution)/shard_map/ppermute | solution.py:331
  235.9 3.0 %copy-start.9 = (f32[7,16,128]{2,1,0:T(8,128)}, f32[7,16,128]{2,1,0:T(8,128)S(1)}, u32[]{:S(2)}) copy-start(f32[7,16,128]{2,1,0:T(8,128)S(1)} %collective-permute-done.14.refs_3_) | copy-start | bytes 172036
  238.5 0.6 copy-start.10
  239.1 0.6 copy-start.11

commit v3 on v2

--- a/solution.py
+++ b/solution.py
@@ -18,9 +18,17 @@
 NZ = 8
 NY = 4
 SLICE = BLOCK // NY
-PARAMS = pltpu.CompilerParams(vmem_limit_bytes=58 * 2**20)
+NAMES = ("x1", "x0", "z", "core", "zh", "y")
+PARAMS = pltpu.CompilerParams(vmem_limit_bytes=16 * 2**20)
 WHOLE = pl.BlockSpec(memory_space=pltpu.VMEM)
 SCALARS = pl.BlockSpec(memory_space=pltpu.SMEM)
+
+
+class Place:
+    def __init__(self, me):
+        index = me[0]
+        self.y, self.core, self.z, self.x0 = index & 3, index >> 3 & 1, index >> 4 & 7, index >> 7 & 1
+        self.first_row = (index >> 3) * ROWS
 
 
 def dot(a, b):
@@ -59,15 +67,14 @@
             size = min(end - start, chunk - at)
             out[block, at : at + size] = turned[start - t * ROWS : start - t * ROWS + size]
             start += size
-    row = me[4] + iota((ROWS, BLOCK), 0)
-    tile = jnp.zeros((ROWS, ROWS), F32)
+    place = Place(me)
+    row = place.first_row + iota((BLOCK, ROWS), 1)
+    sides = []
     for side in range(2):
-        level = jnp.minimum(2 * me[0] + side, TOP)
+        level = jnp.minimum(2 * place.y + side, TOP)
         pick = lax.shift_right_logical(row, level + 5) % 2 * HALF + row % HALF
-        eye = (iota((ROWS, BLOCK), 1) == pick).astype(F32)
-        place = (iota((BLOCK, ROWS), 1) == iota((BLOCK, ROWS), 0) + side * BLOCK).astype(F32).astype(BF)
-        tile = tile + dot((eye + factors[level]).astype(BF), place)
-    tile = tile.astype(BF)
+        sides.append((iota((BLOCK, ROWS), 0) == pick).astype(F32) + factors[level])
+    tile = jnp.concatenate(sides, axis=0).T.astype(BF)
     for block in range(out.shape[0]):
         half = block % 2 * BLOCK
         out[block, chunk:] = tile[half : half + BLOCK]
@@ -85,8 +92,28 @@
     )(me, upstream, factors)
 
 
-def expand_kernel(me, near, away, dense):
-    my_y, my_core, my_x = me[0], me[2], me[3]
+def stack_kernel(me, *refs):
+    *parts, _, out, top = refs
+    place = Place(me)
+    for k, part in enumerate(parts):
+        out[k] = part[...]
+    which = jnp.bitwise_xor(place.y, NY - 1)
+    top[...] = out[which]
+
+
+def stack(me, parts, after):
+    return pl.pallas_call(
+        stack_kernel,
+        in_specs=[SCALARS] + [WHOLE] * NY + [pl.BlockSpec(memory_space=pl.ANY)],
+        out_specs=[WHOLE] * 2,
+        out_shape=[jax.ShapeDtypeStruct((NY,) + parts[0].shape, BF), jax.ShapeDtypeStruct(parts[0].shape, BF)],
+        compiler_params=PARAMS,
+        name="stack",
+    )(me, *parts, after)
+
+
+def expand_kernel(me, near, away, partner_near, partner_away, dense):
+    place = Place(me)
 
     def run(level):
         width = ROWS if level < 2 else 2 * ROWS
@@ -99,11 +126,11 @@
         elif level < TOP:
             pick = src == lane + col // ROWS * HALF + col % HALF
         else:
-            pick = src == HALF * my_x + col // ROWS * BLOCK + col % HALF
+            pick = src == HALF * place.x0 + col % HALF
         pick = pick.astype(F32).astype(BF)
-        which = jnp.bitwise_xor(my_y, level // 2)
-        for c, ref in enumerate((near, away)):
-            at = pl.multiple_of(jnp.bitwise_xor(my_core, c) * BLOCK, BLOCK)
+        which = jnp.bitwise_xor(place.y, level // 2)
+        for c, (ref, partner) in enumerate(((near, partner_near), (away, partner_away))):
+            at = pl.multiple_of(jnp.bitwise_xor(place.core, c) * BLOCK, BLOCK)
             row, col = at + iota((BLOCK, width), 0), iota((BLOCK, width), 1)
             if level == 0:
                 keep = row // BLOCK == col // BLOCK
@@ -112,24 +139,27 @@
             else:
                 keep = row // HALF == (col // HALF) % 4
             for block in range(2 * NZ):
-                full = jnp.where(keep, dot(ref[which, block], pick), 0.0).astype(BF)
-                dense[0, block, pl.ds(at, BLOCK), :width] = full
+                if level == TOP:
+                    full = jnp.concatenate([dot(ref[which, block], pick[:, :ROWS]), dot(partner[block], pick[:, ROWS:])], axis=1)
+                else:
+                    full = dot(ref[which, block], pick)
+                dense[0, block, pl.ds(at, BLOCK), :width] = jnp.where(keep, full, 0.0).astype(BF)
 
     for level in range(LEVELS):
         pl.when(pl.program_id(0) == level)(functools.partial(run, level))
 
 
-def expand(me, near, away):
+def expand(me, near, away, partner_near, partner_away):
     shape = (2 * NZ, ROWS, 2 * ROWS)
     return pl.pallas_call(
         expand_kernel,
         grid=(LEVELS,),
-        in_specs=[SCALARS, WHOLE, WHOLE],
+        in_specs=[SCALARS] + [WHOLE] * 4,
         out_specs=pl.BlockSpec((1,) + shape, lambda s: (s, 0, 0, 0)),
         out_shape=jax.ShapeDtypeStruct((LEVELS,) + shape, BF),
         compiler_params=PARAMS,
         name="expand",
-    )(me, near, away)
+    )(me, near, away, partner_near, partner_away)
 
 
 def grad_kernel(dense, mine, theirs, grads, state):
@@ -179,7 +209,7 @@
 
 
 def score_kernel(me, base, dense, grads, mine, theirs, own, away, state):
-    first_core = me[2] == 0
+    first_core = Place(me).core == 0
 
     def store(z, parts):
         zero, one = parts
@@ -254,87 +284,80 @@
     )(me, base, dense, grads, mine, theirs)
 
 
-def core_sum_kernel(me, own, got, *outs):
-    for k, out in enumerate(outs):
-        y = jnp.bitwise_xor(me[0], k)
-        out[...] = (own[y].astype(F32) + got[y].astype(F32)).astype(BF)
-
-
-def core_sum(me, own, got):
-    return pl.pallas_call(
-        core_sum_kernel,
-        in_specs=[SCALARS, WHOLE, WHOLE],
-        out_specs=[WHOLE] * NY,
-        out_shape=[jax.ShapeDtypeStruct(own.shape[1:], BF)] * NY,
-        compiler_params=PARAMS,
-        name="core_sum",
-    )(me, own, got)
-
-
-def finish_kernel(me, *refs):
-    *pieces, out, rows = refs
-    for k, piece in enumerate(pieces):
-        y = jnp.bitwise_xor(me[0], k)
-        rows[:, pl.ds(pl.multiple_of(y * SLICE, SLICE), SLICE), :] = piece[...]
-    for level in range(TOP):
-        out[level] = rows[level].T
-    last = rows[TOP]
-    swapped = jnp.concatenate([last[HALF:], last[:HALF]], axis=0)
-    out[TOP] = jnp.where(me[3] == 0, last, swapped).T
-
-
-def finish(me, pieces):
-    return pl.pallas_call(
-        finish_kernel,
-        in_specs=[SCALARS] + [WHOLE] * NY,
+def call(kernel, shape, *args):
+    return pl.pallas_call(
+        kernel,
+        in_specs=[SCALARS] + [WHOLE] * (len(args) - 1),
         out_specs=WHOLE,
-        out_shape=jax.ShapeDtypeStruct((LEVELS, ROWS, BLOCK), F32),
-        scratch_shapes=[pltpu.VMEM((LEVELS, BLOCK, ROWS), F32)],
-        compiler_params=PARAMS,
-        name="finish",
-    )(me, *pieces)
+        out_shape=shape,
+        compiler_params=PARAMS,
+        name=kernel.__name__,
+    )(*args)
+
+
+def core_sum(me, own, got, out):
+    for y in range(NY):
+        out[y] = (own[y].astype(F32) + got[y].astype(F32)).astype(BF)
+
+
+def copies_of_sum(me, parts, out):
+    total = parts[0].astype(F32)
+    for k in range(1, parts.shape[0]):
+        total = total + parts[k].astype(F32)
+    for k in range(out.shape[0]):
+        out[k] = total.astype(out.dtype)
+
+
+def finish(me, slices, out):
+    my_x = Place(me).x0
+    own, other = my_x * NY, (1 - my_x) * NY
+    for y in range(NY):
+        at = slice(y * SLICE, (y + 1) * SLICE)
+        out[:TOP, at] = slices[own + y, :TOP].astype(F32)
+    near = [slices[own + y, TOP].astype(F32) for y in range(NY // 2)]
+    far = [slices[other + y, TOP].astype(F32) for y in range(NY // 2, NY)]
+    for h, (even, odd) in enumerate(((near, far), (far, near))):
+        for y in range(NY // 2):
+            at = h * HALF + y * SLICE
+            out[TOP, at : at + SLICE] = jnp.where(my_x == 0, even[y], odd[y])
 
 
 def per_device(codes, scales, factors, upstream):
     rows, wide = codes.shape
     blocks = 2 * NZ
     chunk = wide // blocks
-    side, my_z, my_core, my_y = (lax.axis_index(name) for name in ("x0", "z", "core", "y"))
-    first = (((lax.axis_index("x1") * 2 + side) * NZ + my_z) * 2 + my_core) * rows
-    me = jnp.stack([my_y, my_z, my_core, side, first]).astype(jnp.int32)
-
-    got = lax.all_to_all(pack(me, upstream, factors), ("z", "core"), 0, 0)
+    me = lax.axis_index(NAMES).astype(jnp.int32).reshape(1)
+
+    got = lax.all_to_all(pack(me, upstream, factors.transpose(0, 2, 1)), ("z", "core"), 0, 0)
     mine, mixing = got[:, :chunk], got[:, chunk:]
     base = codes.astype(F32).reshape(rows, wide // rows, rows) * scales[0][None, :, None]
     base = base.reshape(rows, wide).astype(BF).T.reshape(blocks, chunk, rows)
     base = lax.all_to_all(base, ("z", "core"), 0, 0)
     theirs = lax.ppermute(mine, "x0", flips(2))
 
-    partner = lax.ppermute(mixing[..., :BLOCK], "x0", flips(2))
-    beside = jnp.where(my_y == NY - 1, partner, mixing[..., BLOCK:])
-    mixing = jnp.concatenate([mixing[..., :BLOCK], beside], axis=2)
-    near = jnp.stack([mixing] + [lax.ppermute(mixing, "y", flips(NY, k)) for k in range(1, NY)])
-    dense = expand(me, near, lax.ppermute(near, "core", flips(2)))
+    near = [mixing] + [lax.ppermute(mixing, "y", flips(NY, k)) for k in range(1, NY)]
+    near, top = stack(me, near, theirs)
+    away = lax.ppermute(near, "core", flips(2))
+    partner_near = lax.ppermute(top, "x0", flips(2))
+    partner_away = lax.ppermute(top, ("x0", "core"), flips(4, 3))
+    dense = expand(me, near, away, partner_near, partner_away)
     grads = grad_chain(dense, mine, theirs)
     own, away = scores(me, base, dense, grads, mine, theirs)
 
-    pieces = core_sum(me, own, lax.ppermute(away, "core", flips(2)))
-    total = pieces[0].astype(F32)
-    for k in range(1, NY):
-        total = total + lax.ppermute(pieces[k], "y", flips(NY, k)).astype(F32)
-    total = total.astype(BF)
-    far = lax.ppermute(total[:, TOP], "x0", flips(2))
-    last = jnp.where(my_y < NY // 2, total[:, TOP], far)
-    total = jnp.concatenate([total[:, :TOP], last[:, None]], axis=1)
-    total = jnp.sum(lax.all_to_all(total, "z", 0, 0).astype(F32), axis=0)
-    total = total + lax.ppermute(total, "zh", flips(2))
-    return finish(me, [total] + [lax.ppermute(total, "y", flips(NY, k)) for k in range(1, NY)])
+    part = (LEVELS, SLICE, rows)
+    total = call(core_sum, jax.ShapeDtypeStruct(own.shape, BF), me, own, lax.ppermute(away, "core", flips(2)))
+    total = lax.all_to_all(total, "y", 0, 0)
+    total = call(copies_of_sum, jax.ShapeDtypeStruct((2, NZ) + part, BF), me, total)
+    total = lax.all_to_all(total.reshape((2 * NZ,) + part), ("zh", "z"), 0, 0)
+    total = call(copies_of_sum, jax.ShapeDtypeStruct((2 * NY,) + part, BF), me, total)
+    total = lax.all_to_all(total, ("x0", "y"), 0, 0)
+    total = call(finish, jax.ShapeDtypeStruct((LEVELS, BLOCK, rows), F32), me, total)
+    return total.transpose(0, 2, 1)
 
 
 def solution(mesh):
     fsdp, col = mesh.devices.shape
-    names = ("x1", "x0", "z", "core", "zh", "y")
-    fine = Mesh(mesh.devices.reshape(fsdp // (4 * NZ), 2, NZ, 2, col // NY, NY), names)
+    fine = Mesh(mesh.devices.reshape(fsdp // (4 * NZ), 2, NZ, 2, col // NY, NY), NAMES)
     rows, cols = ("x1", "x0", "z", "core"), ("zh", "y")
     return jax.shard_map(
         per_device,

time: 247 us -> 209 us (0.85)
  blocking collectives: 22.9 us -> 59.5 us
  starting transfers between devices: 76.9 us -> 47.4 us
  waiting for transfers between devices: 96.5 us -> 67 us
  Pallas kernels: 34.7 us -> 16.1 us
  local copies, waits for them, and re-layouts: 10.6 us -> 15.2 us
    all_to_all x1 -> x3, blocking collectives: 22.9 us -> 59.5 us  [the longest x1 33.9 us: per_device(): total = lax.all_to_all(total.reshape((2 * NZ,) + part), ('zh', 'z'), 0, 0)]
    ppermute x11 -> x4, starting transfers between devices: 39.1 us -> 9.97 us  [the longest x1 3.46 us: per_device(): partner_near = lax.ppermute(top, 'x0', flips(2))]
    ppermute x11 -> x4, waiting for transfers between devices: 31 us -> 12.4 us  [the longest x1 6.25 us: per_device(): partner_near = lax.ppermute(top, 'x0', flips(2))]
    ppermute x1, waiting for transfers between devices: 11.4 us -> 0.01 us  [per_device(): theirs = lax.ppermute(mine, 'x0', flips(2))]
    pallas_call x3 -> x6, Pallas kernels: 11.6 us -> 4.63 us  [the longest x1 3.44 us: expand(): pl.pallas_call(expand_kernel, grid=(LEVELS,), in_specs=[SCALARS] + [WHOLE...]
    unnamed x25 -> x18, local copies, waits for them, and re-layouts: 6.64 us -> 12.8 us
    pallas_call x1, Pallas kernels: 8.48 us -> 3.01 us  [grad_chain(): pl.pallas_call(grad_kernel, grid=(TOP,), in_specs=[pl.BlockSpec((1, block...]
    pallas_call x1, Pallas kernels: 12 us -> 7.16 us  [scores(): pl.pallas_call(score_kernel, grid=(LEVELS,), in_specs=[SCALARS, WHOLE, pl...]
  transfers between devices with their start and end apart: 17 -> 10, of which waited for: 13 -> 6; matrix products, arithmetic and copies ran while one was open for 1% -> 1% of each run, Pallas kernels for 6% -> 3%
where the time goes in v3:
time: 209 us; the launch traced here: 206 us
  waiting for transfers between devices  67 us (32%)
  blocking collectives  59.5 us (28%)
  starting transfers between devices  47.4 us (23%)
  Pallas kernels  16.1 us (8%)
  local copies, waits for them, and re-layouts  15.2 us (7%)
    all_to_all x1, waiting for transfers between devices, per_device(): lax.all_to_all(pack(me, upstream, factors.transpose(0, 2, 1)), ('z', 'cor...  44.8 us
    all_to_all x1, blocking collectives, per_device(): total = lax.all_to_all(total.reshape((2 * NZ,) + part), ('zh', 'z'), 0, 0)  33.9 us
    all_to_all x1, blocking collectives, per_device(): total = lax.all_to_all(total, 'y', 0, 0)  16.4 us
    unnamed x18, local copies, waits for them, and re-layouts  12.8 us
    all_to_all x1, starting transfers between devices, per_device(): lax.all_to_all(pack(me, upstream, factors.transpose(0, 2, 1)), ('z', 'cor...  12.6 us
    all_to_all x1, starting transfers between devices, per_device(): base = lax.all_to_all(base, ('z', 'core'), 0, 0)  11.6 us
    ppermute x3, starting transfers between devices, per_device(): lax.ppermute(mixing, 'y', flips(NY, k))  9.82 us
    ppermute x3, waiting for transfers between devices, per_device(): lax.ppermute(mixing, 'y', flips(NY, k))  9.78 us
  transfers between devices with their start and end apart: 10, of which 6 were waited for; matrix products, arithmetic and copies ran while one was open for 1% of the time, Pallas kernels for 3%

profile of v3, /device:TPU:24, one launch (start us, length us, event | category | flops | bytes accessed | tf_op | source)
XLA Modules:
  0.0 205.6 jit_solution(7475417004020938011)
XLA Ops:
  0.0 1.2 copy-done.5
  1.2 0.9 copy-done.6
  2.1 1.3 pack.1
  3.5 12.6 %all-to-all-start.1 = ((bf16[16,272,128]{2,1,0:T(8,128)(2,1)}), bf16[16,272,128]{2,1,0:T(8,128)(2,1)S(1)}, u32[]{:S(2)}, u32[]{:S(2)}) async-start(bf16[16,272,128]{2,1,0:T(8,128)(2,1)} %pack.1), calls=%async_computation.1 | async-start | bytes 2228224 | tf_op jit(solution)/shard_map/all_to_all | solution.py:331
  16.3 1.3 copy.5
  17.6 44.8 %all-to-all-done.1 = bf16[16,272,128]{2,1,0:T(8,128)(2,1)S(1)} async-done(((bf16[16,272,128]{2,1,0:T(8,128)(2,1)}), bf16[16,272,128]{2,1,0:T(8,128)(2,1)S(1)}, u32[]{:S(2)}, u32[]{:S(2)}) %all-to-all-start.1) | async-done | bytes 1114144 | tf_op jit(solution)/shard_map/all_to_all | solution.py:331
  62.4 11.6 %all-to-all-start = ((bf16[16,208,128]{2,1,0:T(8,128)(2,1)}), bf16[16,208,128]{2,1,0:T(8,128)(2,1)S(1)}, u32[]{:S(2)}, u32[]{:S(2)}) async-start(bf16[16,208,128]{2,1,0:T(8,128)(2,1)} %bitcast.4), calls=%async_computation | async-start | bytes 1703936 | tf_op jit(solution)/shard_map/all_to_all | solution.py:335
  74.2 3.4 %collective-permute-start.3 = (bf16[16,208,128]{2,1,0:T(8,128)(2,1)S(1)}, bf16[16,208,128]{2,1,0:T(8,128)(2,1)S(1)}, u32[]{:S(2)}, u32[]{:S(2)}) collective-permute-start(bf16[16,208,128]{2,1,0:T(8,128)(2,1)S(1)} %slice.9.mine), channel_id=1, source_target_pairs={{0,128},{128,0},{1,129},{129,1},{2,130},{130,2},{3,131},{131,3},{4... | collective-permute-start | bytes 2555912 | tf_op jit(solution)/shard_map/ppermute | solution.py:336
  77.6 1.0 slice.8.refs_0_
  78.5 2.1 %collective-permute-start.2 = (bf16[16,64,128]{2,1,0:T(8,128)(2,1)S(1)}, bf16[16,64,128]{2,1,0:T(8,128)(2,1)S(1)}, u32[]{:S(2)}, u32[]{:S(2)}) collective-permute-start(bf16[16,64,128]{2,1,0:T(8,128)(2,1)S(1)} %slice.8.refs_0_), channel_id=1, source_target_pairs={{0,3},{1,2},{2,1},{3,0},{4,7},{5,6},{6,5},{7,4},{8,11},{9,10},{10,... | collective-permute-start | bytes 786440 | tf_op jit(solution)/shard_map/ppermute | solution.py:338
  80.7 4.5 %collective-permute-start.1 = (bf16[16,64,128]{2,1,0:T(8,128)(2,1)S(1)}, bf16[16,64,128]{2,1,0:T(8,128)(2,1)S(1)}, u32[]{:S(2)}, u32[]{:S(2)}) collective-permute-start(bf16[16,64,128]{2,1,0:T(8,128)(2,1)S(1)} %slice.8.refs_0_), channel_id=1, source_target_pairs={{0,2},{1,3},{2,0},{3,1},{4,6},{5,7},{6,4},{7,5},{8,10},{9,11},{10,... | collective-permute-start | bytes 786440 | tf_op jit(solution)/shard_map/ppermute | solution.py:338
  85.2 3.2 %collective-permute-start = (bf16[16,64,128]{2,1,0:T(8,128)(2,1)S(1)}, bf16[16,64,128]{2,1,0:T(8,128)(2,1)S(1)}, u32[]{:S(2)}, u32[]{:S(2)}) collective-permute-start(bf16[16,64,128]{2,1,0:T(8,128)(2,1)S(1)} %slice.8.refs_0_), channel_id=1, source_target_pairs={{0,1},{1,0},{2,3},{3,2},{4,5},{5,4},{6,7},{7,6},{8,9},{9,8},{10,11... | collective-permute-start | bytes 786440 | tf_op jit(solution)/shard_map/ppermute | solution.py:338
  88.4 7.2 %collective-permute-done.2.refs_3_ = bf16[16,64,128]{2,1,0:T(8,128)(2,1)S(1)} collective-permute-done((bf16[16,64,128]{2,1,0:T(8,128)(2,1)S(1)}, bf16[16,64,128]{2,1,0:T(8,128)(2,1)S(1)}, u32[]{:S(2)}, u32[]{:S(2)}) %collective-permute-start.2) | collective-permute-done | bytes 262176 | tf_op jit(solution)/shard_map/ppermute | solution.py:338
  95.6 2.5 %collective-permute-done.refs_1_ = bf16[16,64,128]{2,1,0:T(8,128)(2,1)S(1)} collective-permute-done((bf16[16,64,128]{2,1,0:T(8,128)(2,1)S(1)}, bf16[16,64,128]{2,1,0:T(8,128)(2,1)S(1)}, u32[]{:S(2)}, u32[]{:S(2)}) %collective-permute-start) | collective-permute-done | bytes 262176 | tf_op jit(solution)/shard_map/ppermute | solution.py:338
  98.3 1.9 collective-permute-start.4
  100.2 2.7 %collective-permute-start.6 = (bf16[16,64,128]{2,1,0:T(8,128)(2,1)S(1)}, bf16[16,64,128]{2,1,0:T(8,128)(2,1)S(1)}, u32[]{:S(2)}, u32[]{:S(2)}) collective-permute-start(bf16[16,64,128]{2,1,0:T(8,128)(2,1)S(1)} %get-tuple-element.10), channel_id=1, source_target_pairs={{0,136},{8,128},{128,8},{136,0},{1,137},{9,129},{129,9},{137,1},{2... | collective-permute-start | bytes 786440 | tf_op jit(solution)/shard_map/ppermute | solution.py:342
  102.9 3.5 %collective-permute-start.5 = (bf16[16,64,128]{2,1,0:T(8,128)(2,1)S(1)}, bf16[16,64,128]{2,1,0:T(8,128)(2,1)S(1)}, u32[]{:S(2)}, u32[]{:S(2)}) collective-permute-start(bf16[16,64,128]{2,1,0:T(8,128)(2,1)S(1)} %get-tuple-element.10), channel_id=1, source_target_pairs={{0,128},{128,0},{1,129},{129,1},{2,130},{130,2},{3,131},{131,3},{4... | collective-permute-start | bytes 786440 | tf_op jit(solution)/shard_map/ppermute | solution.py:341
  106.3 3.7 %collective-permute-done.6.partner_away = bf16[16,64,128]{2,1,0:T(8,128)(2,1)S(1)} collective-permute-done((bf16[16,64,128]{2,1,0:T(8,128)(2,1)S(1)}, bf16[16,64,128]{2,1,0:T(8,128)(2,1)S(1)}, u32[]{:S(2)}, u32[]{:S(2)}) %collective-permute-start.6) | collective-permute-done | bytes 262176 | tf_op jit(solution)/shard_map/ppermute | solution.py:342
  110.0 6.2 %collective-permute-done.5.partner_near = bf16[16,64,128]{2,1,0:T(8,128)(2,1)S(1)} collective-permute-done((bf16[16,64,128]{2,1,0:T(8,128)(2,1)S(1)}, bf16[16,64,128]{2,1,0:T(8,128)(2,1)S(1)}, u32[]{:S(2)}, u32[]{:S(2)}) %collective-permute-start.5) | collective-permute-done | bytes 262176 | tf_op jit(solution)/shard_map/ppermute | solution.py:341
  116.3 3.4 %expand.1.dense = bf16[7,16,128,256]{3,2,1,0:T(8,128)(2,1)S(1)} custom-call(s32[1]{0:T(128)} %bitcast.me, bf16[4,16,64,128]{3,2,1,0:T(8,128)(2,1)S(1)} %get-tuple-element.9.near, bf16[4,16,64,128]{3,2,1,0:T(8,128)(2,1)S(1)} %collective-permute-done.4.away, bf16[16,64,128]{2,1,0:T(8,128)(2,1)S(1)} %collective-permute-done.5.partner_near, ...), custom_call_target="tpu_custom_call" | custom-call | tf_op jit(solution)/shard_map/expand/pallas_call | solution.py:154
  119.8 3.0 %grad_chain.1.grads = bf16[6,16,208,128]{3,2,1,0:T(8,128)(2,1)S(1)} custom-call(bf16[7,16,128,256]{3,2,1,0:T(8,128)(2,1)S(1)} %expand.1.dense, bf16[16,208,128]{2,1,0:T(8,128)(2,1)S(1)} %slice.9.mine, bf16[16,208,128]{2,1,0:T(8,128)(2,1)S(1)} %collective-permute-done.3.refs_4_.theirs), custom_call_target="tpu_custom_call" | custom-call | tf_op jit(solution)/shard_map/grad_chain/pallas_call | solution.py:191
  122.8 2.9 %copy-done.1 = bf16[7,16,128,256]{3,2,1,0:T(8,128)(2,1)} copy-done((bf16[7,16,128,256]{3,2,1,0:T(8,128)(2,1)}, bf16[7,16,128,256]{3,2,1,0:T(8,128)(2,1)S(1)}, u32[]{:S(2)}) %copy-start.1) | copy-done | bytes 7340056
  125.7 2.2 %copy-done.3 = bf16[6,16,208,128]{3,2,1,0:T(8,128)(2,1)} copy-done((bf16[6,16,208,128]{3,2,1,0:T(8,128)(2,1)}, bf16[6,16,208,128]{3,2,1,0:T(8,128)(2,1)S(1)}, u32[]{:S(2)}) %copy-start.3) | copy-done | bytes 5111832
  128.0 3.1 %copy-done.2 = bf16[7,16,128,256]{3,2,1,0:T(8,128)(2,1)S(1)} copy-done((bf16[7,16,128,256]{3,2,1,0:T(8,128)(2,1)S(1)}, bf16[7,16,128,256]{3,2,1,0:T(8,128)(2,1)}, u32[]{:S(2)}) %copy-start.2) | copy-done | bytes 7340056
  131.0 2.4 %copy-done.4 = bf16[6,16,208,128]{3,2,1,0:T(8,128)(2,1)S(1)} copy-done((bf16[6,16,208,128]{3,2,1,0:T(8,128)(2,1)S(1)}, bf16[6,16,208,128]{3,2,1,0:T(8,128)(2,1)}, u32[]{:S(2)}) %copy-start.4) | copy-done | bytes 5111832
  133.5 7.2 %scores.1 = (bf16[4,8,7,16,128]{4,3,2,1,0:T(8,128)(2,1)S(1)}, bf16[4,8,7,16,128]{4,3,2,1,0:T(8,128)(2,1)S(1)}) custom-call(s32[1]{0:T(128)} %bitcast.me, bf16[16,208,128]{2,1,0:T(8,128)(2,1)S(1)} %all-to-all-done.base, bf16[7,16,128,256]{3,2,1,0:T(8,128)(2,1)S(1)} %copy-done.2, bf16[6,16,208,128]{3,2,1,0:T(8,128)(2,1)S(1)} %copy-done.4, ...), custom_call_target="tpu_custom_call" | custom-call | tf_op jit(solution)/shard_map/scores/pallas_call | solution.py:268
  140.7 1.9 collective-permute-start.7
  142.6 2.4 %collective-permute-done.7.got = bf16[4,8,7,16,128]{4,3,2,1,0:T(8,128)(2,1)S(1)} collective-permute-done((bf16[4,8,7,16,128]{4,3,2,1,0:T(8,128)(2,1)S(1)}, bf16[4,8,7,16,128]{4,3,2,1,0:T(8,128)(2,1)S(1)}, u32[]{:S(2)}, u32[]{:S(2)}) %collective-permute-start.7) | collective-permute-done | bytes 917536 | tf_op jit(solution)/shard_map/ppermute | solution.py:348
  145.2 16.4 %all_to_all.25.parts = bf16[4,8,7,16,128]{4,3,2,1,0:T(8,128)(2,1)S(1)} all-to-all(bf16[4,8,7,16,128]{4,3,2,1,0:T(8,128)(2,1)S(1)} %core_sum.1), channel_id=1, replica_groups=mesh['x1'=2,'x0'=2,'z'=8,'core'=2,'zh'=2,'y'=4] {'y'}, dimensions={0} | all-to-all | bytes 1835008 | tf_op jit(solution)/shard_map/all_to_all | solution.py:349
  161.8 33.9 %all_to_all.26.parts = bf16[16,7,16,128]{3,2,1,0:T(8,128)(2,1)S(1)} all-to-all(bf16[16,7,16,128]{3,2,1,0:T(8,128)(2,1)S(1)} %bitcast.11), channel_id=1, replica_groups=mesh['x1'=2,'x0'=2,'z'=8,'core'=2,'zh'=2,'y'=4] {'zh','z'}, dimensions={0} | all-to-all | bytes 917504 | tf_op jit(solution)/shard_map/all_to_all | solution.py:351
  195.7 9.2 %all_to_all.27.slices = bf16[8,7,16,128]{3,2,1,0:T(8,128)(2,1)S(1)} all-to-all(bf16[8,7,16,128]{3,2,1,0:T(8,128)(2,1)S(1)} %copies_of_sum.3), channel_id=1, replica_groups=mesh['x1'=2,'x0'=2,'z'=8,'core'=2,'zh'=2,'y'=4] {'x0','y'}, dimensions={0} | all-to-all | bytes 458752 | tf_op jit(solution)/shard_map/all_to_all | solution.py:353
  204.9 0.7 finish.1
  (23 shorter events, 0.8 us)
Async XLA Ops:
  0.0 16.1 %copy-start = (f32[1,26]{1,0:T(1,128)S(1)}, f32[1,26]{1,0:T(1,128)}, u32[]{:S(2)}) copy-start(f32[1,26]{1,0:T(1,128)} %param.5) | copy-start | bytes 316
  0.0 1.2 copy-start.5
  1.2 0.9 copy-start.6
  2.1 14.1 %copy-start.8 = (bf16[128,3328]{1,0:T(8,128)(2,1)S(1)}, bf16[128,3328]{1,0:T(8,128)(2,1)}, u32[]{:S(2)}) copy-start(bf16[128,3328]{1,0:T(8,128)(2,1)} %param.4) | copy-start | bytes 2555908
  3.5 59.0 %all-to-all-start.1 = ((bf16[16,272,128]{2,1,0:T(8,128)(2,1)}), bf16[16,272,128]{2,1,0:T(8,128)(2,1)S(1)}, u32[]{:S(2)}, u32[]{:S(2)}) async-start(bf16[16,272,128]{2,1,0:T(8,128)(2,1)} %pack.1), calls=%async_computation.1 | async-start | bytes 2228224 | tf_op jit(solution)/shard_map/all_to_all | solution.py:331
  62.4 11.6 %copy-start.7 = (bf16[16,272,128]{2,1,0:T(8,128)(2,1)}, bf16[16,272,128]{2,1,0:T(8,128)(2,1)S(1)}, u32[]{:S(2)}) copy-start(bf16[16,272,128]{2,1,0:T(8,128)(2,1)S(1)} %all-to-all-done.1) | copy-start | bytes 3342340
  62.4 65.5 %all-to-all-start = ((bf16[16,208,128]{2,1,0:T(8,128)(2,1)}), bf16[16,208,128]{2,1,0:T(8,128)(2,1)S(1)}, u32[]{:S(2)}, u32[]{:S(2)}) async-start(bf16[16,208,128]{2,1,0:T(8,128)(2,1)} %bitcast.4), calls=%async_computation | async-start | bytes 1703936 | tf_op jit(solution)/shard_map/all_to_all | solution.py:335
  74.2 24.0 %collective-permute-start.3 = (bf16[16,208,128]{2,1,0:T(8,128)(2,1)S(1)}, bf16[16,208,128]{2,1,0:T(8,128)(2,1)S(1)}, u32[]{:S(2)}, u32[]{:S(2)}) collective-permute-start(bf16[16,208,128]{2,1,0:T(8,128)(2,1)S(1)} %slice.9.mine), channel_id=1, source_target_pairs={{0,128},{128,0},{1,129},{129,1},{2,130},{130,2},{3,131},{131,3},{4... | collective-permute-start | bytes 2555912 | tf_op jit(solution)/shard_map/ppermute | solution.py:336
  78.5 17.1 %collective-permute-start.2 = (bf16[16,64,128]{2,1,0:T(8,128)(2,1)S(1)}, bf16[16,64,128]{2,1,0:T(8,128)(2,1)S(1)}, u32[]{:S(2)}, u32[]{:S(2)}) collective-permute-start(bf16[16,64,128]{2,1,0:T(8,128)(2,1)S(1)} %slice.8.refs_0_), channel_id=1, source_target_pairs={{0,3},{1,2},{2,1},{3,0},{4,7},{5,6},{6,5},{7,4},{8,11},{9,10},{10,... | collective-permute-start | bytes 786440 | tf_op jit(solution)/shard_map/ppermute | solution.py:338
  80.7 14.9 %collective-permute-start.1 = (bf16[16,64,128]{2,1,0:T(8,128)(2,1)S(1)}, bf16[16,64,128]{2,1,0:T(8,128)(2,1)S(1)}, u32[]{:S(2)}, u32[]{:S(2)}) collective-permute-start(bf16[16,64,128]{2,1,0:T(8,128)(2,1)S(1)} %slice.8.refs_0_), channel_id=1, source_target_pairs={{0,2},{1,3},{2,0},{3,1},{4,6},{5,7},{6,4},{7,5},{8,10},{9,11},{10,... | collective-permute-start | bytes 786440 | tf_op jit(solution)/shard_map/ppermute | solution.py:338
  85.2 13.0 %collective-permute-start = (bf16[16,64,128]{2,1,0:T(8,128)(2,1)S(1)}, bf16[16,64,128]{2,1,0:T(8,128)(2,1)S(1)}, u32[]{:S(2)}, u32[]{:S(2)}) collective-permute-start(bf16[16,64,128]{2,1,0:T(8,128)(2,1)S(1)} %slice.8.refs_0_), channel_id=1, source_target_pairs={{0,1},{1,0},{2,3},{3,2},{4,5},{5,4},{6,7},{7,6},{8,9},{9,8},{10,11... | collective-permute-start | bytes 786440 | tf_op jit(solution)/shard_map/ppermute | solution.py:338
  98.3 18.0 %collective-permute-start.4 = (bf16[4,16,64,128]{3,2,1,0:T(8,128)(2,1)S(1)}, bf16[4,16,64,128]{3,2,1,0:T(8,128)(2,1)S(1)}, u32[]{:S(2)}, u32[]{:S(2)}) collective-permute-start(bf16[4,16,64,128]{3,2,1,0:T(8,128)(2,1)S(1)} %get-tuple-element.9.near), channel_id=1, source_target_pairs={{0,8},{8,0},{1,9},{9,1},{2,10},{10,2},{3,11},{11,3},{4,12},{12,4},... | collective-permute-start | bytes 3145736 | tf_op jit(solution)/shard_map/ppermute | solution.py:340
  100.2 9.9 %collective-permute-start.6 = (bf16[16,64,128]{2,1,0:T(8,128)(2,1)S(1)}, bf16[16,64,128]{2,1,0:T(8,128)(2,1)S(1)}, u32[]{:S(2)}, u32[]{:S(2)}) collective-permute-start(bf16[16,64,128]{2,1,0:T(8,128)(2,1)S(1)} %get-tuple-element.10), channel_id=1, source_target_pairs={{0,136},{8,128},{128,8},{136,0},{1,137},{9,129},{129,9},{137,1},{2... | collective-permute-start | bytes 786440 | tf_op jit(solution)/shard_map/ppermute | solution.py:342
  102.9 13.4 %collective-permute-start.5 = (bf16[16,64,128]{2,1,0:T(8,128)(2,1)S(1)}, bf16[16,64,128]{2,1,0:T(8,128)(2,1)S(1)}, u32[]{:S(2)}, u32[]{:S(2)}) collective-permute-start(bf16[16,64,128]{2,1,0:T(8,128)(2,1)S(1)} %get-tuple-element.10), channel_id=1, source_target_pairs={{0,128},{128,0},{1,129},{129,1},{2,130},{130,2},{3,131},{131,3},{4... | collective-permute-start | bytes 786440 | tf_op jit(solution)/shard_map/ppermute | solution.py:341
  122.8 2.9 %copy-start.1 = (bf16[7,16,128,256]{3,2,1,0:T(8,128)(2,1)}, bf16[7,16,128,256]{3,2,1,0:T(8,128)(2,1)S(1)}, u32[]{:S(2)}) copy-start(bf16[7,16,128,256]{3,2,1,0:T(8,128)(2,1)S(1)} %expand.1.dense) | copy-start | bytes 22020100
  125.7 2.2 %copy-start.3 = (bf16[6,16,208,128]{3,2,1,0:T(8,128)(2,1)}, bf16[6,16,208,128]{3,2,1,0:T(8,128)(2,1)S(1)}, u32[]{:S(2)}) copy-start(bf16[6,16,208,128]{3,2,1,0:T(8,128)(2,1)S(1)} %grad_chain.1.grads) | copy-start | bytes 15335428
  128.0 3.1 %copy-start.2 = (bf16[7,16,128,256]{3,2,1,0:T(8,128)(2,1)S(1)}, bf16[7,16,128,256]{3,2,1,0:T(8,128)(2,1)}, u32[]{:S(2)}) copy-start(bf16[7,16,128,256]{3,2,1,0:T(8,128)(2,1)} %copy-done.1) | copy-start | bytes 22020100
  131.0 2.4 %copy-start.4 = (bf16[6,16,208,128]{3,2,1,0:T(8,128)(2,1)S(1)}, bf16[6,16,208,128]{3,2,1,0:T(8,128)(2,1)}, u32[]{:S(2)}) copy-start(bf16[6,16,208,128]{3,2,1,0:T(8,128)(2,1)} %copy-done.3) | copy-start | bytes 15335428
  140.7 4.4 %collective-permute-start.7 = (bf16[4,8,7,16,128]{4,3,2,1,0:T(8,128)(2,1)S(1)}, bf16[4,8,7,16,128]{4,3,2,1,0:T(8,128)(2,1)S(1)}, u32[]{:S(2)}, u32[]{:S(2)}) collective-permute-start(bf16[4,8,7,16,128]{4,3,2,1,0:T(8,128)(2,1)S(1)} %get-tuple-element.12), channel_id=1, source_target_pairs={{0,8},{8,0},{1,9},{9,1},{2,10},{10,2},{3,11},{11,3},{4,12},{12,4},... | collective-permute-start | bytes 2752520 | tf_op jit(solution)/shard_map/ppermute | solution.py:348

commit v4 on v3

--- a/solution.py
+++ b/solution.py
@@ -98,106 +98,114 @@
     for k, part in enumerate(parts):
         out[k] = part[...]
     which = jnp.bitwise_xor(place.y, NY - 1)
-    top[...] = out[which]
+    src, col = iota((ROWS, ROWS), 0), iota((ROWS, ROWS), 1)
+    picks = []
+    for j in range(4):
+        pick = (col // HALF == j) & (src == HALF * (1 - place.x0) + col % HALF)
+        picks.append(pick.astype(F32).astype(BF))
+    for k in range(top.shape[0]):
+        packed = dot(out[which, 4 * k], picks[0])
+        for j in range(1, 4):
+            packed = packed + dot(out[which, 4 * k + j], picks[j])
+        top[k] = packed.astype(BF)
 
 
 def stack(me, parts, after):
+    blocks, rows, wide = parts[0].shape
     return pl.pallas_call(
         stack_kernel,
         in_specs=[SCALARS] + [WHOLE] * NY + [pl.BlockSpec(memory_space=pl.ANY)],
         out_specs=[WHOLE] * 2,
-        out_shape=[jax.ShapeDtypeStruct((NY,) + parts[0].shape, BF), jax.ShapeDtypeStruct(parts[0].shape, BF)],
+        out_shape=[
+            jax.ShapeDtypeStruct((NY, blocks, rows, wide), BF),
+            jax.ShapeDtypeStruct((blocks // 4, rows, wide), BF),
+        ],
         compiler_params=PARAMS,
         name="stack",
     )(me, *parts, after)
 
 
-def expand_kernel(me, near, away, partner_near, partner_away, dense):
+def spreader(level, my_x):
+    width = 2 * ROWS if 2 <= level < TOP else ROWS
+    src, col = iota((ROWS, width), 0), iota((ROWS, width), 1)
+    lane = level % 2 * BLOCK
+
+    def keep(first):
+        row, column = first + iota((BLOCK, width), 0), iota((BLOCK, width), 1)
+        if level == 0:
+            return row // BLOCK == column // BLOCK
+        parts = 2 if level == 1 else 4
+        return (row // HALF) % parts == (column // HALF) % parts
+
+    if level == 0:
+        picks = [src == lane + col % BLOCK]
+    elif level == 1:
+        picks = [src == lane + col // BLOCK * HALF + col % HALF]
+    elif level < TOP:
+        picks = [src == lane + col // ROWS * HALF + col % HALF]
+    else:
+        picks = [src == HALF * my_x + col % HALF] + [src == HALF * j + col % HALF for j in range(4)]
+    return [pick.astype(F32).astype(BF) for pick in picks], keep
+
+
+def expand_kernel(me, near, away, partner_near, partner_away, _, *dense):
     place = Place(me)
-
-    def run(level):
-        width = ROWS if level < 2 else 2 * ROWS
-        src, col = iota((ROWS, width), 0), iota((ROWS, width), 1)
-        lane = level % 2 * BLOCK
-        if level == 0:
-            pick = src == lane + col % BLOCK
-        elif level == 1:
-            pick = src == lane + col // BLOCK * HALF + col % HALF
-        elif level < TOP:
-            pick = src == lane + col // ROWS * HALF + col % HALF
-        else:
-            pick = src == HALF * place.x0 + col % HALF
-        pick = pick.astype(F32).astype(BF)
+    for level in reversed(range(LEVELS)):
+        picks, keep = spreader(level, place.x0)
         which = jnp.bitwise_xor(place.y, level // 2)
         for c, (ref, partner) in enumerate(((near, partner_near), (away, partner_away))):
-            at = pl.multiple_of(jnp.bitwise_xor(place.core, c) * BLOCK, BLOCK)
-            row, col = at + iota((BLOCK, width), 0), iota((BLOCK, width), 1)
-            if level == 0:
-                keep = row // BLOCK == col // BLOCK
-            elif level == 1:
-                keep = (row // HALF) % 2 == (col // HALF) % 2
-            else:
-                keep = row // HALF == (col // HALF) % 4
+            first = jnp.bitwise_xor(place.core, c) * BLOCK
+            at = pl.ds(pl.multiple_of(first, BLOCK), BLOCK)
+            mask = keep(first)
             for block in range(2 * NZ):
+                full = jnp.where(mask, dot(ref[which, block], picks[0]), 0.0).astype(BF)
+                dense[level][block, at, : full.shape[1]] = full
                 if level == TOP:
-                    full = jnp.concatenate([dot(ref[which, block], pick[:, :ROWS]), dot(partner[block], pick[:, ROWS:])], axis=1)
-                else:
-                    full = dot(ref[which, block], pick)
-                dense[0, block, pl.ds(at, BLOCK), :width] = jnp.where(keep, full, 0.0).astype(BF)
-
-    for level in range(LEVELS):
-        pl.when(pl.program_id(0) == level)(functools.partial(run, level))
-
-
-def expand(me, near, away, partner_near, partner_away):
-    shape = (2 * NZ, ROWS, 2 * ROWS)
+                    far = dot(partner[block // 4], picks[1 + block % 4])
+                    dense[level][block, at, ROWS:] = jnp.where(mask, far, 0.0).astype(BF)
+
+
+def expand(me, near, away, partner_near, partner_away, after):
+    narrow, wide = (2 * NZ, ROWS, ROWS), (2 * NZ, ROWS, 2 * ROWS)
     return pl.pallas_call(
         expand_kernel,
-        grid=(LEVELS,),
-        in_specs=[SCALARS] + [WHOLE] * 4,
-        out_specs=pl.BlockSpec((1,) + shape, lambda s: (s, 0, 0, 0)),
-        out_shape=jax.ShapeDtypeStruct((LEVELS,) + shape, BF),
+        in_specs=[SCALARS] + [WHOLE] * 4 + [pl.BlockSpec(memory_space=pl.ANY)],
+        out_specs=[WHOLE] * LEVELS,
+        out_shape=[jax.ShapeDtypeStruct(narrow if level < 2 else wide, BF) for level in range(LEVELS)],
         compiler_params=PARAMS,
         name="expand",
-    )(me, near, away, partner_near, partner_away)
-
-
-def grad_kernel(dense, mine, theirs, grads, state):
-    def run(level):
+    )(me, near, away, partner_near, partner_away, after)
+
+
+def grad_kernel(*refs):
+    dense, mine, theirs, grads = refs[:TOP], refs[TOP], refs[TOP + 1], refs[TOP + 2 :]
+    for level in range(TOP, 0, -1):
+        mix, above, out_ref = dense[level - 1], grads[level] if level < TOP else None, grads[level - 1]
         for unit in units(level):
             for lo, hi in unit:
                 if level == TOP:
                     both = jnp.concatenate([mine[lo], theirs[lo]], axis=1)
-                    full = jnp.concatenate([dense[0, lo, :, :ROWS], dense[0, lo, :, ROWS:]], axis=0)
+                    full = jnp.concatenate([mix[lo, :, :ROWS], mix[lo, :, ROWS:]], axis=0)
                 elif level == 1:
-                    both, full = state[lo], dense[0, lo, :, :ROWS]
+                    both, full = above[lo], mix[lo]
                 else:
-                    both = jnp.concatenate([state[lo], state[hi]], axis=1)
-                    full = jnp.concatenate([dense[0, lo], dense[0, hi]], axis=0)
+                    both = jnp.concatenate([above[lo], above[hi]], axis=1)
+                    full = jnp.concatenate([mix[lo], mix[hi]], axis=0)
                 out = dot(both, full).astype(BF)
-                grads[0, lo] = out[:, :ROWS]
-                if level > 1:
-                    state[lo] = out[:, :ROWS]
+                out_ref[lo] = out[:, :ROWS]
                 if hi is not None:
-                    grads[0, hi] = out[:, ROWS:]
-                    state[hi] = out[:, ROWS:]
-
-    for s in range(TOP):
-        pl.when(pl.program_id(0) == s)(functools.partial(run, TOP - s))
+                    out_ref[hi] = out[:, ROWS:]
 
 
 def grad_chain(dense, mine, theirs):
-    blocks, wide, rows = mine.shape
     return pl.pallas_call(
         grad_kernel,
-        grid=(TOP,),
-        in_specs=[pl.BlockSpec((1, blocks, rows, 2 * rows), lambda s: (TOP - s, 0, 0, 0)), WHOLE, WHOLE],
-        out_specs=pl.BlockSpec((1, blocks, wide, rows), lambda s: (TOP - 1 - s, 0, 0, 0)),
-        out_shape=jax.ShapeDtypeStruct((TOP, blocks, wide, rows), BF),
-        scratch_shapes=[pltpu.VMEM((blocks, wide, rows), BF)],
+        in_specs=[WHOLE] * (TOP + 2),
+        out_specs=[WHOLE] * TOP,
+        out_shape=[jax.ShapeDtypeStruct(mine.shape, BF)] * TOP,
         compiler_params=PARAMS,
         name="grad_chain",
-    )(dense, mine, theirs)
+    )(*dense, mine, theirs)
 
 
 def fold(quad):
@@ -208,19 +216,21 @@
     return out
 
 
-def score_kernel(me, base, dense, grads, mine, theirs, own, away, state):
+def score_kernel(me, base, *refs):
+    dense, grads = refs[:TOP], refs[TOP : 2 * TOP]
+    mine, theirs, own, away, *states = refs[2 * TOP :]
     first_core = Place(me).core == 0
 
-    def store(z, parts):
+    def store(level, z, parts):
         zero, one = parts
         mine_, other = jnp.where(first_core, zero, one), jnp.where(first_core, one, zero)
         for y in range(NY):
-            own[y, z, 0] = mine_[y * SLICE : (y + 1) * SLICE].astype(BF)
-            away[y, z, 0] = other[y * SLICE : (y + 1) * SLICE].astype(BF)
-
-    def run(level):
-        if level == 0:
-            eye = (iota((ROWS, ROWS), 0) == iota((ROWS, ROWS), 1)).astype(F32).astype(BF)
+            own[y, z, level] = mine_[y * SLICE : (y + 1) * SLICE].astype(BF)
+            away[y, z, level] = other[y * SLICE : (y + 1) * SLICE].astype(BF)
+
+    eye = (iota((ROWS, ROWS), 0) == iota((ROWS, ROWS), 1)).astype(F32).astype(BF)
+    for level in range(LEVELS):
+        state, after = states[level % 2], states[1 - level % 2]
         for unit in units(level):
             parts = {}
             for lo, hi in unit:
@@ -233,9 +243,15 @@
                 if level == TOP:
                     g = jnp.concatenate([mine[lo], theirs[lo]], axis=1)
                 elif hi is None:
-                    g = grads[0, lo]
+                    g = grads[level][lo]
                 else:
-                    g = jnp.concatenate([grads[0, lo], grads[0, hi]], axis=1)
+                    g = jnp.concatenate([grads[level][lo], grads[level][hi]], axis=1)
+                if level < 2:
+                    after[lo] = dot(dense[level][lo], x).astype(BF)
+                elif level < TOP:
+                    full = jnp.concatenate([dense[level][lo], dense[level][hi]], axis=0)
+                    out = dot(full, x).astype(BF)
+                    after[lo], after[hi] = out[:ROWS], out[ROWS:]
                 quad = dot(x, g)
                 if level == 0:
                     parts[lo] = jnp.where(iota((BLOCK, ROWS), 1) < BLOCK, quad[:BLOCK], quad[BLOCK:])
@@ -248,40 +264,22 @@
                 else:
                     for b, at in ((lo, slice(0, ROWS)), (hi, slice(ROWS, 2 * ROWS))):
                         parts[b] = jnp.concatenate([fold(quad[:ROWS, at]), fold(quad[ROWS:, at])], axis=0)
-                if level < 2:
-                    state[lo] = dot(dense[0, lo, :, :ROWS], x).astype(BF)
-                elif level < TOP:
-                    full = jnp.concatenate([dense[0, lo], dense[0, hi]], axis=0)
-                    out = dot(full, x).astype(BF)
-                    state[lo], state[hi] = out[:ROWS], out[ROWS:]
             for z in sorted({b // 2 for b in parts}):
-                store(z, (parts[2 * z], parts[2 * z + 1]))
-
-    for level in range(LEVELS):
-        pl.when(pl.program_id(0) == level)(functools.partial(run, level))
+                store(level, z, (parts[2 * z], parts[2 * z + 1]))
 
 
 def scores(me, base, dense, grads, mine, theirs):
     blocks, wide, rows = base.shape
     shape = (NY, NZ, LEVELS, SLICE, rows)
-    out_spec = pl.BlockSpec((NY, NZ, 1, SLICE, rows), lambda s: (0, 0, s, 0, 0))
     return pl.pallas_call(
         score_kernel,
-        grid=(LEVELS,),
-        in_specs=[
-            SCALARS,
-            WHOLE,
-            pl.BlockSpec((1, blocks, rows, 2 * rows), lambda s: (jnp.minimum(s, TOP - 1), 0, 0, 0)),
-            pl.BlockSpec((1, blocks, wide, rows), lambda s: (jnp.minimum(s, TOP - 1), 0, 0, 0)),
-            WHOLE,
-            WHOLE,
-        ],
-        out_specs=[out_spec, out_spec],
+        in_specs=[SCALARS] + [WHOLE] * (2 * TOP + 3),
+        out_specs=[WHOLE] * 2,
         out_shape=[jax.ShapeDtypeStruct(shape, BF)] * 2,
-        scratch_shapes=[pltpu.VMEM((blocks, rows, wide), BF)],
+        scratch_shapes=[pltpu.VMEM((blocks, rows, wide), BF)] * 2,
         compiler_params=PARAMS,
         name="scores",
-    )(me, base, dense, grads, mine, theirs)
+    )(me, base, *dense, *grads, mine, theirs)
 
 
 def call(kernel, shape, *args):
@@ -340,9 +338,9 @@
     away = lax.ppermute(near, "core", flips(2))
     partner_near = lax.ppermute(top, "x0", flips(2))
     partner_away = lax.ppermute(top, ("x0", "core"), flips(4, 3))
-    dense = expand(me, near, away, partner_near, partner_away)
-    grads = grad_chain(dense, mine, theirs)
-    own, away = scores(me, base, dense, grads, mine, theirs)
+    dense = expand(me, near, away, partner_near, partner_away, base)
+    grads = grad_chain(dense[1:], mine, theirs)
+    own, away = scores(me, base, dense[:TOP], grads, mine, theirs)
 
     part = (LEVELS, SLICE, rows)
     total = call(core_sum, jax.ShapeDtypeStruct(own.shape, BF), me, own, lax.ppermute(away, "core", flips(2)))

time: 209 us -> 195 us (0.933)
  local copies, waits for them, and re-layouts: 15.2 us -> 4.5 us
  waiting for transfers between devices: 67 us -> 60.9 us
  blocking collectives: 59.5 us -> 62.1 us
    unnamed x18 -> x10, local copies, waits for them, and re-layouts: 12.8 us -> 2.12 us
    ppermute x1, waiting for transfers between devices: 6.25 us -> 0.01 us  [per_device(): partner_near = lax.ppermute(top, 'x0', flips(2))]
    all_to_all x1, waiting for transfers between devices: 0.01 us -> 4.19 us  [per_device(): base = lax.all_to_all(base, ('z', 'core'), 0, 0)]
    ppermute x1, waiting for transfers between devices: 3.73 us -> 0.01 us  [per_device(): partner_away = lax.ppermute(top, ('x0', 'core'), flips(4, 3))]
  transfers between devices with their start and end apart: 10 -> 10, of which waited for: 6 -> 5; matrix products, arithmetic and copies ran while one was open for 1% -> 1% of each run, Pallas kernels for 3% -> 1%
where the time goes in v4:
time: 195 us; the launch traced here: 191 us
  blocking collectives  62.1 us (32%)
  waiting for transfers between devices  60.9 us (31%)
  starting transfers between devices  48.1 us (25%)
  Pallas kernels  15.4 us (8%)
  local copies, waits for them, and re-layouts  4.5 us (2%)
    all_to_all x1, waiting for transfers between devices, per_device(): lax.all_to_all(pack(me, upstream, factors.transpose(0, 2, 1)), ('z', 'cor...  44.8 us
    all_to_all x1, blocking collectives, per_device(): total = lax.all_to_all(total.reshape((2 * NZ,) + part), ('zh', 'z'), 0, 0)  35.5 us
    all_to_all x1, blocking collectives, per_device(): total = lax.all_to_all(total, 'y', 0, 0)  16.6 us
    all_to_all x1, starting transfers between devices, per_device(): lax.all_to_all(pack(me, upstream, factors.transpose(0, 2, 1)), ('z', 'cor...  12.8 us
    all_to_all x1, starting transfers between devices, per_device(): base = lax.all_to_all(base, ('z', 'core'), 0, 0)  11.6 us
    all_to_all x1, blocking collectives, per_device(): total = lax.all_to_all(total, ('x0', 'y'), 0, 0)  9.94 us
    ppermute x3, starting transfers between devices, per_device(): lax.ppermute(mixing, 'y', flips(NY, k))  9.82 us
    ppermute x3, waiting for transfers between devices, per_device(): lax.ppermute(mixing, 'y', flips(NY, k))  9.78 us
  transfers between devices with their start and end apart: 10, of which 5 were waited for; matrix products, arithmetic and copies ran while one was open for 1% of the time, Pallas kernels for 1%

profile of v4, /device:TPU:24, one launch (start us, length us, event | category | flops | bytes accessed | tf_op | source)
XLA Modules:
  0.0 191.3 jit_solution(3892839703397600963)
XLA Ops:
  0.0 1.2 copy-done.1
  1.2 0.9 copy-done.2
  2.1 1.3 pack.1
  3.4 12.8 %all-to-all-start.1 = ((bf16[16,272,128]{2,1,0:T(8,128)(2,1)}), bf16[16,272,128]{2,1,0:T(8,128)(2,1)S(1)}, u32[]{:S(2)}, u32[]{:S(2)}) async-start(bf16[16,272,128]{2,1,0:T(8,128)(2,1)} %pack.1), calls=%async_computation.1 | async-start | bytes 2228224 | tf_op jit(solution)/shard_map/all_to_all | solution.py:329
  16.2 0.1 broadcast_bitcast_fusion
  16.3 0.1 fusion
  16.4 1.3 copy.5
  17.7 44.8 %all-to-all-done.1 = bf16[16,272,128]{2,1,0:T(8,128)(2,1)S(1)} async-done(((bf16[16,272,128]{2,1,0:T(8,128)(2,1)}), bf16[16,272,128]{2,1,0:T(8,128)(2,1)S(1)}, u32[]{:S(2)}, u32[]{:S(2)}) %all-to-all-start.1) | async-done | bytes 1114144 | tf_op jit(solution)/shard_map/all_to_all | solution.py:329
  62.5 11.6 %all-to-all-start = ((bf16[16,208,128]{2,1,0:T(8,128)(2,1)}), bf16[16,208,128]{2,1,0:T(8,128)(2,1)S(1)}, u32[]{:S(2)}, u32[]{:S(2)}) async-start(bf16[16,208,128]{2,1,0:T(8,128)(2,1)} %bitcast.4), calls=%async_computation | async-start | bytes 1703936 | tf_op jit(solution)/shard_map/all_to_all | solution.py:333
  74.3 3.4 %collective-permute-start.3 = (bf16[16,208,128]{2,1,0:T(8,128)(2,1)S(1)}, bf16[16,208,128]{2,1,0:T(8,128)(2,1)S(1)}, u32[]{:S(2)}, u32[]{:S(2)}) collective-permute-start(bf16[16,208,128]{2,1,0:T(8,128)(2,1)S(1)} %slice.9.refs_6_.refs_12_), channel_id=1, source_target_pairs={{0,128},{128,0},{1,129},{129,1},{2,130},{130,2},{3,131},{131,3},{4... | collective-permute-start | bytes 2555912 | tf_op jit(solution)/shard_map/ppermute | solution.py:334
  77.7 1.0 slice.8.refs_0_
  78.6 2.1 %collective-permute-start.2 = (bf16[16,64,128]{2,1,0:T(8,128)(2,1)S(1)}, bf16[16,64,128]{2,1,0:T(8,128)(2,1)S(1)}, u32[]{:S(2)}, u32[]{:S(2)}) collective-permute-start(bf16[16,64,128]{2,1,0:T(8,128)(2,1)S(1)} %slice.8.refs_0_), channel_id=1, source_target_pairs={{0,3},{1,2},{2,1},{3,0},{4,7},{5,6},{6,5},{7,4},{8,11},{9,10},{10,... | collective-permute-start | bytes 786440 | tf_op jit(solution)/shard_map/ppermute | solution.py:336
  80.8 4.5 %collective-permute-start.1 = (bf16[16,64,128]{2,1,0:T(8,128)(2,1)S(1)}, bf16[16,64,128]{2,1,0:T(8,128)(2,1)S(1)}, u32[]{:S(2)}, u32[]{:S(2)}) collective-permute-start(bf16[16,64,128]{2,1,0:T(8,128)(2,1)S(1)} %slice.8.refs_0_), channel_id=1, source_target_pairs={{0,2},{1,3},{2,0},{3,1},{4,6},{5,7},{6,4},{7,5},{8,10},{9,11},{10,... | collective-permute-start | bytes 786440 | tf_op jit(solution)/shard_map/ppermute | solution.py:336
  85.3 3.2 %collective-permute-start = (bf16[16,64,128]{2,1,0:T(8,128)(2,1)S(1)}, bf16[16,64,128]{2,1,0:T(8,128)(2,1)S(1)}, u32[]{:S(2)}, u32[]{:S(2)}) collective-permute-start(bf16[16,64,128]{2,1,0:T(8,128)(2,1)S(1)} %slice.8.refs_0_), channel_id=1, source_target_pairs={{0,1},{1,0},{2,3},{3,2},{4,5},{5,4},{6,7},{7,6},{8,9},{9,8},{10,11... | collective-permute-start | bytes 786440 | tf_op jit(solution)/shard_map/ppermute | solution.py:336
  88.5 7.2 %collective-permute-done.2.refs_3_ = bf16[16,64,128]{2,1,0:T(8,128)(2,1)S(1)} collective-permute-done((bf16[16,64,128]{2,1,0:T(8,128)(2,1)S(1)}, bf16[16,64,128]{2,1,0:T(8,128)(2,1)S(1)}, u32[]{:S(2)}, u32[]{:S(2)}) %collective-permute-start.2) | collective-permute-done | bytes 262176 | tf_op jit(solution)/shard_map/ppermute | solution.py:336
  95.7 2.5 %collective-permute-done.refs_1_ = bf16[16,64,128]{2,1,0:T(8,128)(2,1)S(1)} collective-permute-done((bf16[16,64,128]{2,1,0:T(8,128)(2,1)S(1)}, bf16[16,64,128]{2,1,0:T(8,128)(2,1)S(1)}, u32[]{:S(2)}, u32[]{:S(2)}) %collective-permute-start) | collective-permute-done | bytes 262176 | tf_op jit(solution)/shard_map/ppermute | solution.py:336
  98.3 1.1 stack.1
  99.3 1.9 collective-permute-start.4
  101.2 2.7 %collective-permute-start.6 = (bf16[4,64,128]{2,1,0:T(8,128)(2,1)S(1)}, bf16[4,64,128]{2,1,0:T(8,128)(2,1)S(1)}, u32[]{:S(2)}, u32[]{:S(2)}) collective-permute-start(bf16[4,64,128]{2,1,0:T(8,128)(2,1)S(1)} %get-tuple-element.23), channel_id=1, source_target_pairs={{0,136},{8,128},{128,8},{136,0},{1,137},{9,129},{129,9},{137,1},{2... | collective-permute-start | bytes 196616 | tf_op jit(solution)/shard_map/ppermute | solution.py:340
  103.9 3.3 %collective-permute-start.5 = (bf16[4,64,128]{2,1,0:T(8,128)(2,1)S(1)}, bf16[4,64,128]{2,1,0:T(8,128)(2,1)S(1)}, u32[]{:S(2)}, u32[]{:S(2)}) collective-permute-start(bf16[4,64,128]{2,1,0:T(8,128)(2,1)S(1)} %get-tuple-element.23), channel_id=1, source_target_pairs={{0,128},{128,0},{1,129},{129,1},{2,130},{130,2},{3,131},{131,3},{4... | collective-permute-start | bytes 196616 | tf_op jit(solution)/shard_map/ppermute | solution.py:339
  107.2 4.2 %all-to-all-done._.base = bf16[16,208,128]{2,1,0:T(8,128)(2,1)S(1)} async-done(((bf16[16,208,128]{2,1,0:T(8,128)(2,1)}), bf16[16,208,128]{2,1,0:T(8,128)(2,1)S(1)}, u32[]{:S(2)}, u32[]{:S(2)}) %all-to-all-start) | async-done | bytes 852000 | tf_op jit(solution)/shard_map/all_to_all | solution.py:333
  111.4 3.7 %expand.1 = (bf16[16,128,128]{2,1,0:T(8,128)(2,1)S(1)}, bf16[16,128,128]{2,1,0:T(8,128)(2,1)S(1)}, bf16[16,128,256]{2,1,0:T(8,128)(2,1)S(1)}, bf16[16,128,256]{2...) custom-call(s32[1]{0:T(128)} %bitcast.me, ...), custom_call_target="tpu_custom_call" | custom-call | tf_op jit(solution)/shard_map/expand/pallas_call | solution.py:170
  115.1 2.0 %grad_chain.1 = (bf16[16,208,128]{2,1,0:T(8,128)(2,1)S(1)}, bf16[16,208,128]{2,1,0:T(8,128)(2,1)S(1)}, bf16[16,208,128]{2,1,0:T(8,128)(2,1)S(1)}, bf16[16,208,12...) custom-call(bf16[16,128,128]{2,1,0:T(8,128)(2,1)S(1)} %get-tuple-element.25.refs_0_.refs_1_, ...), custom_call_target="tpu_custom_call" | custom-call | tf_op jit(solution)/shard_map/grad_chain/pallas_call | solution.py:201
  117.1 6.3 %scores.1 = (bf16[4,8,7,16,128]{4,3,2,1,0:T(8,128)(2,1)S(1)}, bf16[4,8,7,16,128]{4,3,2,1,0:T(8,128)(2,1)S(1)}) custom-call(s32[1]{0:T(128)} %bitcast.me, bf16[16,208,128]{2,1,0:T(8,128)(2,1)S(1)} %all-to-all-done._.base, bf16[16,128,128]{2,1,0:T(8,128)(2,1)S(1)} %get-tuple-element.24.refs_0_, bf16[16,128,128]{2,1,0:T(8,128)(2,1)S(1)} %get-tuple-element.25.refs_0_.refs_1_, ...), custom_call_target="tpu_custom_call" | custom-call | tf_op jit(solution)/shard_map/scores/pallas_call | solution.py:274
  123.4 2.7 %collective-permute-start.7 = (bf16[4,8,7,16,128]{4,3,2,1,0:T(8,128)(2,1)S(1)}, bf16[4,8,7,16,128]{4,3,2,1,0:T(8,128)(2,1)S(1)}, u32[]{:S(2)}, u32[]{:S(2)}) collective-permute-start(bf16[4,8,7,16,128]{4,3,2,1,0:T(8,128)(2,1)S(1)} %get-tuple-element.38), channel_id=1, source_target_pairs={{0,8},{8,0},{1,9},{9,1},{2,10},{10,2},{3,11},{11,3},{4,12},{12,4},... | collective-permute-start | bytes 2752520 | tf_op jit(solution)/shard_map/ppermute | solution.py:346
  126.1 2.1 %collective-permute-done.7.got = bf16[4,8,7,16,128]{4,3,2,1,0:T(8,128)(2,1)S(1)} collective-permute-done((bf16[4,8,7,16,128]{4,3,2,1,0:T(8,128)(2,1)S(1)}, bf16[4,8,7,16,128]{4,3,2,1,0:T(8,128)(2,1)S(1)}, u32[]{:S(2)}, u32[]{:S(2)}) %collective-permute-start.7) | collective-permute-done | bytes 917536 | tf_op jit(solution)/shard_map/ppermute | solution.py:346
  128.1 0.2 core_sum.1
  128.4 16.6 %all_to_all.25.parts = bf16[4,8,7,16,128]{4,3,2,1,0:T(8,128)(2,1)S(1)} all-to-all(bf16[4,8,7,16,128]{4,3,2,1,0:T(8,128)(2,1)S(1)} %core_sum.1), channel_id=1, replica_groups=mesh['x1'=2,'x0'=2,'z'=8,'core'=2,'zh'=2,'y'=4] {'y'}, dimensions={0} | all-to-all | bytes 1835008 | tf_op jit(solution)/shard_map/all_to_all | solution.py:347
  145.0 0.1 copies_of_sum.2
  145.1 35.5 %all_to_all.26.parts = bf16[16,7,16,128]{3,2,1,0:T(8,128)(2,1)S(1)} all-to-all(bf16[16,7,16,128]{3,2,1,0:T(8,128)(2,1)S(1)} %bitcast.11), channel_id=1, replica_groups=mesh['x1'=2,'x0'=2,'z'=8,'core'=2,'zh'=2,'y'=4] {'zh','z'}, dimensions={0} | all-to-all | bytes 917504 | tf_op jit(solution)/shard_map/all_to_all | solution.py:349
  180.7 9.9 %all_to_all.27.slices = bf16[8,7,16,128]{3,2,1,0:T(8,128)(2,1)S(1)} all-to-all(bf16[8,7,16,128]{3,2,1,0:T(8,128)(2,1)S(1)} %copies_of_sum.3), channel_id=1, replica_groups=mesh['x1'=2,'x0'=2,'z'=8,'core'=2,'zh'=2,'y'=4] {'x0','y'}, dimensions={0} | all-to-all | bytes 458752 | tf_op jit(solution)/shard_map/all_to_all | solution.py:351
  190.6 0.7 finish.1
  (15 shorter events, 0.2 us)
Async XLA Ops:
  0.0 16.2 %copy-start = (f32[1,26]{1,0:T(1,128)S(1)}, f32[1,26]{1,0:T(1,128)}, u32[]{:S(2)}) copy-start(f32[1,26]{1,0:T(1,128)} %param.5) | copy-start | bytes 316
  0.0 1.2 copy-start.1
  1.2 0.9 copy-start.2
  3.4 12.9 %copy-start.4 = (bf16[128,3328]{1,0:T(8,128)(2,1)S(1)}, bf16[128,3328]{1,0:T(8,128)(2,1)}, u32[]{:S(2)}) copy-start(bf16[128,3328]{1,0:T(8,128)(2,1)} %param.4) | copy-start | bytes 2555908
  3.4 59.1 %all-to-all-start.1 = ((bf16[16,272,128]{2,1,0:T(8,128)(2,1)}), bf16[16,272,128]{2,1,0:T(8,128)(2,1)S(1)}, u32[]{:S(2)}, u32[]{:S(2)}) async-start(bf16[16,272,128]{2,1,0:T(8,128)(2,1)} %pack.1), calls=%async_computation.1 | async-start | bytes 2228224 | tf_op jit(solution)/shard_map/all_to_all | solution.py:329
  62.5 11.6 %copy-start.3 = (bf16[16,272,128]{2,1,0:T(8,128)(2,1)}, bf16[16,272,128]{2,1,0:T(8,128)(2,1)S(1)}, u32[]{:S(2)}) copy-start(bf16[16,272,128]{2,1,0:T(8,128)(2,1)S(1)} %all-to-all-done.1) | copy-start | bytes 3342340
  62.5 48.9 %all-to-all-start = ((bf16[16,208,128]{2,1,0:T(8,128)(2,1)}), bf16[16,208,128]{2,1,0:T(8,128)(2,1)S(1)}, u32[]{:S(2)}, u32[]{:S(2)}) async-start(bf16[16,208,128]{2,1,0:T(8,128)(2,1)} %bitcast.4), calls=%async_computation | async-start | bytes 1703936 | tf_op jit(solution)/shard_map/all_to_all | solution.py:333
  74.3 24.0 %collective-permute-start.3 = (bf16[16,208,128]{2,1,0:T(8,128)(2,1)S(1)}, bf16[16,208,128]{2,1,0:T(8,128)(2,1)S(1)}, u32[]{:S(2)}, u32[]{:S(2)}) collective-permute-start(bf16[16,208,128]{2,1,0:T(8,128)(2,1)S(1)} %slice.9.refs_6_.refs_12_), channel_id=1, source_target_pairs={{0,128},{128,0},{1,129},{129,1},{2,130},{130,2},{3,131},{131,3},{4... | collective-permute-start | bytes 2555912 | tf_op jit(solution)/shard_map/ppermute | solution.py:334
  78.6 17.1 %collective-permute-start.2 = (bf16[16,64,128]{2,1,0:T(8,128)(2,1)S(1)}, bf16[16,64,128]{2,1,0:T(8,128)(2,1)S(1)}, u32[]{:S(2)}, u32[]{:S(2)}) collective-permute-start(bf16[16,64,128]{2,1,0:T(8,128)(2,1)S(1)} %slice.8.refs_0_), channel_id=1, source_target_pairs={{0,3},{1,2},{2,1},{3,0},{4,7},{5,6},{6,5},{7,4},{8,11},{9,10},{10,... | collective-permute-start | bytes 786440 | tf_op jit(solution)/shard_map/ppermute | solution.py:336
  80.8 14.9 %collective-permute-start.1 = (bf16[16,64,128]{2,1,0:T(8,128)(2,1)S(1)}, bf16[16,64,128]{2,1,0:T(8,128)(2,1)S(1)}, u32[]{:S(2)}, u32[]{:S(2)}) collective-permute-start(bf16[16,64,128]{2,1,0:T(8,128)(2,1)S(1)} %slice.8.refs_0_), channel_id=1, source_target_pairs={{0,2},{1,3},{2,0},{3,1},{4,6},{5,7},{6,4},{7,5},{8,10},{9,11},{10,... | collective-permute-start | bytes 786440 | tf_op jit(solution)/shard_map/ppermute | solution.py:336
  85.3 13.0 %collective-permute-start = (bf16[16,64,128]{2,1,0:T(8,128)(2,1)S(1)}, bf16[16,64,128]{2,1,0:T(8,128)(2,1)S(1)}, u32[]{:S(2)}, u32[]{:S(2)}) collective-permute-start(bf16[16,64,128]{2,1,0:T(8,128)(2,1)S(1)} %slice.8.refs_0_), channel_id=1, source_target_pairs={{0,1},{1,0},{2,3},{3,2},{4,5},{5,4},{6,7},{7,6},{8,9},{9,8},{10,11... | collective-permute-start | bytes 786440 | tf_op jit(solution)/shard_map/ppermute | solution.py:336
  99.3 12.1 %collective-permute-start.4 = (bf16[4,16,64,128]{3,2,1,0:T(8,128)(2,1)}, bf16[4,16,64,128]{3,2,1,0:T(8,128)(2,1)}, u32[]{:S(2)}, u32[]{:S(2)}) collective-permute-start(bf16[4,16,64,128]{3,2,1,0:T(8,128)(2,1)} %get-tuple-element.22.near), channel_id=1, source_target_pairs={{0,8},{8,0},{1,9},{9,1},{2,10},{10,2},{3,11},{11,3},{4,12},{12,4},... | collective-permute-start | bytes 3145736 | tf_op jit(solution)/shard_map/ppermute | solution.py:338
  101.2 10.2 %collective-permute-start.6 = (bf16[4,64,128]{2,1,0:T(8,128)(2,1)S(1)}, bf16[4,64,128]{2,1,0:T(8,128)(2,1)S(1)}, u32[]{:S(2)}, u32[]{:S(2)}) collective-permute-start(bf16[4,64,128]{2,1,0:T(8,128)(2,1)S(1)} %get-tuple-element.23), channel_id=1, source_target_pairs={{0,136},{8,128},{128,8},{136,0},{1,137},{9,129},{129,9},{137,1},{2... | collective-permute-start | bytes 196616 | tf_op jit(solution)/shard_map/ppermute | solution.py:340
  103.9 7.5 %collective-permute-start.5 = (bf16[4,64,128]{2,1,0:T(8,128)(2,1)S(1)}, bf16[4,64,128]{2,1,0:T(8,128)(2,1)S(1)}, u32[]{:S(2)}, u32[]{:S(2)}) collective-permute-start(bf16[4,64,128]{2,1,0:T(8,128)(2,1)S(1)} %get-tuple-element.23), channel_id=1, source_target_pairs={{0,128},{128,0},{1,129},{129,1},{2,130},{130,2},{3,131},{131,3},{4... | collective-permute-start | bytes 196616 | tf_op jit(solution)/shard_map/ppermute | solution.py:339
  123.4 4.8 %collective-permute-start.7 = (bf16[4,8,7,16,128]{4,3,2,1,0:T(8,128)(2,1)S(1)}, bf16[4,8,7,16,128]{4,3,2,1,0:T(8,128)(2,1)S(1)}, u32[]{:S(2)}, u32[]{:S(2)}) collective-permute-start(bf16[4,8,7,16,128]{4,3,2,1,0:T(8,128)(2,1)S(1)} %get-tuple-element.38), channel_id=1, source_target_pairs={{0,8},{8,0},{1,9},{9,1},{2,10},{10,2},{3,11},{11,3},{4,12},{12,4},... | collective-permute-start | bytes 2752520 | tf_op jit(solution)/shard_map/ppermute | solution.py:346

commit v5 on v4

--- a/solution.py
+++ b/solution.py
@@ -57,37 +57,70 @@
     return [[(2 * z + c, 2 * (z | 1 << bit) + c) for c in range(2)] for z in lows]
 
 
-def pack_kernel(me, upstream, factors, out):
-    chunk = out.shape[1] - BLOCK
-    for t in range(upstream.shape[1] // ROWS):
-        turned = upstream[:, t * ROWS : (t + 1) * ROWS].T
-        start, end = t * ROWS, (t + 1) * ROWS
-        while start < end:
-            block, at = start // chunk, start % chunk
-            size = min(end - start, chunk - at)
-            out[block, at : at + size] = turned[start - t * ROWS : start - t * ROWS + size]
-            start += size
+def pack_kernel(me, upstream, factors, out, wide, mix, turned, in_sems, mix_sem, out_sems):
     place = Place(me)
+    blocks = turned.shape[0]
+    chunk = turned.shape[1] - BLOCK
+    tiles = wide.shape[1] // ROWS
+    count = in_sems.shape[0]
+    edges = [ROWS * (tiles * i // count) for i in range(count + 1)]
+    loads = [
+        pltpu.make_async_copy(upstream.at[:, lo:hi], wide.at[:, lo:hi], in_sems.at[i])
+        for i, (lo, hi) in enumerate(zip(edges, edges[1:]))
+    ]
+    load_mix = pltpu.make_async_copy(factors, mix, mix_sem)
+    load_mix.start()
+    for load in loads:
+        load.start()
+    load_mix.wait()
     row = place.first_row + iota((BLOCK, ROWS), 1)
     sides = []
     for side in range(2):
         level = jnp.minimum(2 * place.y + side, TOP)
         pick = lax.shift_right_logical(row, level + 5) % 2 * HALF + row % HALF
-        sides.append((iota((BLOCK, ROWS), 0) == pick).astype(F32) + factors[level])
+        sides.append((iota((BLOCK, ROWS), 0) == pick).astype(F32) + mix[level])
     tile = jnp.concatenate(sides, axis=0).T.astype(BF)
-    for block in range(out.shape[0]):
+    for block in range(blocks):
         half = block % 2 * BLOCK
-        out[block, chunk:] = tile[half : half + BLOCK]
+        turned[block, chunk:] = tile[half : half + BLOCK]
+    stores = []
+    group = blocks // out_sems.shape[0]
+    for t in range(tiles):
+        if t * ROWS in edges:
+            loads[edges.index(t * ROWS)].wait()
+        columns = wide[:, t * ROWS : (t + 1) * ROWS].T
+        start, end = t * ROWS, (t + 1) * ROWS
+        while start < end:
+            block, at = start // chunk, start % chunk
+            size = min(end - start, chunk - at)
+            turned[block, at : at + size] = columns[start - t * ROWS : start - t * ROWS + size]
+            start += size
+        while len(stores) < out_sems.shape[0] and end >= (len(stores) + 1) * group * chunk:
+            at = slice(len(stores) * group, (len(stores) + 1) * group)
+            stores.append(pltpu.make_async_copy(turned.at[at], out.at[at], out_sems.at[len(stores)]))
+            stores[-1].start()
+    for store in stores:
+        store.wait()
 
 
 def pack(me, upstream, factors):
     rows, wide = upstream.shape
+    shape = (2 * NZ, wide // (2 * NZ) + BLOCK, rows)
+    hbm = pl.BlockSpec(memory_space=pltpu.HBM)
     return pl.pallas_call(
         pack_kernel,
-        in_specs=[SCALARS, WHOLE, WHOLE],
-        out_specs=WHOLE,
-        out_shape=jax.ShapeDtypeStruct((2 * NZ, wide // (2 * NZ) + BLOCK, rows), BF),
-        compiler_params=PARAMS,
+        in_specs=[SCALARS, hbm, hbm],
+        out_specs=hbm,
+        out_shape=jax.ShapeDtypeStruct(shape, BF),
+        scratch_shapes=[
+            pltpu.VMEM((rows, wide), BF),
+            pltpu.VMEM(factors.shape, F32),
+            pltpu.VMEM(shape, BF),
+            pltpu.SemaphoreType.DMA((4,)),
+            pltpu.SemaphoreType.DMA,
+            pltpu.SemaphoreType.DMA((4,)),
+        ],
+        compiler_params=pltpu.CompilerParams(vmem_limit_bytes=58 * 2**20),
         name="pack",
     )(me, upstream, factors)
 
@@ -129,16 +162,10 @@
     width = 2 * ROWS if 2 <= level < TOP else ROWS
     src, col = iota((ROWS, width), 0), iota((ROWS, width), 1)
     lane = level % 2 * BLOCK
-
-    def keep(first):
-        row, column = first + iota((BLOCK, width), 0), iota((BLOCK, width), 1)
-        if level == 0:
-            return row // BLOCK == column // BLOCK
-        parts = 2 if level == 1 else 4
-        return (row // HALF) % parts == (column // HALF) % parts
-
+    parts = 2 if level == 1 else 4
+    keep = (src // HALF) % parts == (col // HALF) % parts
     if level == 0:
-        picks = [src == lane + col % BLOCK]
+        picks, keep = [src == lane + col % BLOCK], src // BLOCK == col // BLOCK
     elif level == 1:
         picks = [src == lane + col // BLOCK * HALF + col % HALF]
     elif level < TOP:
@@ -148,30 +175,46 @@
     return [pick.astype(F32).astype(BF) for pick in picks], keep
 
 
-def expand_kernel(me, near, away, partner_near, partner_away, _, *dense):
+def expand_kernel(me, near, away, partner_near, partner_away, _, *refs):
+    dense, held, sems = refs[:LEVELS], refs[LEVELS:-1], refs[-1]
     place = Place(me)
+    first_core = place.core == 0
+    loads = [[] for _ in range(NY)]
+    for j in reversed(range(NY)):
+        for c, ref in enumerate((near, away)):
+            loads[j].append(pltpu.make_async_copy(ref.at[jnp.bitwise_xor(place.y, j)], held[c].at[j], sems.at[j, c]))
+        if j == NY - 1:
+            for c, ref in enumerate((partner_near, partner_away)):
+                loads[j].append(pltpu.make_async_copy(ref, held[2 + c], sems.at[NY, c]))
+        for load in loads[j]:
+            load.start()
+
+    def rows(one, other):
+        return jnp.concatenate([jnp.where(first_core, one, other), jnp.where(first_core, other, one)], axis=0)
+
     for level in reversed(range(LEVELS)):
+        if level == TOP or level % 2:
+            for load in loads[level // 2]:
+                load.wait()
         picks, keep = spreader(level, place.x0)
-        which = jnp.bitwise_xor(place.y, level // 2)
-        for c, (ref, partner) in enumerate(((near, partner_near), (away, partner_away))):
-            first = jnp.bitwise_xor(place.core, c) * BLOCK
-            at = pl.ds(pl.multiple_of(first, BLOCK), BLOCK)
-            mask = keep(first)
-            for block in range(2 * NZ):
-                full = jnp.where(mask, dot(ref[which, block], picks[0]), 0.0).astype(BF)
-                dense[level][block, at, : full.shape[1]] = full
-                if level == TOP:
-                    far = dot(partner[block // 4], picks[1 + block % 4])
-                    dense[level][block, at, ROWS:] = jnp.where(mask, far, 0.0).astype(BF)
+        for block in range(2 * NZ):
+            full = dot(rows(held[0][level // 2, block], held[1][level // 2, block]), picks[0])
+            dense[level][block, :, : full.shape[1]] = jnp.where(keep, full, 0.0).astype(BF)
+            if level == TOP:
+                far = dot(rows(held[2][block // 4], held[3][block // 4]), picks[1 + block % 4])
+                dense[level][block, :, ROWS:] = jnp.where(keep, far, 0.0).astype(BF)
 
 
 def expand(me, near, away, partner_near, partner_away, after):
     narrow, wide = (2 * NZ, ROWS, ROWS), (2 * NZ, ROWS, 2 * ROWS)
     return pl.pallas_call(
         expand_kernel,
-        in_specs=[SCALARS] + [WHOLE] * 4 + [pl.BlockSpec(memory_space=pl.ANY)],
+        in_specs=[SCALARS] + [pl.BlockSpec(memory_space=pl.ANY)] * 5,
         out_specs=[WHOLE] * LEVELS,
         out_shape=[jax.ShapeDtypeStruct(narrow if level < 2 else wide, BF) for level in range(LEVELS)],
+        scratch_shapes=[pltpu.VMEM(near.shape, BF)] * 2
+        + [pltpu.VMEM(partner_near.shape, BF)] * 2
+        + [pltpu.SemaphoreType.DMA((NY + 1, 2))],
         compiler_params=PARAMS,
         name="expand",
     )(me, near, away, partner_near, partner_away, after)

time: 195 us -> 194 us (level)
  local copies, waits for them, and re-layouts: 4.5 us -> 2.4 us
    unnamed x10 -> x6, local copies, waits for them, and re-layouts: 2.12 us -> 0.01 us
where the time goes in v5:
time: 194 us; the launch traced here: 190 us
  blocking collectives  62.1 us (32%)
  waiting for transfers between devices  60.9 us (31%)
  starting transfers between devices  48.1 us (25%)
  Pallas kernels  16.5 us (9%)
  local copies, waits for them, and re-layouts  2.4 us (1%)
    all_to_all x1, waiting for transfers between devices, per_device(): lax.all_to_all(pack(me, upstream, factors.transpose(0, 2, 1)), ('z', 'cor...  44.8 us
    all_to_all x1, blocking collectives, per_device(): total = lax.all_to_all(total.reshape((2 * NZ,) + part), ('zh', 'z'), 0, 0)  35.5 us
    all_to_all x1, blocking collectives, per_device(): total = lax.all_to_all(total, 'y', 0, 0)  16.6 us
    all_to_all x1, starting transfers between devices, per_device(): lax.all_to_all(pack(me, upstream, factors.transpose(0, 2, 1)), ('z', 'cor...  12.8 us
    all_to_all x1, starting transfers between devices, per_device(): base = lax.all_to_all(base, ('z', 'core'), 0, 0)  11.6 us
    all_to_all x1, blocking collectives, per_device(): total = lax.all_to_all(total, ('x0', 'y'), 0, 0)  9.95 us
    ppermute x3, starting transfers between devices, per_device(): lax.ppermute(mixing, 'y', flips(NY, k))  9.82 us
    ppermute x3, waiting for transfers between devices, per_device(): lax.ppermute(mixing, 'y', flips(NY, k))  9.78 us
  transfers between devices with their start and end apart: 10, of which 5 were waited for; matrix products, arithmetic and copies ran while one was open for 1% of the time, Pallas kernels for 1%

profile of v5, /device:TPU:24, one launch (start us, length us, event | category | flops | bytes accessed | tf_op | source)
XLA Modules:
  0.0 190.4 jit_solution(14617561379490392894)
XLA Ops:
  0.0 2.7 %pack.1 = bf16[16,272,128]{2,1,0:T(8,128)(2,1)} custom-call(s32[1]{0:T(128)} %bitcast.me, bf16[128,3328]{1,0:T(8,128)(2,1)} %upstream.1, f32[7,64,128]{2,1,0:T(8,128)} %bitcast.12), custom_call_target="tpu_custom_call" | custom-call | tf_op jit(solution)/shard_map/pack/pallas_call | solution.py:110
  2.7 12.8 %all-to-all-start.1 = ((bf16[16,272,128]{2,1,0:T(8,128)(2,1)}), bf16[16,272,128]{2,1,0:T(8,128)(2,1)S(1)}, u32[]{:S(2)}, u32[]{:S(2)}) async-start(bf16[16,272,128]{2,1,0:T(8,128)(2,1)} %pack.1), calls=%async_computation.1 | async-start | bytes 2228224 | tf_op jit(solution)/shard_map/all_to_all | solution.py:372
  15.5 0.1 broadcast_bitcast_fusion
  15.6 0.1 fusion
  15.7 1.3 copy.5
  17.0 44.8 %all-to-all-done.1 = bf16[16,272,128]{2,1,0:T(8,128)(2,1)S(1)} async-done(((bf16[16,272,128]{2,1,0:T(8,128)(2,1)}), bf16[16,272,128]{2,1,0:T(8,128)(2,1)S(1)}, u32[]{:S(2)}, u32[]{:S(2)}) %all-to-all-start.1) | async-done | bytes 1114144 | tf_op jit(solution)/shard_map/all_to_all | solution.py:372
  61.8 11.6 %all-to-all-start = ((bf16[16,208,128]{2,1,0:T(8,128)(2,1)}), bf16[16,208,128]{2,1,0:T(8,128)(2,1)S(1)}, u32[]{:S(2)}, u32[]{:S(2)}) async-start(bf16[16,208,128]{2,1,0:T(8,128)(2,1)} %bitcast.4), calls=%async_computation | async-start | bytes 1703936 | tf_op jit(solution)/shard_map/all_to_all | solution.py:376
  73.5 0.1 slice.9.refs_6_.refs_12_
  73.5 3.4 %collective-permute-start.3 = (bf16[16,208,128]{2,1,0:T(8,128)(2,1)S(1)}, bf16[16,208,128]{2,1,0:T(8,128)(2,1)S(1)}, u32[]{:S(2)}, u32[]{:S(2)}) collective-permute-start(bf16[16,208,128]{2,1,0:T(8,128)(2,1)S(1)} %slice.9.refs_6_.refs_12_), channel_id=1, source_target_pairs={{0,128},{128,0},{1,129},{129,1},{2,130},{130,2},{3,131},{131,3},{4... | collective-permute-start | bytes 2555912 | tf_op jit(solution)/shard_map/ppermute | solution.py:377
  76.9 1.0 slice.8.refs_0_
  77.9 2.1 %collective-permute-start.2 = (bf16[16,64,128]{2,1,0:T(8,128)(2,1)S(1)}, bf16[16,64,128]{2,1,0:T(8,128)(2,1)S(1)}, u32[]{:S(2)}, u32[]{:S(2)}) collective-permute-start(bf16[16,64,128]{2,1,0:T(8,128)(2,1)S(1)} %slice.8.refs_0_), channel_id=1, source_target_pairs={{0,3},{1,2},{2,1},{3,0},{4,7},{5,6},{6,5},{7,4},{8,11},{9,10},{10,... | collective-permute-start | bytes 786440 | tf_op jit(solution)/shard_map/ppermute | solution.py:379
  80.1 4.5 %collective-permute-start.1 = (bf16[16,64,128]{2,1,0:T(8,128)(2,1)S(1)}, bf16[16,64,128]{2,1,0:T(8,128)(2,1)S(1)}, u32[]{:S(2)}, u32[]{:S(2)}) collective-permute-start(bf16[16,64,128]{2,1,0:T(8,128)(2,1)S(1)} %slice.8.refs_0_), channel_id=1, source_target_pairs={{0,2},{1,3},{2,0},{3,1},{4,6},{5,7},{6,4},{7,5},{8,10},{9,11},{10,... | collective-permute-start | bytes 786440 | tf_op jit(solution)/shard_map/ppermute | solution.py:379
  84.6 3.2 %collective-permute-start = (bf16[16,64,128]{2,1,0:T(8,128)(2,1)S(1)}, bf16[16,64,128]{2,1,0:T(8,128)(2,1)S(1)}, u32[]{:S(2)}, u32[]{:S(2)}) collective-permute-start(bf16[16,64,128]{2,1,0:T(8,128)(2,1)S(1)} %slice.8.refs_0_), channel_id=1, source_target_pairs={{0,1},{1,0},{2,3},{3,2},{4,5},{5,4},{6,7},{7,6},{8,9},{9,8},{10,11... | collective-permute-start | bytes 786440 | tf_op jit(solution)/shard_map/ppermute | solution.py:379
  87.8 7.2 %collective-permute-done.2.refs_3_ = bf16[16,64,128]{2,1,0:T(8,128)(2,1)S(1)} collective-permute-done((bf16[16,64,128]{2,1,0:T(8,128)(2,1)S(1)}, bf16[16,64,128]{2,1,0:T(8,128)(2,1)S(1)}, u32[]{:S(2)}, u32[]{:S(2)}) %collective-permute-start.2) | collective-permute-done | bytes 262176 | tf_op jit(solution)/shard_map/ppermute | solution.py:379
  95.0 2.5 %collective-permute-done.refs_1_ = bf16[16,64,128]{2,1,0:T(8,128)(2,1)S(1)} collective-permute-done((bf16[16,64,128]{2,1,0:T(8,128)(2,1)S(1)}, bf16[16,64,128]{2,1,0:T(8,128)(2,1)S(1)}, u32[]{:S(2)}, u32[]{:S(2)}) %collective-permute-start) | collective-permute-done | bytes 262176 | tf_op jit(solution)/shard_map/ppermute | solution.py:379
  97.5 1.1 stack.1
  98.6 1.9 %collective-permute-start.4 = (bf16[4,16,64,128]{3,2,1,0:T(8,128)(2,1)}, bf16[4,16,64,128]{3,2,1,0:T(8,128)(2,1)}, u32[]{:S(2)}, u32[]{:S(2)}) collective-permute-start(bf16[4,16,64,128]{3,2,1,0:T(8,128)(2,1)} %get-tuple-element.22.near), channel_id=1, source_target_pairs={{0,8},{8,0},{1,9},{9,1},{2,10},{10,2},{3,11},{11,3},{4,12},{12,4},... | collective-permute-start | bytes 3145736 | tf_op jit(solution)/shard_map/ppermute | solution.py:381
  100.5 2.7 %collective-permute-start.6 = (bf16[4,64,128]{2,1,0:T(8,128)(2,1)S(1)}, bf16[4,64,128]{2,1,0:T(8,128)(2,1)S(1)}, u32[]{:S(2)}, u32[]{:S(2)}) collective-permute-start(bf16[4,64,128]{2,1,0:T(8,128)(2,1)S(1)} %get-tuple-element.23), channel_id=1, source_target_pairs={{0,136},{8,128},{128,8},{136,0},{1,137},{9,129},{129,9},{137,1},{2... | collective-permute-start | bytes 196616 | tf_op jit(solution)/shard_map/ppermute | solution.py:383
  103.2 3.3 %collective-permute-start.5 = (bf16[4,64,128]{2,1,0:T(8,128)(2,1)S(1)}, bf16[4,64,128]{2,1,0:T(8,128)(2,1)S(1)}, u32[]{:S(2)}, u32[]{:S(2)}) collective-permute-start(bf16[4,64,128]{2,1,0:T(8,128)(2,1)S(1)} %get-tuple-element.23), channel_id=1, source_target_pairs={{0,128},{128,0},{1,129},{129,1},{2,130},{130,2},{3,131},{131,3},{4... | collective-permute-start | bytes 196616 | tf_op jit(solution)/shard_map/ppermute | solution.py:382
  106.5 4.2 %all-to-all-done._.base = bf16[16,208,128]{2,1,0:T(8,128)(2,1)S(1)} async-done(((bf16[16,208,128]{2,1,0:T(8,128)(2,1)}), bf16[16,208,128]{2,1,0:T(8,128)(2,1)S(1)}, u32[]{:S(2)}, u32[]{:S(2)}) %all-to-all-start) | async-done | bytes 852000 | tf_op jit(solution)/shard_map/all_to_all | solution.py:376
  110.7 3.4 %expand.1 = (bf16[16,128,128]{2,1,0:T(8,128)(2,1)S(1)}, bf16[16,128,128]{2,1,0:T(8,128)(2,1)S(1)}, bf16[16,128,256]{2,1,0:T(8,128)(2,1)S(1)}, bf16[16,128,256]{2...) custom-call(s32[1]{0:T(128)} %bitcast.me, ...), custom_call_target="tpu_custom_call" | custom-call | tf_op jit(solution)/shard_map/expand/pallas_call | solution.py:210
  114.1 2.0 %grad_chain.1 = (bf16[16,208,128]{2,1,0:T(8,128)(2,1)S(1)}, bf16[16,208,128]{2,1,0:T(8,128)(2,1)S(1)}, bf16[16,208,128]{2,1,0:T(8,128)(2,1)S(1)}, bf16[16,208,12...) custom-call(bf16[16,128,128]{2,1,0:T(8,128)(2,1)S(1)} %get-tuple-element.25.refs_0_.refs_1_, ...), custom_call_target="tpu_custom_call" | custom-call | tf_op jit(solution)/shard_map/grad_chain/pallas_call | solution.py:244
  116.1 6.3 %scores.1 = (bf16[4,8,7,16,128]{4,3,2,1,0:T(8,128)(2,1)S(1)}, bf16[4,8,7,16,128]{4,3,2,1,0:T(8,128)(2,1)S(1)}) custom-call(s32[1]{0:T(128)} %bitcast.me, bf16[16,208,128]{2,1,0:T(8,128)(2,1)S(1)} %all-to-all-done._.base, bf16[16,128,128]{2,1,0:T(8,128)(2,1)S(1)} %get-tuple-element.24.refs_0_, bf16[16,128,128]{2,1,0:T(8,128)(2,1)S(1)} %get-tuple-element.25.refs_0_.refs_1_, ...), custom_call_target="tpu_custom_call" | custom-call | tf_op jit(solution)/shard_map/scores/pallas_call | solution.py:317
  122.4 2.7 %collective-permute-start.7 = (bf16[4,8,7,16,128]{4,3,2,1,0:T(8,128)(2,1)S(1)}, bf16[4,8,7,16,128]{4,3,2,1,0:T(8,128)(2,1)S(1)}, u32[]{:S(2)}, u32[]{:S(2)}) collective-permute-start(bf16[4,8,7,16,128]{4,3,2,1,0:T(8,128)(2,1)S(1)} %get-tuple-element.38), channel_id=1, source_target_pairs={{0,8},{8,0},{1,9},{9,1},{2,10},{10,2},{3,11},{11,3},{4,12},{12,4},... | collective-permute-start | bytes 2752520 | tf_op jit(solution)/shard_map/ppermute | solution.py:389
  125.1 2.1 %collective-permute-done.7.got = bf16[4,8,7,16,128]{4,3,2,1,0:T(8,128)(2,1)S(1)} collective-permute-done((bf16[4,8,7,16,128]{4,3,2,1,0:T(8,128)(2,1)S(1)}, bf16[4,8,7,16,128]{4,3,2,1,0:T(8,128)(2,1)S(1)}, u32[]{:S(2)}, u32[]{:S(2)}) %collective-permute-start.7) | collective-permute-done | bytes 917536 | tf_op jit(solution)/shard_map/ppermute | solution.py:389
  127.2 0.2 core_sum.1
  127.4 16.6 %all_to_all.25.parts = bf16[4,8,7,16,128]{4,3,2,1,0:T(8,128)(2,1)S(1)} all-to-all(bf16[4,8,7,16,128]{4,3,2,1,0:T(8,128)(2,1)S(1)} %core_sum.1), channel_id=1, replica_groups=mesh['x1'=2,'x0'=2,'z'=8,'core'=2,'zh'=2,'y'=4] {'y'}, dimensions={0} | all-to-all | bytes 1835008 | tf_op jit(solution)/shard_map/all_to_all | solution.py:390
  144.0 0.1 copies_of_sum.2
  144.2 35.5 %all_to_all.26.parts = bf16[16,7,16,128]{3,2,1,0:T(8,128)(2,1)S(1)} all-to-all(bf16[16,7,16,128]{3,2,1,0:T(8,128)(2,1)S(1)} %bitcast.11), channel_id=1, replica_groups=mesh['x1'=2,'x0'=2,'z'=8,'core'=2,'zh'=2,'y'=4] {'zh','z'}, dimensions={0} | all-to-all | bytes 917504 | tf_op jit(solution)/shard_map/all_to_all | solution.py:392
  179.6 0.1 copies_of_sum.3
  179.7 10.0 %all_to_all.27.slices = bf16[8,7,16,128]{3,2,1,0:T(8,128)(2,1)S(1)} all-to-all(bf16[8,7,16,128]{3,2,1,0:T(8,128)(2,1)S(1)} %copies_of_sum.3), channel_id=1, replica_groups=mesh['x1'=2,'x0'=2,'z'=8,'core'=2,'zh'=2,'y'=4] {'x0','y'}, dimensions={0} | all-to-all | bytes 458752 | tf_op jit(solution)/shard_map/all_to_all | solution.py:394
  189.7 0.7 finish.1
  (11 shorter events, 0.0 us)
Async XLA Ops:
  0.0 15.5 %copy-start = (f32[1,26]{1,0:T(1,128)S(1)}, f32[1,26]{1,0:T(1,128)}, u32[]{:S(2)}) copy-start(f32[1,26]{1,0:T(1,128)} %param.5) | copy-start | bytes 316
  2.7 12.9 %copy-start.2 = (bf16[128,3328]{1,0:T(8,128)(2,1)S(1)}, bf16[128,3328]{1,0:T(8,128)(2,1)}, u32[]{:S(2)}) copy-start(bf16[128,3328]{1,0:T(8,128)(2,1)} %param.4) | copy-start | bytes 2555908
  2.7 59.1 %all-to-all-start.1 = ((bf16[16,272,128]{2,1,0:T(8,128)(2,1)}), bf16[16,272,128]{2,1,0:T(8,128)(2,1)S(1)}, u32[]{:S(2)}, u32[]{:S(2)}) async-start(bf16[16,272,128]{2,1,0:T(8,128)(2,1)} %pack.1), calls=%async_computation.1 | async-start | bytes 2228224 | tf_op jit(solution)/shard_map/all_to_all | solution.py:372
  61.8 11.6 %copy-start.1 = (bf16[16,272,128]{2,1,0:T(8,128)(2,1)}, bf16[16,272,128]{2,1,0:T(8,128)(2,1)S(1)}, u32[]{:S(2)}) copy-start(bf16[16,272,128]{2,1,0:T(8,128)(2,1)S(1)} %all-to-all-done.1) | copy-start | bytes 3342340
  61.8 48.9 %all-to-all-start = ((bf16[16,208,128]{2,1,0:T(8,128)(2,1)}), bf16[16,208,128]{2,1,0:T(8,128)(2,1)S(1)}, u32[]{:S(2)}, u32[]{:S(2)}) async-start(bf16[16,208,128]{2,1,0:T(8,128)(2,1)} %bitcast.4), calls=%async_computation | async-start | bytes 1703936 | tf_op jit(solution)/shard_map/all_to_all | solution.py:376
  73.5 24.0 %collective-permute-start.3 = (bf16[16,208,128]{2,1,0:T(8,128)(2,1)S(1)}, bf16[16,208,128]{2,1,0:T(8,128)(2,1)S(1)}, u32[]{:S(2)}, u32[]{:S(2)}) collective-permute-start(bf16[16,208,128]{2,1,0:T(8,128)(2,1)S(1)} %slice.9.refs_6_.refs_12_), channel_id=1, source_target_pairs={{0,128},{128,0},{1,129},{129,1},{2,130},{130,2},{3,131},{131,3},{4... | collective-permute-start | bytes 2555912 | tf_op jit(solution)/shard_map/ppermute | solution.py:377
  77.9 17.1 %collective-permute-start.2 = (bf16[16,64,128]{2,1,0:T(8,128)(2,1)S(1)}, bf16[16,64,128]{2,1,0:T(8,128)(2,1)S(1)}, u32[]{:S(2)}, u32[]{:S(2)}) collective-permute-start(bf16[16,64,128]{2,1,0:T(8,128)(2,1)S(1)} %slice.8.refs_0_), channel_id=1, source_target_pairs={{0,3},{1,2},{2,1},{3,0},{4,7},{5,6},{6,5},{7,4},{8,11},{9,10},{10,... | collective-permute-start | bytes 786440 | tf_op jit(solution)/shard_map/ppermute | solution.py:379
  80.1 14.9 %collective-permute-start.1 = (bf16[16,64,128]{2,1,0:T(8,128)(2,1)S(1)}, bf16[16,64,128]{2,1,0:T(8,128)(2,1)S(1)}, u32[]{:S(2)}, u32[]{:S(2)}) collective-permute-start(bf16[16,64,128]{2,1,0:T(8,128)(2,1)S(1)} %slice.8.refs_0_), channel_id=1, source_target_pairs={{0,2},{1,3},{2,0},{3,1},{4,6},{5,7},{6,4},{7,5},{8,10},{9,11},{10,... | collective-permute-start | bytes 786440 | tf_op jit(solution)/shard_map/ppermute | solution.py:379
  84.6 13.0 %collective-permute-start = (bf16[16,64,128]{2,1,0:T(8,128)(2,1)S(1)}, bf16[16,64,128]{2,1,0:T(8,128)(2,1)S(1)}, u32[]{:S(2)}, u32[]{:S(2)}) collective-permute-start(bf16[16,64,128]{2,1,0:T(8,128)(2,1)S(1)} %slice.8.refs_0_), channel_id=1, source_target_pairs={{0,1},{1,0},{2,3},{3,2},{4,5},{5,4},{6,7},{7,6},{8,9},{9,8},{10,11... | collective-permute-start | bytes 786440 | tf_op jit(solution)/shard_map/ppermute | solution.py:379
  98.6 12.1 %collective-permute-start.4 = (bf16[4,16,64,128]{3,2,1,0:T(8,128)(2,1)}, bf16[4,16,64,128]{3,2,1,0:T(8,128)(2,1)}, u32[]{:S(2)}, u32[]{:S(2)}) collective-permute-start(bf16[4,16,64,128]{3,2,1,0:T(8,128)(2,1)} %get-tuple-element.22.near), channel_id=1, source_target_pairs={{0,8},{8,0},{1,9},{9,1},{2,10},{10,2},{3,11},{11,3},{4,12},{12,4},... | collective-permute-start | bytes 3145736 | tf_op jit(solution)/shard_map/ppermute | solution.py:381
  100.5 10.2 %collective-permute-start.6 = (bf16[4,64,128]{2,1,0:T(8,128)(2,1)S(1)}, bf16[4,64,128]{2,1,0:T(8,128)(2,1)S(1)}, u32[]{:S(2)}, u32[]{:S(2)}) collective-permute-start(bf16[4,64,128]{2,1,0:T(8,128)(2,1)S(1)} %get-tuple-element.23), channel_id=1, source_target_pairs={{0,136},{8,128},{128,8},{136,0},{1,137},{9,129},{129,9},{137,1},{2... | collective-permute-start | bytes 196616 | tf_op jit(solution)/shard_map/ppermute | solution.py:383
  103.2 7.5 %collective-permute-start.5 = (bf16[4,64,128]{2,1,0:T(8,128)(2,1)S(1)}, bf16[4,64,128]{2,1,0:T(8,128)(2,1)S(1)}, u32[]{:S(2)}, u32[]{:S(2)}) collective-permute-start(bf16[4,64,128]{2,1,0:T(8,128)(2,1)S(1)} %get-tuple-element.23), channel_id=1, source_target_pairs={{0,128},{128,0},{1,129},{129,1},{2,130},{130,2},{3,131},{131,3},{4... | collective-permute-start | bytes 196616 | tf_op jit(solution)/shard_map/ppermute | solution.py:382
  122.4 4.8 %collective-permute-start.7 = (bf16[4,8,7,16,128]{4,3,2,1,0:T(8,128)(2,1)S(1)}, bf16[4,8,7,16,128]{4,3,2,1,0:T(8,128)(2,1)S(1)}, u32[]{:S(2)}, u32[]{:S(2)}) collective-permute-start(bf16[4,8,7,16,128]{4,3,2,1,0:T(8,128)(2,1)S(1)} %get-tuple-element.38), channel_id=1, source_target_pairs={{0,8},{8,0},{1,9},{9,1},{2,10},{10,2},{3,11},{11,3},{4,12},{12,4},... | collective-permute-start | bytes 2752520 | tf_op jit(solution)/shard_map/ppermute | solution.py:389

commit v6 on v5

--- a/solution.py
+++ b/solution.py
@@ -259,70 +259,90 @@
     return out
 
 
-def score_kernel(me, base, *refs):
+def products(level, core, x_ref, grads, mine, theirs, out):
+    def store(z, halves):
+        for y in range(NY):
+            piece = halves[y // 2][y % 2 * SLICE : (y % 2 + 1) * SLICE]
+            out[y, z, level] = piece.astype(BF)
+
+    if level < 3 or level == TOP:
+        for z in range(NZ):
+            block = 2 * z + core
+            if level == TOP:
+                quad = dot(x_ref[block], jnp.concatenate([mine[block], theirs[block]], axis=1))
+                store(z, (fold(quad[:, :ROWS]), fold(quad[:, ROWS:])))
+            elif level == 2:
+                quad = dot(jnp.concatenate([x_ref[2 * z], x_ref[2 * z + 1]], axis=0), grads[level][block])
+                store(z, (fold(quad[:ROWS]), fold(quad[ROWS:])))
+            elif level == 1:
+                quad = dot(x_ref[block], grads[level][block])
+                even = (iota((HALF, ROWS), 1) // HALF) % 2 == 0
+                rows = [quad[q * HALF : (q + 1) * HALF] for q in range(4)]
+                store(z, (jnp.where(even, rows[0], rows[1]), jnp.where(even, rows[2], rows[3])))
+            else:
+                quad = dot(x_ref[block], grads[level][block])
+                both = jnp.where(iota((BLOCK, ROWS), 1) < BLOCK, quad[:BLOCK], quad[BLOCK:])
+                store(z, (both[:HALF], both[HALF:]))
+        return
+    bit = level - 3
+    for lo in [z for z in range(NZ) if not z >> bit & 1]:
+        hi = lo | 1 << bit
+        x = jnp.concatenate([x_ref[2 * lo + core], x_ref[2 * hi + core]], axis=0)
+        g = jnp.concatenate([grads[level][2 * lo + core], grads[level][2 * hi + core]], axis=1)
+        quad = dot(x, g)
+        for z, at in ((lo, slice(0, ROWS)), (hi, slice(ROWS, 2 * ROWS))):
+            store(z, (fold(quad[:ROWS, at]), fold(quad[ROWS:, at])))
+
+
+def forward_kernel(me, base, *refs):
     dense, grads = refs[:TOP], refs[TOP : 2 * TOP]
-    mine, theirs, own, away, *states = refs[2 * TOP :]
-    first_core = Place(me).core == 0
-
-    def store(level, z, parts):
-        zero, one = parts
-        mine_, other = jnp.where(first_core, zero, one), jnp.where(first_core, one, zero)
-        for y in range(NY):
-            own[y, z, level] = mine_[y * SLICE : (y + 1) * SLICE].astype(BF)
-            away[y, z, level] = other[y * SLICE : (y + 1) * SLICE].astype(BF)
-
-    eye = (iota((ROWS, ROWS), 0) == iota((ROWS, ROWS), 1)).astype(F32).astype(BF)
+    mine, theirs, out, *states = refs[2 * TOP :]
+    other = 1 - Place(me).core
+    for block in range(2 * NZ):
+        states[0][block] = base[block].T
     for level in range(LEVELS):
-        state, after = states[level % 2], states[1 - level % 2]
-        for unit in units(level):
-            parts = {}
-            for lo, hi in unit:
-                if level == 0:
-                    x = dot_nt(eye, base[lo]).astype(BF)
-                elif hi is None:
-                    x = state[lo]
+        if level < TOP:
+            for lo, hi in [pair for unit in units(level) for pair in unit]:
+                if hi is None:
+                    states[level + 1][lo] = dot(dense[level][lo], states[level][lo]).astype(BF)
                 else:
-                    x = jnp.concatenate([state[lo], state[hi]], axis=0)
-                if level == TOP:
-                    g = jnp.concatenate([mine[lo], theirs[lo]], axis=1)
-                elif hi is None:
-                    g = grads[level][lo]
-                else:
-                    g = jnp.concatenate([grads[level][lo], grads[level][hi]], axis=1)
-                if level < 2:
-                    after[lo] = dot(dense[level][lo], x).astype(BF)
-                elif level < TOP:
-                    full = jnp.concatenate([dense[level][lo], dense[level][hi]], axis=0)
-                    out = dot(full, x).astype(BF)
-                    after[lo], after[hi] = out[:ROWS], out[ROWS:]
-                quad = dot(x, g)
-                if level == 0:
-                    parts[lo] = jnp.where(iota((BLOCK, ROWS), 1) < BLOCK, quad[:BLOCK], quad[BLOCK:])
-                elif level == 1:
-                    even = (iota((HALF, ROWS), 1) // HALF) % 2 == 0
-                    rows = [quad[q * HALF : (q + 1) * HALF] for q in range(4)]
-                    parts[lo] = jnp.concatenate([jnp.where(even, rows[0], rows[1]), jnp.where(even, rows[2], rows[3])], axis=0)
-                elif level == TOP:
-                    parts[lo] = jnp.concatenate([fold(quad[:, :ROWS]), fold(quad[:, ROWS:])], axis=0)
-                else:
-                    for b, at in ((lo, slice(0, ROWS)), (hi, slice(ROWS, 2 * ROWS))):
-                        parts[b] = jnp.concatenate([fold(quad[:ROWS, at]), fold(quad[ROWS:, at])], axis=0)
-            for z in sorted({b // 2 for b in parts}):
-                store(level, z, (parts[2 * z], parts[2 * z + 1]))
-
-
-def scores(me, base, dense, grads, mine, theirs):
+                    x = jnp.concatenate([states[level][lo], states[level][hi]], axis=0)
+                    both = dot(jnp.concatenate([dense[level][lo], dense[level][hi]], axis=0), x).astype(BF)
+                    states[level + 1][lo], states[level + 1][hi] = both[:ROWS], both[ROWS:]
+        products(level, other, states[level], grads, mine, theirs, out)
+
+
+def own_kernel(me, *refs):
+    states, grads = refs[:LEVELS], refs[LEVELS : LEVELS + TOP]
+    mine, theirs, out = refs[LEVELS + TOP :]
+    for level in range(LEVELS):
+        products(level, Place(me).core, states[level], grads, mine, theirs, out)
+
+
+def forward(me, base, dense, grads, mine, theirs):
     blocks, wide, rows = base.shape
-    shape = (NY, NZ, LEVELS, SLICE, rows)
-    return pl.pallas_call(
-        score_kernel,
+    shape = jax.ShapeDtypeStruct((NY, NZ, LEVELS, SLICE, rows), BF)
+    out, *states = pl.pallas_call(
+        forward_kernel,
         in_specs=[SCALARS] + [WHOLE] * (2 * TOP + 3),
-        out_specs=[WHOLE] * 2,
-        out_shape=[jax.ShapeDtypeStruct(shape, BF)] * 2,
-        scratch_shapes=[pltpu.VMEM((blocks, rows, wide), BF)] * 2,
-        compiler_params=PARAMS,
-        name="scores",
+        out_specs=[WHOLE] * (1 + LEVELS),
+        out_shape=[shape] + [jax.ShapeDtypeStruct((blocks, rows, wide), BF)] * LEVELS,
+        compiler_params=PARAMS,
+        name="forward",
     )(me, base, *dense, *grads, mine, theirs)
+    return out, states
+
+
+def own_products(me, states, grads, mine, theirs):
+    rows = mine.shape[2]
+    return pl.pallas_call(
+        own_kernel,
+        in_specs=[SCALARS] + [WHOLE] * (LEVELS + TOP + 2),
+        out_specs=WHOLE,
+        out_shape=jax.ShapeDtypeStruct((NY, NZ, LEVELS, SLICE, rows), BF),
+        compiler_params=PARAMS,
+        name="own_products",
+    )(me, *states, *grads, mine, theirs)
 
 
 def call(kernel, shape, *args):
@@ -383,10 +403,12 @@
     partner_away = lax.ppermute(top, ("x0", "core"), flips(4, 3))
     dense = expand(me, near, away, partner_near, partner_away, base)
     grads = grad_chain(dense[1:], mine, theirs)
-    own, away = scores(me, base, dense[:TOP], grads, mine, theirs)
+    away, states = forward(me, base, dense[:TOP], grads, mine, theirs)
+    got = lax.ppermute(away, "core", flips(2))
+    own = own_products(me, states, grads, mine, theirs)
 
     part = (LEVELS, SLICE, rows)
-    total = call(core_sum, jax.ShapeDtypeStruct(own.shape, BF), me, own, lax.ppermute(away, "core", flips(2)))
+    total = call(core_sum, jax.ShapeDtypeStruct(own.shape, BF), me, own, got)
     total = lax.all_to_all(total, "y", 0, 0)
     total = call(copies_of_sum, jax.ShapeDtypeStruct((2, NZ) + part, BF), me, total)
     total = lax.all_to_all(total.reshape((2 * NZ,) + part), ("zh", "z"), 0, 0)

time: 194 us -> 191 us (0.985)
  waiting for transfers between devices: 60.9 us -> 58.5 us
  local copies, waits for them, and re-layouts: 2.4 us -> 4.58 us
    pallas_call x1 -> x2, Pallas kernels: 6.34 us -> 4.38 us  [the longest x1 3.11 us: forward(): pl.pallas_call(forward_kernel, in_specs=[SCALARS] + [WHOLE] * (2 * TOP +...]
  transfers between devices with their start and end apart: 10 -> 10, of which waited for: 5 -> 5; matrix products, arithmetic and copies ran while one was open for 1% -> 2% of each run, Pallas kernels for 1% -> 1%
where the time goes in v6:
time: 191 us; the launch traced here: 188 us
  blocking collectives  62.1 us (33%)
  waiting for transfers between devices  58.5 us (31%)
  starting transfers between devices  48.1 us (25%)
  Pallas kernels  14.6 us (8%)
  local copies, waits for them, and re-layouts  4.58 us (2%)
    all_to_all x1, waiting for transfers between devices, per_device(): lax.all_to_all(pack(me, upstream, factors.transpose(0, 2, 1)), ('z', 'cor...  44.8 us
    all_to_all x1, blocking collectives, per_device(): total = lax.all_to_all(total.reshape((2 * NZ,) + part), ('zh', 'z'), 0, 0)  35.5 us
    all_to_all x1, blocking collectives, per_device(): total = lax.all_to_all(total, 'y', 0, 0)  16.6 us
    all_to_all x1, starting transfers between devices, per_device(): lax.all_to_all(pack(me, upstream, factors.transpose(0, 2, 1)), ('z', 'cor...  12.8 us
    all_to_all x1, starting transfers between devices, per_device(): base = lax.all_to_all(base, ('z', 'core'), 0, 0)  11.6 us
    all_to_all x1, blocking collectives, per_device(): total = lax.all_to_all(total, ('x0', 'y'), 0, 0)  9.95 us
    ppermute x3, starting transfers between devices, per_device(): lax.ppermute(mixing, 'y', flips(NY, k))  9.82 us
    ppermute x3, waiting for transfers between devices, per_device(): lax.ppermute(mixing, 'y', flips(NY, k))  9.78 us
  transfers between devices with their start and end apart: 10, of which 5 were waited for; matrix products, arithmetic and copies ran while one was open for 2% of the time, Pallas kernels for 1%

profile of v6, /device:TPU:24, one launch (start us, length us, event | category | flops | bytes accessed | tf_op | source)
XLA Modules:
  0.0 188.2 jit_solution(10970733083380571928)
XLA Ops:
  0.0 2.7 %pack.1 = bf16[16,272,128]{2,1,0:T(8,128)(2,1)} custom-call(s32[1]{0:T(128)} %bitcast.me, bf16[128,3328]{1,0:T(8,128)(2,1)} %upstream.1, f32[7,64,128]{2,1,0:T(8,128)} %bitcast.12), custom_call_target="tpu_custom_call" | custom-call | tf_op jit(solution)/shard_map/pack/pallas_call | solution.py:110
  2.7 12.8 %all-to-all-start.1 = ((bf16[16,272,128]{2,1,0:T(8,128)(2,1)}), bf16[16,272,128]{2,1,0:T(8,128)(2,1)S(1)}, u32[]{:S(2)}, u32[]{:S(2)}) async-start(bf16[16,272,128]{2,1,0:T(8,128)(2,1)} %pack.1), calls=%async_computation.1 | async-start | bytes 2228224 | tf_op jit(solution)/shard_map/all_to_all | solution.py:392
  15.6 0.1 fusion
  15.7 1.3 copy.5
  17.0 44.8 %all-to-all-done.1 = bf16[16,272,128]{2,1,0:T(8,128)(2,1)S(1)} async-done(((bf16[16,272,128]{2,1,0:T(8,128)(2,1)}), bf16[16,272,128]{2,1,0:T(8,128)(2,1)S(1)}, u32[]{:S(2)}, u32[]{:S(2)}) %all-to-all-start.1) | async-done | bytes 1114144 | tf_op jit(solution)/shard_map/all_to_all | solution.py:392
  61.8 1.0 copy-done.1
  62.8 11.6 %all-to-all-start = ((bf16[16,208,128]{2,1,0:T(8,128)(2,1)}), bf16[16,208,128]{2,1,0:T(8,128)(2,1)S(1)}, u32[]{:S(2)}, u32[]{:S(2)}) async-start(bf16[16,208,128]{2,1,0:T(8,128)(2,1)} %bitcast.4), calls=%async_computation | async-start | bytes 1703936 | tf_op jit(solution)/shard_map/all_to_all | solution.py:396
  74.5 1.2 slice.9.refs_6_.refs_12_.refs_13_
  75.7 3.4 %collective-permute-start.3 = (bf16[16,208,128]{2,1,0:T(8,128)(2,1)S(1)}, bf16[16,208,128]{2,1,0:T(8,128)(2,1)S(1)}, u32[]{:S(2)}, u32[]{:S(2)}) collective-permute-start(bf16[16,208,128]{2,1,0:T(8,128)(2,1)S(1)} %slice.9.refs_6_.refs_12_.refs_13_), channel_id=1, source_target_pairs={{0,128},{128,0},{1,129},{129,1},{2,130},{130,2},{3,131},{131,3},{4... | collective-permute-start | bytes 2555912 | tf_op jit(solution)/shard_map/ppermute | solution.py:397
  79.1 1.0 slice.8.refs_0_
  80.1 2.1 %collective-permute-start.2 = (bf16[16,64,128]{2,1,0:T(8,128)(2,1)S(1)}, bf16[16,64,128]{2,1,0:T(8,128)(2,1)S(1)}, u32[]{:S(2)}, u32[]{:S(2)}) collective-permute-start(bf16[16,64,128]{2,1,0:T(8,128)(2,1)S(1)} %slice.8.refs_0_), channel_id=1, source_target_pairs={{0,3},{1,2},{2,1},{3,0},{4,7},{5,6},{6,5},{7,4},{8,11},{9,10},{10,... | collective-permute-start | bytes 786440 | tf_op jit(solution)/shard_map/ppermute | solution.py:399
  82.2 4.5 %collective-permute-start.1 = (bf16[16,64,128]{2,1,0:T(8,128)(2,1)S(1)}, bf16[16,64,128]{2,1,0:T(8,128)(2,1)S(1)}, u32[]{:S(2)}, u32[]{:S(2)}) collective-permute-start(bf16[16,64,128]{2,1,0:T(8,128)(2,1)S(1)} %slice.8.refs_0_), channel_id=1, source_target_pairs={{0,2},{1,3},{2,0},{3,1},{4,6},{5,7},{6,4},{7,5},{8,10},{9,11},{10,... | collective-permute-start | bytes 786440 | tf_op jit(solution)/shard_map/ppermute | solution.py:399
  86.7 3.2 %collective-permute-start = (bf16[16,64,128]{2,1,0:T(8,128)(2,1)S(1)}, bf16[16,64,128]{2,1,0:T(8,128)(2,1)S(1)}, u32[]{:S(2)}, u32[]{:S(2)}) collective-permute-start(bf16[16,64,128]{2,1,0:T(8,128)(2,1)S(1)} %slice.8.refs_0_), channel_id=1, source_target_pairs={{0,1},{1,0},{2,3},{3,2},{4,5},{5,4},{6,7},{7,6},{8,9},{9,8},{10,11... | collective-permute-start | bytes 786440 | tf_op jit(solution)/shard_map/ppermute | solution.py:399
  89.9 7.2 %collective-permute-done.2.refs_3_ = bf16[16,64,128]{2,1,0:T(8,128)(2,1)S(1)} collective-permute-done((bf16[16,64,128]{2,1,0:T(8,128)(2,1)S(1)}, bf16[16,64,128]{2,1,0:T(8,128)(2,1)S(1)}, u32[]{:S(2)}, u32[]{:S(2)}) %collective-permute-start.2) | collective-permute-done | bytes 262176 | tf_op jit(solution)/shard_map/ppermute | solution.py:399
  97.2 2.5 %collective-permute-done.refs_1_ = bf16[16,64,128]{2,1,0:T(8,128)(2,1)S(1)} collective-permute-done((bf16[16,64,128]{2,1,0:T(8,128)(2,1)S(1)}, bf16[16,64,128]{2,1,0:T(8,128)(2,1)S(1)}, u32[]{:S(2)}, u32[]{:S(2)}) %collective-permute-start) | collective-permute-done | bytes 262176 | tf_op jit(solution)/shard_map/ppermute | solution.py:399
  99.7 1.1 stack.1
  100.8 1.9 %collective-permute-start.4 = (bf16[4,16,64,128]{3,2,1,0:T(8,128)(2,1)}, bf16[4,16,64,128]{3,2,1,0:T(8,128)(2,1)}, u32[]{:S(2)}, u32[]{:S(2)}) collective-permute-start(bf16[4,16,64,128]{3,2,1,0:T(8,128)(2,1)} %get-tuple-element.28.near), channel_id=1, source_target_pairs={{0,8},{8,0},{1,9},{9,1},{2,10},{10,2},{3,11},{11,3},{4,12},{12,4},... | collective-permute-start | bytes 3145736 | tf_op jit(solution)/shard_map/ppermute | solution.py:401
  102.7 2.7 %collective-permute-start.6 = (bf16[4,64,128]{2,1,0:T(8,128)(2,1)S(1)}, bf16[4,64,128]{2,1,0:T(8,128)(2,1)S(1)}, u32[]{:S(2)}, u32[]{:S(2)}) collective-permute-start(bf16[4,64,128]{2,1,0:T(8,128)(2,1)S(1)} %get-tuple-element.29), channel_id=1, source_target_pairs={{0,136},{8,128},{128,8},{136,0},{1,137},{9,129},{129,9},{137,1},{2... | collective-permute-start | bytes 196616 | tf_op jit(solution)/shard_map/ppermute | solution.py:403
  105.3 3.3 %collective-permute-start.5 = (bf16[4,64,128]{2,1,0:T(8,128)(2,1)S(1)}, bf16[4,64,128]{2,1,0:T(8,128)(2,1)S(1)}, u32[]{:S(2)}, u32[]{:S(2)}) collective-permute-start(bf16[4,64,128]{2,1,0:T(8,128)(2,1)S(1)} %get-tuple-element.29), channel_id=1, source_target_pairs={{0,128},{128,0},{1,129},{129,1},{2,130},{130,2},{3,131},{131,3},{4... | collective-permute-start | bytes 196616 | tf_op jit(solution)/shard_map/ppermute | solution.py:402
  108.6 3.1 %all-to-all-done._.base = bf16[16,208,128]{2,1,0:T(8,128)(2,1)S(1)} async-done(((bf16[16,208,128]{2,1,0:T(8,128)(2,1)}), bf16[16,208,128]{2,1,0:T(8,128)(2,1)S(1)}, u32[]{:S(2)}, u32[]{:S(2)}) %all-to-all-start) | async-done | bytes 852000 | tf_op jit(solution)/shard_map/all_to_all | solution.py:396
  111.7 3.4 %expand.1 = (bf16[16,128,128]{2,1,0:T(8,128)(2,1)S(1)}, bf16[16,128,128]{2,1,0:T(8,128)(2,1)S(1)}, bf16[16,128,256]{2,1,0:T(8,128)(2,1)S(1)}, bf16[16,128,256]{2...) custom-call(s32[1]{0:T(128)} %bitcast.me, ...), custom_call_target="tpu_custom_call" | custom-call | tf_op jit(solution)/shard_map/expand/pallas_call | solution.py:210
  115.1 2.0 %grad_chain.1 = (bf16[16,208,128]{2,1,0:T(8,128)(2,1)S(1)}, bf16[16,208,128]{2,1,0:T(8,128)(2,1)S(1)}, bf16[16,208,128]{2,1,0:T(8,128)(2,1)S(1)}, bf16[16,208,12...) custom-call(bf16[16,128,128]{2,1,0:T(8,128)(2,1)S(1)} %get-tuple-element.31.refs_0_.refs_1_, ...), custom_call_target="tpu_custom_call" | custom-call | tf_op jit(solution)/shard_map/grad_chain/pallas_call | solution.py:244
  117.1 3.1 %forward.1 = (bf16[4,8,7,16,128]{4,3,2,1,0:T(8,128)(2,1)S(1)}, bf16[16,128,208]{2,1,0:T(8,128)(2,1)S(1)}, bf16[16,128,208]{2,1,0:T(8,128)(2,1)S(1)}, bf16[16,128...) custom-call(s32[1]{0:T(128)} %bitcast.me, ...), custom_call_target="tpu_custom_call" | custom-call | tf_op jit(solution)/shard_map/forward/pallas_call | solution.py:325
  120.2 2.7 %collective-permute-start.7 = (bf16[4,8,7,16,128]{4,3,2,1,0:T(8,128)(2,1)S(1)}, bf16[4,8,7,16,128]{4,3,2,1,0:T(8,128)(2,1)S(1)}, u32[]{:S(2)}, u32[]{:S(2)}) collective-permute-start(bf16[4,8,7,16,128]{4,3,2,1,0:T(8,128)(2,1)S(1)} %get-tuple-element.50), channel_id=1, source_target_pairs={{0,8},{8,0},{1,9},{9,1},{2,10},{10,2},{3,11},{11,3},{4,12},{12,4},... | collective-permute-start | bytes 2752520 | tf_op jit(solution)/shard_map/ppermute | solution.py:407
  122.9 1.3 own_products.1.own
  124.2 0.8 collective-permute-done.7.got
  125.0 0.2 core_sum.1
  125.2 16.6 %all_to_all.25.parts = bf16[4,8,7,16,128]{4,3,2,1,0:T(8,128)(2,1)S(1)} all-to-all(bf16[4,8,7,16,128]{4,3,2,1,0:T(8,128)(2,1)S(1)} %core_sum.1), channel_id=1, replica_groups=mesh['x1'=2,'x0'=2,'z'=8,'core'=2,'zh'=2,'y'=4] {'y'}, dimensions={0} | all-to-all | bytes 1835008 | tf_op jit(solution)/shard_map/all_to_all | solution.py:412
  141.8 0.1 copies_of_sum.2
  141.9 35.5 %all_to_all.26.parts = bf16[16,7,16,128]{3,2,1,0:T(8,128)(2,1)S(1)} all-to-all(bf16[16,7,16,128]{3,2,1,0:T(8,128)(2,1)S(1)} %bitcast.11), channel_id=1, replica_groups=mesh['x1'=2,'x0'=2,'z'=8,'core'=2,'zh'=2,'y'=4] {'zh','z'}, dimensions={0} | all-to-all | bytes 917504 | tf_op jit(solution)/shard_map/all_to_all | solution.py:414
  177.5 10.0 %all_to_all.27.slices = bf16[8,7,16,128]{3,2,1,0:T(8,128)(2,1)S(1)} all-to-all(bf16[8,7,16,128]{3,2,1,0:T(8,128)(2,1)S(1)} %copies_of_sum.3), channel_id=1, replica_groups=mesh['x1'=2,'x0'=2,'z'=8,'core'=2,'zh'=2,'y'=4] {'x0','y'}, dimensions={0} | all-to-all | bytes 458752 | tf_op jit(solution)/shard_map/all_to_all | solution.py:416
  187.5 0.7 finish.1
  (12 shorter events, 0.2 us)
Async XLA Ops:
  0.0 15.5 %copy-start = (f32[1,26]{1,0:T(1,128)S(1)}, f32[1,26]{1,0:T(1,128)}, u32[]{:S(2)}) copy-start(f32[1,26]{1,0:T(1,128)} %param.5) | copy-start | bytes 316
  2.7 12.9 %copy-start.2 = (bf16[128,3328]{1,0:T(8,128)(2,1)S(1)}, bf16[128,3328]{1,0:T(8,128)(2,1)}, u32[]{:S(2)}) copy-start(bf16[128,3328]{1,0:T(8,128)(2,1)} %param.4) | copy-start | bytes 2555908
  2.7 59.1 %all-to-all-start.1 = ((bf16[16,272,128]{2,1,0:T(8,128)(2,1)}), bf16[16,272,128]{2,1,0:T(8,128)(2,1)S(1)}, u32[]{:S(2)}, u32[]{:S(2)}) async-start(bf16[16,272,128]{2,1,0:T(8,128)(2,1)} %pack.1), calls=%async_computation.1 | async-start | bytes 2228224 | tf_op jit(solution)/shard_map/all_to_all | solution.py:392
  61.8 1.0 copy-start.1
  62.8 48.8 %all-to-all-start = ((bf16[16,208,128]{2,1,0:T(8,128)(2,1)}), bf16[16,208,128]{2,1,0:T(8,128)(2,1)S(1)}, u32[]{:S(2)}, u32[]{:S(2)}) async-start(bf16[16,208,128]{2,1,0:T(8,128)(2,1)} %bitcast.4), calls=%async_computation | async-start | bytes 1703936 | tf_op jit(solution)/shard_map/all_to_all | solution.py:396
  75.7 24.0 %collective-permute-start.3 = (bf16[16,208,128]{2,1,0:T(8,128)(2,1)S(1)}, bf16[16,208,128]{2,1,0:T(8,128)(2,1)S(1)}, u32[]{:S(2)}, u32[]{:S(2)}) collective-permute-start(bf16[16,208,128]{2,1,0:T(8,128)(2,1)S(1)} %slice.9.refs_6_.refs_12_.refs_13_), channel_id=1, source_target_pairs={{0,128},{128,0},{1,129},{129,1},{2,130},{130,2},{3,131},{131,3},{4... | collective-permute-start | bytes 2555912 | tf_op jit(solution)/shard_map/ppermute | solution.py:397
  80.1 17.1 %collective-permute-start.2 = (bf16[16,64,128]{2,1,0:T(8,128)(2,1)S(1)}, bf16[16,64,128]{2,1,0:T(8,128)(2,1)S(1)}, u32[]{:S(2)}, u32[]{:S(2)}) collective-permute-start(bf16[16,64,128]{2,1,0:T(8,128)(2,1)S(1)} %slice.8.refs_0_), channel_id=1, source_target_pairs={{0,3},{1,2},{2,1},{3,0},{4,7},{5,6},{6,5},{7,4},{8,11},{9,10},{10,... | collective-permute-start | bytes 786440 | tf_op jit(solution)/shard_map/ppermute | solution.py:399
  82.2 14.9 %collective-permute-start.1 = (bf16[16,64,128]{2,1,0:T(8,128)(2,1)S(1)}, bf16[16,64,128]{2,1,0:T(8,128)(2,1)S(1)}, u32[]{:S(2)}, u32[]{:S(2)}) collective-permute-start(bf16[16,64,128]{2,1,0:T(8,128)(2,1)S(1)} %slice.8.refs_0_), channel_id=1, source_target_pairs={{0,2},{1,3},{2,0},{3,1},{4,6},{5,7},{6,4},{7,5},{8,10},{9,11},{10,... | collective-permute-start | bytes 786440 | tf_op jit(solution)/shard_map/ppermute | solution.py:399
  86.7 13.0 %collective-permute-start = (bf16[16,64,128]{2,1,0:T(8,128)(2,1)S(1)}, bf16[16,64,128]{2,1,0:T(8,128)(2,1)S(1)}, u32[]{:S(2)}, u32[]{:S(2)}) collective-permute-start(bf16[16,64,128]{2,1,0:T(8,128)(2,1)S(1)} %slice.8.refs_0_), channel_id=1, source_target_pairs={{0,1},{1,0},{2,3},{3,2},{4,5},{5,4},{6,7},{7,6},{8,9},{9,8},{10,11... | collective-permute-start | bytes 786440 | tf_op jit(solution)/shard_map/ppermute | solution.py:399
  100.8 10.9 %collective-permute-start.4 = (bf16[4,16,64,128]{3,2,1,0:T(8,128)(2,1)}, bf16[4,16,64,128]{3,2,1,0:T(8,128)(2,1)}, u32[]{:S(2)}, u32[]{:S(2)}) collective-permute-start(bf16[4,16,64,128]{3,2,1,0:T(8,128)(2,1)} %get-tuple-element.28.near), channel_id=1, source_target_pairs={{0,8},{8,0},{1,9},{9,1},{2,10},{10,2},{3,11},{11,3},{4,12},{12,4},... | collective-permute-start | bytes 3145736 | tf_op jit(solution)/shard_map/ppermute | solution.py:401
  102.7 9.0 %collective-permute-start.6 = (bf16[4,64,128]{2,1,0:T(8,128)(2,1)S(1)}, bf16[4,64,128]{2,1,0:T(8,128)(2,1)S(1)}, u32[]{:S(2)}, u32[]{:S(2)}) collective-permute-start(bf16[4,64,128]{2,1,0:T(8,128)(2,1)S(1)} %get-tuple-element.29), channel_id=1, source_target_pairs={{0,136},{8,128},{128,8},{136,0},{1,137},{9,129},{129,9},{137,1},{2... | collective-permute-start | bytes 196616 | tf_op jit(solution)/shard_map/ppermute | solution.py:403
  105.3 6.3 %collective-permute-start.5 = (bf16[4,64,128]{2,1,0:T(8,128)(2,1)S(1)}, bf16[4,64,128]{2,1,0:T(8,128)(2,1)S(1)}, u32[]{:S(2)}, u32[]{:S(2)}) collective-permute-start(bf16[4,64,128]{2,1,0:T(8,128)(2,1)S(1)} %get-tuple-element.29), channel_id=1, source_target_pairs={{0,128},{128,0},{1,129},{129,1},{2,130},{130,2},{3,131},{131,3},{4... | collective-permute-start | bytes 196616 | tf_op jit(solution)/shard_map/ppermute | solution.py:402
  120.2 4.8 %collective-permute-start.7 = (bf16[4,8,7,16,128]{4,3,2,1,0:T(8,128)(2,1)S(1)}, bf16[4,8,7,16,128]{4,3,2,1,0:T(8,128)(2,1)S(1)}, u32[]{:S(2)}, u32[]{:S(2)}) collective-permute-start(bf16[4,8,7,16,128]{4,3,2,1,0:T(8,128)(2,1)S(1)} %get-tuple-element.50), channel_id=1, source_target_pairs={{0,8},{8,0},{1,9},{9,1},{2,10},{10,2},{3,11},{11,3},{4,12},{12,4},... | collective-permute-start | bytes 2752520 | tf_op jit(solution)/shard_map/ppermute | solution.py:407

commit v7 on v6

--- a/solution.py
+++ b/solution.py
@@ -35,10 +35,6 @@
     return lax.dot_general(a, b, (((1,), (0,)), ((), ())), preferred_element_type=F32)
 
 
-def dot_nt(a, b):
-    return lax.dot_general(a, b, (((1,), (1,)), ((), ())), preferred_element_type=F32)
-
-
 def iota(shape, dim):
     return lax.broadcasted_iota(jnp.int32, shape, dim)
 
@@ -57,7 +53,7 @@
     return [[(2 * z + c, 2 * (z | 1 << bit) + c) for c in range(2)] for z in lows]
 
 
-def pack_kernel(me, upstream, factors, out, wide, mix, turned, in_sems, mix_sem, out_sems):
+def pack_kernel(me, upstream, factors, out, wide, mix, turned, in_sems, mix_sems, out_sems):
     place = Place(me)
     blocks = turned.shape[0]
     chunk = turned.shape[1] - BLOCK
@@ -68,17 +64,17 @@
         pltpu.make_async_copy(upstream.at[:, lo:hi], wide.at[:, lo:hi], in_sems.at[i])
         for i, (lo, hi) in enumerate(zip(edges, edges[1:]))
     ]
-    load_mix = pltpu.make_async_copy(factors, mix, mix_sem)
-    load_mix.start()
-    for load in loads:
+    levels = [jnp.minimum(2 * place.y + side, TOP) for side in range(2)]
+    load_mix = [pltpu.make_async_copy(factors.at[level], mix.at[i], mix_sems.at[i]) for i, level in enumerate(levels)]
+    for load in load_mix + loads:
         load.start()
-    load_mix.wait()
+    for load in load_mix:
+        load.wait()
     row = place.first_row + iota((BLOCK, ROWS), 1)
     sides = []
-    for side in range(2):
-        level = jnp.minimum(2 * place.y + side, TOP)
+    for side, level in enumerate(levels):
         pick = lax.shift_right_logical(row, level + 5) % 2 * HALF + row % HALF
-        sides.append((iota((BLOCK, ROWS), 0) == pick).astype(F32) + mix[level])
+        sides.append((iota((BLOCK, ROWS), 0) == pick).astype(F32) + mix[side])
     tile = jnp.concatenate(sides, axis=0).T.astype(BF)
     for block in range(blocks):
         half = block % 2 * BLOCK
@@ -114,10 +110,10 @@
         out_shape=jax.ShapeDtypeStruct(shape, BF),
         scratch_shapes=[
             pltpu.VMEM((rows, wide), BF),
-            pltpu.VMEM(factors.shape, F32),
+            pltpu.VMEM((2,) + factors.shape[1:], F32),
             pltpu.VMEM(shape, BF),
             pltpu.SemaphoreType.DMA((4,)),
-            pltpu.SemaphoreType.DMA,
+            pltpu.SemaphoreType.DMA((2,)),
             pltpu.SemaphoreType.DMA((4,)),
         ],
         compiler_params=pltpu.CompilerParams(vmem_limit_bytes=58 * 2**20),
@@ -220,35 +216,30 @@
     )(me, near, away, partner_near, partner_away, after)
 
 
-def grad_kernel(*refs):
-    dense, mine, theirs, grads = refs[:TOP], refs[TOP], refs[TOP + 1], refs[TOP + 2 :]
-    for level in range(TOP, 0, -1):
-        mix, above, out_ref = dense[level - 1], grads[level] if level < TOP else None, grads[level - 1]
-        for unit in units(level):
-            for lo, hi in unit:
-                if level == TOP:
-                    both = jnp.concatenate([mine[lo], theirs[lo]], axis=1)
-                    full = jnp.concatenate([mix[lo, :, :ROWS], mix[lo, :, ROWS:]], axis=0)
-                elif level == 1:
-                    both, full = above[lo], mix[lo]
-                else:
-                    both = jnp.concatenate([above[lo], above[hi]], axis=1)
-                    full = jnp.concatenate([mix[lo], mix[hi]], axis=0)
-                out = dot(both, full).astype(BF)
-                out_ref[lo] = out[:, :ROWS]
-                if hi is not None:
-                    out_ref[hi] = out[:, ROWS:]
-
-
-def grad_chain(dense, mine, theirs):
-    return pl.pallas_call(
-        grad_kernel,
-        in_specs=[WHOLE] * (TOP + 2),
-        out_specs=[WHOLE] * TOP,
-        out_shape=[jax.ShapeDtypeStruct(mine.shape, BF)] * TOP,
-        compiler_params=PARAMS,
-        name="grad_chain",
-    )(*dense, mine, theirs)
+def grad_step(level, mix, above, mine, theirs, below):
+    for lo, hi in [pair for unit in units(level) for pair in unit]:
+        if level == TOP:
+            both = jnp.concatenate([mine[lo], theirs[lo]], axis=1)
+            full = jnp.concatenate([mix[lo, :, :ROWS], mix[lo, :, ROWS:]], axis=0)
+        elif level == 1:
+            both, full = above[lo], mix[lo]
+        else:
+            both = jnp.concatenate([above[lo], above[hi]], axis=1)
+            full = jnp.concatenate([mix[lo], mix[hi]], axis=0)
+        out = dot(both, full).astype(BF)
+        below[lo] = out[:, :ROWS]
+        if hi is not None:
+            below[hi] = out[:, ROWS:]
+
+
+def forward_step(level, mix, x_ref, after):
+    for lo, hi in [pair for unit in units(level) for pair in unit]:
+        if hi is None:
+            after[lo] = dot(mix[lo], x_ref[lo]).astype(BF)
+        else:
+            x = jnp.concatenate([x_ref[lo], x_ref[hi]], axis=0)
+            both = dot(jnp.concatenate([mix[lo], mix[hi]], axis=0), x).astype(BF)
+            after[lo], after[hi] = both[:ROWS], both[ROWS:]
 
 
 def fold(quad):
@@ -294,21 +285,17 @@
             store(z, (fold(quad[:ROWS, at]), fold(quad[ROWS:, at])))
 
 
-def forward_kernel(me, base, *refs):
-    dense, grads = refs[:TOP], refs[TOP : 2 * TOP]
-    mine, theirs, out, *states = refs[2 * TOP :]
+def chain_kernel(me, base, *refs):
+    dense, (mine, theirs, out) = refs[:LEVELS], refs[LEVELS : LEVELS + 3]
+    grads, states = refs[LEVELS + 3 : LEVELS + 3 + TOP], refs[LEVELS + 3 + TOP :]
     other = 1 - Place(me).core
     for block in range(2 * NZ):
         states[0][block] = base[block].T
+    for step in range(TOP):
+        level = TOP - step
+        grad_step(level, dense[level], grads[level] if level < TOP else None, mine, theirs, grads[level - 1])
+        forward_step(step, dense[step], states[step], states[step + 1])
     for level in range(LEVELS):
-        if level < TOP:
-            for lo, hi in [pair for unit in units(level) for pair in unit]:
-                if hi is None:
-                    states[level + 1][lo] = dot(dense[level][lo], states[level][lo]).astype(BF)
-                else:
-                    x = jnp.concatenate([states[level][lo], states[level][hi]], axis=0)
-                    both = dot(jnp.concatenate([dense[level][lo], dense[level][hi]], axis=0), x).astype(BF)
-                    states[level + 1][lo], states[level + 1][hi] = both[:ROWS], both[ROWS:]
         products(level, other, states[level], grads, mine, theirs, out)
 
 
@@ -319,18 +306,19 @@
         products(level, Place(me).core, states[level], grads, mine, theirs, out)
 
 
-def forward(me, base, dense, grads, mine, theirs):
+def chains(me, base, dense, mine, theirs):
     blocks, wide, rows = base.shape
-    shape = jax.ShapeDtypeStruct((NY, NZ, LEVELS, SLICE, rows), BF)
-    out, *states = pl.pallas_call(
-        forward_kernel,
-        in_specs=[SCALARS] + [WHOLE] * (2 * TOP + 3),
-        out_specs=[WHOLE] * (1 + LEVELS),
-        out_shape=[shape] + [jax.ShapeDtypeStruct((blocks, rows, wide), BF)] * LEVELS,
+    results = pl.pallas_call(
+        chain_kernel,
+        in_specs=[SCALARS] + [WHOLE] * (LEVELS + 3),
+        out_specs=[WHOLE] * (1 + TOP + LEVELS),
+        out_shape=[jax.ShapeDtypeStruct((NY, NZ, LEVELS, SLICE, rows), BF)]
+        + [jax.ShapeDtypeStruct(base.shape, BF)] * TOP
+        + [jax.ShapeDtypeStruct((blocks, rows, wide), BF)] * LEVELS,
         compiler_params=PARAMS,
-        name="forward",
-    )(me, base, *dense, *grads, mine, theirs)
-    return out, states
+        name="chains",
+    )(me, base, *dense, mine, theirs)
+    return results[0], results[1 : 1 + TOP], results[1 + TOP :]
 
 
 def own_products(me, states, grads, mine, theirs):
@@ -402,8 +390,7 @@
     partner_near = lax.ppermute(top, "x0", flips(2))
     partner_away = lax.ppermute(top, ("x0", "core"), flips(4, 3))
     dense = expand(me, near, away, partner_near, partner_away, base)
-    grads = grad_chain(dense[1:], mine, theirs)
-    away, states = forward(me, base, dense[:TOP], grads, mine, theirs)
+    away, grads, states = chains(me, base, dense, mine, theirs)
     got = lax.ppermute(away, "core", flips(2))
     own = own_products(me, states, grads, mine, theirs)
 

time: 191 us -> 191 us (level)
    pallas_call x2 -> x1, Pallas kernels: 5.08 us -> 4.75 us  [chains(): pl.pallas_call(chain_kernel, in_specs=[SCALARS] + [WHOLE] * (LEVELS + 3),...]
where the time goes in v7:
time: 191 us; the launch traced here: 188 us
  blocking collectives  62.1 us (33%)
  waiting for transfers between devices  58.5 us (31%)
  starting transfers between devices  48.2 us (25%)
  Pallas kernels  14.1 us (7%)
  local copies, waits for them, and re-layouts  4.56 us (2%)
    all_to_all x1, waiting for transfers between devices, per_device(): lax.all_to_all(pack(me, upstream, factors.transpose(0, 2, 1)), ('z', 'cor...  44.8 us
    all_to_all x1, blocking collectives, per_device(): total = lax.all_to_all(total.reshape((2 * NZ,) + part), ('zh', 'z'), 0, 0)  35.5 us
    all_to_all x1, blocking collectives, per_device(): total = lax.all_to_all(total, 'y', 0, 0)  16.6 us
    all_to_all x1, starting transfers between devices, per_device(): lax.all_to_all(pack(me, upstream, factors.transpose(0, 2, 1)), ('z', 'cor...  12.8 us
    all_to_all x1, starting transfers between devices, per_device(): base = lax.all_to_all(base, ('z', 'core'), 0, 0)  11.6 us
    all_to_all x1, blocking collectives, per_device(): total = lax.all_to_all(total, ('x0', 'y'), 0, 0)  9.95 us
    ppermute x3, starting transfers between devices, per_device(): lax.ppermute(mixing, 'y', flips(NY, k))  9.82 us
    ppermute x3, waiting for transfers between devices, per_device(): lax.ppermute(mixing, 'y', flips(NY, k))  9.78 us
  transfers between devices with their start and end apart: 10, of which 5 were waited for; matrix products, arithmetic and copies ran while one was open for 2% of the time, Pallas kernels for 1%

profile of v7, /device:TPU:24, one launch (start us, length us, event | category | flops | bytes accessed | tf_op | source)
XLA Modules:
  0.0 187.6 jit_solution(2049297661406187469)
XLA Ops:
  0.0 2.5 %pack.1 = bf16[16,272,128]{2,1,0:T(8,128)(2,1)} custom-call(s32[1]{0:T(128)} %bitcast.me, bf16[128,3328]{1,0:T(8,128)(2,1)} %upstream.1, f32[7,64,128]{2,1,0:T(8,128)} %bitcast.12), custom_call_target="tpu_custom_call" | custom-call | tf_op jit(solution)/shard_map/pack/pallas_call | solution.py:106
  2.5 12.8 %all-to-all-start.1 = ((bf16[16,272,128]{2,1,0:T(8,128)(2,1)}), bf16[16,272,128]{2,1,0:T(8,128)(2,1)S(1)}, u32[]{:S(2)}, u32[]{:S(2)}) async-start(bf16[16,272,128]{2,1,0:T(8,128)(2,1)} %pack.1), calls=%async_computation.1 | async-start | bytes 2228224 | tf_op jit(solution)/shard_map/all_to_all | solution.py:380
  15.3 0.1 broadcast_bitcast_fusion
  15.4 0.1 fusion
  15.5 1.3 copy.5
  16.8 44.8 %all-to-all-done.1 = bf16[16,272,128]{2,1,0:T(8,128)(2,1)S(1)} async-done(((bf16[16,272,128]{2,1,0:T(8,128)(2,1)}), bf16[16,272,128]{2,1,0:T(8,128)(2,1)S(1)}, u32[]{:S(2)}, u32[]{:S(2)}) %all-to-all-start.1) | async-done | bytes 1114144 | tf_op jit(solution)/shard_map/all_to_all | solution.py:380
  61.6 1.0 copy-done.1
  62.6 11.6 %all-to-all-start = ((bf16[16,208,128]{2,1,0:T(8,128)(2,1)}), bf16[16,208,128]{2,1,0:T(8,128)(2,1)S(1)}, u32[]{:S(2)}, u32[]{:S(2)}) async-start(bf16[16,208,128]{2,1,0:T(8,128)(2,1)} %bitcast.4), calls=%async_computation | async-start | bytes 1703936 | tf_op jit(solution)/shard_map/all_to_all | solution.py:384
  74.3 1.2 slice.9.refs_7_.refs_13_
  75.5 3.4 %collective-permute-start.3 = (bf16[16,208,128]{2,1,0:T(8,128)(2,1)S(1)}, bf16[16,208,128]{2,1,0:T(8,128)(2,1)S(1)}, u32[]{:S(2)}, u32[]{:S(2)}) collective-permute-start(bf16[16,208,128]{2,1,0:T(8,128)(2,1)S(1)} %slice.9.refs_7_.refs_13_), channel_id=1, source_target_pairs={{0,128},{128,0},{1,129},{129,1},{2,130},{130,2},{3,131},{131,3},{4... | collective-permute-start | bytes 2555912 | tf_op jit(solution)/shard_map/ppermute | solution.py:385
  78.9 1.0 slice.8.refs_0_
  79.9 2.1 %collective-permute-start.2 = (bf16[16,64,128]{2,1,0:T(8,128)(2,1)S(1)}, bf16[16,64,128]{2,1,0:T(8,128)(2,1)S(1)}, u32[]{:S(2)}, u32[]{:S(2)}) collective-permute-start(bf16[16,64,128]{2,1,0:T(8,128)(2,1)S(1)} %slice.8.refs_0_), channel_id=1, source_target_pairs={{0,3},{1,2},{2,1},{3,0},{4,7},{5,6},{6,5},{7,4},{8,11},{9,10},{10,... | collective-permute-start | bytes 786440 | tf_op jit(solution)/shard_map/ppermute | solution.py:387
  82.0 4.5 %collective-permute-start.1 = (bf16[16,64,128]{2,1,0:T(8,128)(2,1)S(1)}, bf16[16,64,128]{2,1,0:T(8,128)(2,1)S(1)}, u32[]{:S(2)}, u32[]{:S(2)}) collective-permute-start(bf16[16,64,128]{2,1,0:T(8,128)(2,1)S(1)} %slice.8.refs_0_), channel_id=1, source_target_pairs={{0,2},{1,3},{2,0},{3,1},{4,6},{5,7},{6,4},{7,5},{8,10},{9,11},{10,... | collective-permute-start | bytes 786440 | tf_op jit(solution)/shard_map/ppermute | solution.py:387
  86.5 3.2 %collective-permute-start = (bf16[16,64,128]{2,1,0:T(8,128)(2,1)S(1)}, bf16[16,64,128]{2,1,0:T(8,128)(2,1)S(1)}, u32[]{:S(2)}, u32[]{:S(2)}) collective-permute-start(bf16[16,64,128]{2,1,0:T(8,128)(2,1)S(1)} %slice.8.refs_0_), channel_id=1, source_target_pairs={{0,1},{1,0},{2,3},{3,2},{4,5},{5,4},{6,7},{7,6},{8,9},{9,8},{10,11... | collective-permute-start | bytes 786440 | tf_op jit(solution)/shard_map/ppermute | solution.py:387
  89.7 7.2 %collective-permute-done.2.refs_3_ = bf16[16,64,128]{2,1,0:T(8,128)(2,1)S(1)} collective-permute-done((bf16[16,64,128]{2,1,0:T(8,128)(2,1)S(1)}, bf16[16,64,128]{2,1,0:T(8,128)(2,1)S(1)}, u32[]{:S(2)}, u32[]{:S(2)}) %collective-permute-start.2) | collective-permute-done | bytes 262176 | tf_op jit(solution)/shard_map/ppermute | solution.py:387
  97.0 2.5 %collective-permute-done.refs_1_ = bf16[16,64,128]{2,1,0:T(8,128)(2,1)S(1)} collective-permute-done((bf16[16,64,128]{2,1,0:T(8,128)(2,1)S(1)}, bf16[16,64,128]{2,1,0:T(8,128)(2,1)S(1)}, u32[]{:S(2)}, u32[]{:S(2)}) %collective-permute-start) | collective-permute-done | bytes 262176 | tf_op jit(solution)/shard_map/ppermute | solution.py:387
  99.5 1.1 stack.1
  100.6 1.9 %collective-permute-start.4 = (bf16[4,16,64,128]{3,2,1,0:T(8,128)(2,1)}, bf16[4,16,64,128]{3,2,1,0:T(8,128)(2,1)}, u32[]{:S(2)}, u32[]{:S(2)}) collective-permute-start(bf16[4,16,64,128]{3,2,1,0:T(8,128)(2,1)} %get-tuple-element.28.near), channel_id=1, source_target_pairs={{0,8},{8,0},{1,9},{9,1},{2,10},{10,2},{3,11},{11,3},{4,12},{12,4},... | collective-permute-start | bytes 3145736 | tf_op jit(solution)/shard_map/ppermute | solution.py:389
  102.5 2.7 %collective-permute-start.6 = (bf16[4,64,128]{2,1,0:T(8,128)(2,1)S(1)}, bf16[4,64,128]{2,1,0:T(8,128)(2,1)S(1)}, u32[]{:S(2)}, u32[]{:S(2)}) collective-permute-start(bf16[4,64,128]{2,1,0:T(8,128)(2,1)S(1)} %get-tuple-element.29), channel_id=1, source_target_pairs={{0,136},{8,128},{128,8},{136,0},{1,137},{9,129},{129,9},{137,1},{2... | collective-permute-start | bytes 196616 | tf_op jit(solution)/shard_map/ppermute | solution.py:391
  105.2 3.3 %collective-permute-start.5 = (bf16[4,64,128]{2,1,0:T(8,128)(2,1)S(1)}, bf16[4,64,128]{2,1,0:T(8,128)(2,1)S(1)}, u32[]{:S(2)}, u32[]{:S(2)}) collective-permute-start(bf16[4,64,128]{2,1,0:T(8,128)(2,1)S(1)} %get-tuple-element.29), channel_id=1, source_target_pairs={{0,128},{128,0},{1,129},{129,1},{2,130},{130,2},{3,131},{131,3},{4... | collective-permute-start | bytes 196616 | tf_op jit(solution)/shard_map/ppermute | solution.py:390
  108.5 3.0 %all-to-all-done._.base = bf16[16,208,128]{2,1,0:T(8,128)(2,1)S(1)} async-done(((bf16[16,208,128]{2,1,0:T(8,128)(2,1)}), bf16[16,208,128]{2,1,0:T(8,128)(2,1)S(1)}, u32[]{:S(2)}, u32[]{:S(2)}) %all-to-all-start) | async-done | bytes 852000 | tf_op jit(solution)/shard_map/all_to_all | solution.py:384
  111.5 3.4 %expand.1 = (bf16[16,128,128]{2,1,0:T(8,128)(2,1)S(1)}, bf16[16,128,128]{2,1,0:T(8,128)(2,1)S(1)}, bf16[16,128,256]{2,1,0:T(8,128)(2,1)S(1)}, bf16[16,128,256]{2...) custom-call(s32[1]{0:T(128)} %bitcast.me, ...), custom_call_target="tpu_custom_call" | custom-call | tf_op jit(solution)/shard_map/expand/pallas_call | solution.py:206
  114.9 4.8 %chains.1 = (bf16[4,8,7,16,128]{4,3,2,1,0:T(8,128)(2,1)S(1)}, bf16[16,208,128]{2,1,0:T(8,128)(2,1)S(1)}, bf16[16,208,128]{2,1,0:T(8,128)(2,1)S(1)}, bf16[16,208,...) custom-call(s32[1]{0:T(128)} %bitcast.me, ...), custom_call_target="tpu_custom_call" | custom-call | tf_op jit(solution)/shard_map/chains/pallas_call | solution.py:311
  119.7 2.7 %collective-permute-start.7 = (bf16[4,8,7,16,128]{4,3,2,1,0:T(8,128)(2,1)S(1)}, bf16[4,8,7,16,128]{4,3,2,1,0:T(8,128)(2,1)S(1)}, u32[]{:S(2)}, u32[]{:S(2)}) collective-permute-start(bf16[4,8,7,16,128]{4,3,2,1,0:T(8,128)(2,1)S(1)} %get-tuple-element.50), channel_id=1, source_target_pairs={{0,8},{8,0},{1,9},{9,1},{2,10},{10,2},{3,11},{11,3},{4,12},{12,4},... | collective-permute-start | bytes 2752520 | tf_op jit(solution)/shard_map/ppermute | solution.py:394
  122.4 1.3 own_products.1.own
  123.7 0.8 collective-permute-done.7.got
  124.5 0.2 core_sum.1
  124.7 16.6 %all_to_all.25.parts = bf16[4,8,7,16,128]{4,3,2,1,0:T(8,128)(2,1)S(1)} all-to-all(bf16[4,8,7,16,128]{4,3,2,1,0:T(8,128)(2,1)S(1)} %core_sum.1), channel_id=1, replica_groups=mesh['x1'=2,'x0'=2,'z'=8,'core'=2,'zh'=2,'y'=4] {'y'}, dimensions={0} | all-to-all | bytes 1835008 | tf_op jit(solution)/shard_map/all_to_all | solution.py:399
  141.3 0.1 copies_of_sum.2
  141.4 35.5 %all_to_all.26.parts = bf16[16,7,16,128]{3,2,1,0:T(8,128)(2,1)S(1)} all-to-all(bf16[16,7,16,128]{3,2,1,0:T(8,128)(2,1)S(1)} %bitcast.11), channel_id=1, replica_groups=mesh['x1'=2,'x0'=2,'z'=8,'core'=2,'zh'=2,'y'=4] {'zh','z'}, dimensions={0} | all-to-all | bytes 917504 | tf_op jit(solution)/shard_map/all_to_all | solution.py:401
  177.0 9.9 %all_to_all.27.slices = bf16[8,7,16,128]{3,2,1,0:T(8,128)(2,1)S(1)} all-to-all(bf16[8,7,16,128]{3,2,1,0:T(8,128)(2,1)S(1)} %copies_of_sum.3), channel_id=1, replica_groups=mesh['x1'=2,'x0'=2,'z'=8,'core'=2,'zh'=2,'y'=4] {'x0','y'}, dimensions={0} | all-to-all | bytes 458752 | tf_op jit(solution)/shard_map/all_to_all | solution.py:403
  186.9 0.7 finish.1
  (11 shorter events, 0.1 us)
Async XLA Ops:
  0.0 15.3 %copy-start = (f32[1,26]{1,0:T(1,128)S(1)}, f32[1,26]{1,0:T(1,128)}, u32[]{:S(2)}) copy-start(f32[1,26]{1,0:T(1,128)} %param.5) | copy-start | bytes 316
  2.5 12.9 %copy-start.2 = (bf16[128,3328]{1,0:T(8,128)(2,1)S(1)}, bf16[128,3328]{1,0:T(8,128)(2,1)}, u32[]{:S(2)}) copy-start(bf16[128,3328]{1,0:T(8,128)(2,1)} %param.4) | copy-start | bytes 2555908
  2.5 59.1 %all-to-all-start.1 = ((bf16[16,272,128]{2,1,0:T(8,128)(2,1)}), bf16[16,272,128]{2,1,0:T(8,128)(2,1)S(1)}, u32[]{:S(2)}, u32[]{:S(2)}) async-start(bf16[16,272,128]{2,1,0:T(8,128)(2,1)} %pack.1), calls=%async_computation.1 | async-start | bytes 2228224 | tf_op jit(solution)/shard_map/all_to_all | solution.py:380
  61.6 1.0 copy-start.1
  62.6 48.8 %all-to-all-start = ((bf16[16,208,128]{2,1,0:T(8,128)(2,1)}), bf16[16,208,128]{2,1,0:T(8,128)(2,1)S(1)}, u32[]{:S(2)}, u32[]{:S(2)}) async-start(bf16[16,208,128]{2,1,0:T(8,128)(2,1)} %bitcast.4), calls=%async_computation | async-start | bytes 1703936 | tf_op jit(solution)/shard_map/all_to_all | solution.py:384
  75.5 24.0 %collective-permute-start.3 = (bf16[16,208,128]{2,1,0:T(8,128)(2,1)S(1)}, bf16[16,208,128]{2,1,0:T(8,128)(2,1)S(1)}, u32[]{:S(2)}, u32[]{:S(2)}) collective-permute-start(bf16[16,208,128]{2,1,0:T(8,128)(2,1)S(1)} %slice.9.refs_7_.refs_13_), channel_id=1, source_target_pairs={{0,128},{128,0},{1,129},{129,1},{2,130},{130,2},{3,131},{131,3},{4... | collective-permute-start | bytes 2555912 | tf_op jit(solution)/shard_map/ppermute | solution.py:385
  79.9 17.1 %collective-permute-start.2 = (bf16[16,64,128]{2,1,0:T(8,128)(2,1)S(1)}, bf16[16,64,128]{2,1,0:T(8,128)(2,1)S(1)}, u32[]{:S(2)}, u32[]{:S(2)}) collective-permute-start(bf16[16,64,128]{2,1,0:T(8,128)(2,1)S(1)} %slice.8.refs_0_), channel_id=1, source_target_pairs={{0,3},{1,2},{2,1},{3,0},{4,7},{5,6},{6,5},{7,4},{8,11},{9,10},{10,... | collective-permute-start | bytes 786440 | tf_op jit(solution)/shard_map/ppermute | solution.py:387
  82.0 14.9 %collective-permute-start.1 = (bf16[16,64,128]{2,1,0:T(8,128)(2,1)S(1)}, bf16[16,64,128]{2,1,0:T(8,128)(2,1)S(1)}, u32[]{:S(2)}, u32[]{:S(2)}) collective-permute-start(bf16[16,64,128]{2,1,0:T(8,128)(2,1)S(1)} %slice.8.refs_0_), channel_id=1, source_target_pairs={{0,2},{1,3},{2,0},{3,1},{4,6},{5,7},{6,4},{7,5},{8,10},{9,11},{10,... | collective-permute-start | bytes 786440 | tf_op jit(solution)/shard_map/ppermute | solution.py:387
  86.5 13.0 %collective-permute-start = (bf16[16,64,128]{2,1,0:T(8,128)(2,1)S(1)}, bf16[16,64,128]{2,1,0:T(8,128)(2,1)S(1)}, u32[]{:S(2)}, u32[]{:S(2)}) collective-permute-start(bf16[16,64,128]{2,1,0:T(8,128)(2,1)S(1)} %slice.8.refs_0_), channel_id=1, source_target_pairs={{0,1},{1,0},{2,3},{3,2},{4,5},{5,4},{6,7},{7,6},{8,9},{9,8},{10,11... | collective-permute-start | bytes 786440 | tf_op jit(solution)/shard_map/ppermute | solution.py:387
  100.6 10.9 %collective-permute-start.4 = (bf16[4,16,64,128]{3,2,1,0:T(8,128)(2,1)}, bf16[4,16,64,128]{3,2,1,0:T(8,128)(2,1)}, u32[]{:S(2)}, u32[]{:S(2)}) collective-permute-start(bf16[4,16,64,128]{3,2,1,0:T(8,128)(2,1)} %get-tuple-element.28.near), channel_id=1, source_target_pairs={{0,8},{8,0},{1,9},{9,1},{2,10},{10,2},{3,11},{11,3},{4,12},{12,4},... | collective-permute-start | bytes 3145736 | tf_op jit(solution)/shard_map/ppermute | solution.py:389
  102.5 9.0 %collective-permute-start.6 = (bf16[4,64,128]{2,1,0:T(8,128)(2,1)S(1)}, bf16[4,64,128]{2,1,0:T(8,128)(2,1)S(1)}, u32[]{:S(2)}, u32[]{:S(2)}) collective-permute-start(bf16[4,64,128]{2,1,0:T(8,128)(2,1)S(1)} %get-tuple-element.29), channel_id=1, source_target_pairs={{0,136},{8,128},{128,8},{136,0},{1,137},{9,129},{129,9},{137,1},{2... | collective-permute-start | bytes 196616 | tf_op jit(solution)/shard_map/ppermute | solution.py:391
  105.2 6.3 %collective-permute-start.5 = (bf16[4,64,128]{2,1,0:T(8,128)(2,1)S(1)}, bf16[4,64,128]{2,1,0:T(8,128)(2,1)S(1)}, u32[]{:S(2)}, u32[]{:S(2)}) collective-permute-start(bf16[4,64,128]{2,1,0:T(8,128)(2,1)S(1)} %get-tuple-element.29), channel_id=1, source_target_pairs={{0,128},{128,0},{1,129},{129,1},{2,130},{130,2},{3,131},{131,3},{4... | collective-permute-start | bytes 196616 | tf_op jit(solution)/shard_map/ppermute | solution.py:390
  119.7 4.8 %collective-permute-start.7 = (bf16[4,8,7,16,128]{4,3,2,1,0:T(8,128)(2,1)S(1)}, bf16[4,8,7,16,128]{4,3,2,1,0:T(8,128)(2,1)S(1)}, u32[]{:S(2)}, u32[]{:S(2)}) collective-permute-start(bf16[4,8,7,16,128]{4,3,2,1,0:T(8,128)(2,1)S(1)} %get-tuple-element.50), channel_id=1, source_target_pairs={{0,8},{8,0},{1,9},{9,1},{2,10},{10,2},{3,11},{11,3},{4,12},{12,4},... | collective-permute-start | bytes 2752520 | tf_op jit(solution)/shard_map/ppermute | solution.py:394

commit v8 on v7

--- a/solution.py
+++ b/solution.py
@@ -75,6 +75,7 @@
     for side, level in enumerate(levels):
         pick = lax.shift_right_logical(row, level + 5) % 2 * HALF + row % HALF
         sides.append((iota((BLOCK, ROWS), 0) == pick).astype(F32) + mix[side])
+    sides[1] = jnp.where(place.y == NY - 1, pltpu.roll(sides[1], BLOCK, 1), sides[1])
     tile = jnp.concatenate(sides, axis=0).T.astype(BF)
     for block in range(blocks):
         half = block % 2 * BLOCK
@@ -128,15 +129,17 @@
         out[k] = part[...]
     which = jnp.bitwise_xor(place.y, NY - 1)
     src, col = iota((ROWS, ROWS), 0), iota((ROWS, ROWS), 1)
-    picks = []
-    for j in range(4):
-        pick = (col // HALF == j) & (src == HALF * (1 - place.x0) + col % HALF)
-        picks.append(pick.astype(F32).astype(BF))
-    for k in range(top.shape[0]):
-        packed = dot(out[which, 4 * k], picks[0])
-        for j in range(1, 4):
-            packed = packed + dot(out[which, 4 * k + j], picks[j])
-        top[k] = packed.astype(BF)
+    for h in range(2):
+        picks = []
+        for j in range(4):
+            pick = (col // HALF == j) & (src == h * BLOCK + HALF * (1 - place.x0) + col % HALF)
+            picks.append(pick.astype(F32).astype(BF))
+        count = top.shape[0] // 2
+        for k in range(count):
+            packed = dot(out[which, 4 * k], picks[0])
+            for j in range(1, 4):
+                packed = packed + dot(out[which, 4 * k + j], picks[j])
+            top[h * count + k] = packed.astype(BF)
 
 
 def stack(me, parts, after):
@@ -147,7 +150,7 @@
         out_specs=[WHOLE] * 2,
         out_shape=[
             jax.ShapeDtypeStruct((NY, blocks, rows, wide), BF),
-            jax.ShapeDtypeStruct((blocks // 4, rows, wide), BF),
+            jax.ShapeDtypeStruct((blocks // 2, rows, wide), BF),
         ],
         compiler_params=PARAMS,
         name="stack",
@@ -171,57 +174,97 @@
     return [pick.astype(F32).astype(BF) for pick in picks], keep
 
 
-def expand_kernel(me, near, away, partner_near, partner_away, _, *refs):
-    dense, held, sems = refs[:LEVELS], refs[LEVELS:-1], refs[-1]
+def top_kernel(me, near, halves, mine, theirs, out, held, sem):
     place = Place(me)
     first_core = place.core == 0
-    loads = [[] for _ in range(NY)]
-    for j in reversed(range(NY)):
-        for c, ref in enumerate((near, away)):
-            loads[j].append(pltpu.make_async_copy(ref.at[jnp.bitwise_xor(place.y, j)], held[c].at[j], sems.at[j, c]))
-        if j == NY - 1:
-            for c, ref in enumerate((partner_near, partner_away)):
-                loads[j].append(pltpu.make_async_copy(ref, held[2 + c], sems.at[NY, c]))
-        for load in loads[j]:
+    load = pltpu.make_async_copy(near.at[jnp.bitwise_xor(place.y, NY - 1)], held, sem)
+    load.start()
+    load.wait()
+    src, col = iota((ROWS, ROWS), 0), iota((ROWS, ROWS), 1)
+    keep = src // HALF == col // HALF
+    own = [(src == h * BLOCK + HALF * place.x0 + col % HALF).astype(F32).astype(BF) for h in range(2)]
+    far = [(src == HALF * j + col % HALF).astype(F32).astype(BF) for j in range(4)]
+    count = halves.shape[0] // 2
+
+    def rows(one, other):
+        low, high = jnp.where(first_core, one, other), jnp.where(first_core, other, one)
+        return jnp.where(keep, jnp.concatenate([low, high], axis=0), 0.0).astype(BF)
+
+    for block in range(2 * NZ):
+        k, pick = block // 4, far[block % 4]
+        full = [rows(dot(held[block], own[0]), dot(held[block], own[1]))]
+        full.append(rows(dot(halves[k], pick), dot(halves[count + k], pick)))
+        both = jnp.concatenate([mine[block], theirs[block]], axis=1)
+        out[block] = dot(both, jnp.concatenate(full, axis=0)).astype(BF)
+
+
+def top_grad(me, near, halves, mine, theirs):
+    return pl.pallas_call(
+        top_kernel,
+        in_specs=[SCALARS, pl.BlockSpec(memory_space=pl.ANY)] + [WHOLE] * 3,
+        out_specs=WHOLE,
+        out_shape=jax.ShapeDtypeStruct(mine.shape, BF),
+        scratch_shapes=[pltpu.VMEM(near.shape[1:], BF), pltpu.SemaphoreType.DMA],
+        compiler_params=PARAMS,
+        name="top_grad",
+    )(me, near, halves, mine, theirs)
+
+
+def spread(level, place, whole, dense):
+    picks, keep = spreader(level, place.x0)
+    for block in range(2 * NZ):
+        full = dot(whole(block), picks[0])
+        dense[block, :, : full.shape[1]] = jnp.where(keep, full, 0.0).astype(BF)
+
+
+def dense_shape(level):
+    return jax.ShapeDtypeStruct((2 * NZ, ROWS, ROWS if level < 2 else 2 * ROWS), BF)
+
+
+def expand_kernel(me, near, away, _, *refs):
+    dense, held, sems = refs[:TOP], refs[TOP:-1], refs[-1]
+    place = Place(me)
+    first_core = place.core == 0
+    loads = [
+        [
+            pltpu.make_async_copy(ref.at[jnp.bitwise_xor(place.y, j)], held[c].at[j], sems.at[j, c])
+            for c, ref in enumerate((near, away))
+        ]
+        for j in range(TOP // 2)
+    ]
+    for pair in loads:
+        for load in pair:
             load.start()
 
-    def rows(one, other):
-        return jnp.concatenate([jnp.where(first_core, one, other), jnp.where(first_core, other, one)], axis=0)
-
-    for level in reversed(range(LEVELS)):
-        if level == TOP or level % 2:
-            for load in loads[level // 2]:
+    for level in range(TOP):
+        j = level // 2
+        if level % 2 == 0:
+            for load in loads[j]:
                 load.wait()
-        picks, keep = spreader(level, place.x0)
-        for block in range(2 * NZ):
-            full = dot(rows(held[0][level // 2, block], held[1][level // 2, block]), picks[0])
-            dense[level][block, :, : full.shape[1]] = jnp.where(keep, full, 0.0).astype(BF)
-            if level == TOP:
-                far = dot(rows(held[2][block // 4], held[3][block // 4]), picks[1 + block % 4])
-                dense[level][block, :, ROWS:] = jnp.where(keep, far, 0.0).astype(BF)
-
-
-def expand(me, near, away, partner_near, partner_away, after):
-    narrow, wide = (2 * NZ, ROWS, ROWS), (2 * NZ, ROWS, 2 * ROWS)
+
+        def whole(block):
+            one, other = held[0][j, block], held[1][j, block]
+            return jnp.concatenate([jnp.where(first_core, one, other), jnp.where(first_core, other, one)], axis=0)
+
+        spread(level, place, whole, dense[level])
+
+
+def expand(me, near, away, after):
+    held = pltpu.VMEM((TOP // 2,) + near.shape[1:], BF)
     return pl.pallas_call(
         expand_kernel,
-        in_specs=[SCALARS] + [pl.BlockSpec(memory_space=pl.ANY)] * 5,
-        out_specs=[WHOLE] * LEVELS,
-        out_shape=[jax.ShapeDtypeStruct(narrow if level < 2 else wide, BF) for level in range(LEVELS)],
-        scratch_shapes=[pltpu.VMEM(near.shape, BF)] * 2
-        + [pltpu.VMEM(partner_near.shape, BF)] * 2
-        + [pltpu.SemaphoreType.DMA((NY + 1, 2))],
+        in_specs=[SCALARS] + [pl.BlockSpec(memory_space=pl.ANY)] * 3,
+        out_specs=[WHOLE] * TOP,
+        out_shape=[dense_shape(level) for level in range(TOP)],
+        scratch_shapes=[held, held, pltpu.SemaphoreType.DMA((TOP // 2, 2))],
         compiler_params=PARAMS,
         name="expand",
-    )(me, near, away, partner_near, partner_away, after)
-
-
-def grad_step(level, mix, above, mine, theirs, below):
+    )(me, near, away, after)
+
+
+def grad_step(level, mix, above, below):
     for lo, hi in [pair for unit in units(level) for pair in unit]:
-        if level == TOP:
-            both = jnp.concatenate([mine[lo], theirs[lo]], axis=1)
-            full = jnp.concatenate([mix[lo, :, :ROWS], mix[lo, :, ROWS:]], axis=0)
-        elif level == 1:
+        if level == 1:
             both, full = above[lo], mix[lo]
         else:
             both = jnp.concatenate([above[lo], above[hi]], axis=1)
@@ -286,14 +329,15 @@
 
 
 def chain_kernel(me, base, *refs):
-    dense, (mine, theirs, out) = refs[:LEVELS], refs[LEVELS : LEVELS + 3]
-    grads, states = refs[LEVELS + 3 : LEVELS + 3 + TOP], refs[LEVELS + 3 + TOP :]
+    dense, (top, mine, theirs, out) = refs[:TOP], refs[TOP : TOP + 4]
+    grads, states = refs[TOP + 4 : 2 * TOP + 3] + (top,), refs[2 * TOP + 3 :]
     other = 1 - Place(me).core
     for block in range(2 * NZ):
         states[0][block] = base[block].T
     for step in range(TOP):
-        level = TOP - step
-        grad_step(level, dense[level], grads[level] if level < TOP else None, mine, theirs, grads[level - 1])
+        level = TOP - 1 - step
+        if level:
+            grad_step(level, dense[level], grads[level], grads[level - 1])
         forward_step(step, dense[step], states[step], states[step + 1])
     for level in range(LEVELS):
         products(level, other, states[level], grads, mine, theirs, out)
@@ -306,19 +350,19 @@
         products(level, Place(me).core, states[level], grads, mine, theirs, out)
 
 
-def chains(me, base, dense, mine, theirs):
+def chains(me, base, dense, top, mine, theirs):
     blocks, wide, rows = base.shape
     results = pl.pallas_call(
         chain_kernel,
-        in_specs=[SCALARS] + [WHOLE] * (LEVELS + 3),
-        out_specs=[WHOLE] * (1 + TOP + LEVELS),
+        in_specs=[SCALARS] + [WHOLE] * (TOP + 4),
+        out_specs=[WHOLE] * (TOP + LEVELS),
         out_shape=[jax.ShapeDtypeStruct((NY, NZ, LEVELS, SLICE, rows), BF)]
-        + [jax.ShapeDtypeStruct(base.shape, BF)] * TOP
+        + [jax.ShapeDtypeStruct(base.shape, BF)] * (TOP - 1)
         + [jax.ShapeDtypeStruct((blocks, rows, wide), BF)] * LEVELS,
         compiler_params=PARAMS,
         name="chains",
-    )(me, base, *dense, mine, theirs)
-    return results[0], results[1 : 1 + TOP], results[1 + TOP :]
+    )(me, base, *dense, top, mine, theirs)
+    return results[0], [*results[1:TOP], top], results[TOP:]
 
 
 def own_products(me, states, grads, mine, theirs):
@@ -387,10 +431,10 @@
     near = [mixing] + [lax.ppermute(mixing, "y", flips(NY, k)) for k in range(1, NY)]
     near, top = stack(me, near, theirs)
     away = lax.ppermute(near, "core", flips(2))
-    partner_near = lax.ppermute(top, "x0", flips(2))
-    partner_away = lax.ppermute(top, ("x0", "core"), flips(4, 3))
-    dense = expand(me, near, away, partner_near, partner_away, base)
-    away, grads, states = chains(me, base, dense, mine, theirs)
+    halves = lax.ppermute(top, "x0", flips(2))
+    top = top_grad(me, near, halves, mine, theirs)
+    dense = expand(me, near, away, base)
+    away, grads, states = chains(me, base, dense, top, mine, theirs)
     got = lax.ppermute(away, "core", flips(2))
     own = own_products(me, states, grads, mine, theirs)
 

time: 191 us -> 190 us (level)
  starting transfers between devices: 48.2 us -> 44 us
  waiting for transfers between devices: 58.5 us -> 61 us
  Pallas kernels: 14.1 us -> 16.1 us
    ppermute x2 -> x1, waiting for transfers between devices: 0.01 us -> 5.22 us  [per_device(): halves = lax.ppermute(top, 'x0', flips(2))]
    ppermute x2 -> x1, starting transfers between devices: 5.95 us -> 2.56 us  [per_device(): halves = lax.ppermute(top, 'x0', flips(2))]
    all_to_all x1, waiting for transfers between devices: 3.05 us -> 0.01 us  [per_device(): base = lax.all_to_all(base, ('z', 'core'), 0, 0)]
    pallas_call x1 -> x2, Pallas kernels: 4.75 us -> 7.24 us  [the longest x1 4.4 us: chains(): pl.pallas_call(chain_kernel, in_specs=[SCALARS] + [WHOLE] * (TOP + 4), ou...]
  transfers between devices with their start and end apart: 10 -> 9, of which waited for: 5 -> 5; matrix products, arithmetic and copies ran while one was open for 2% -> 2% of each run, Pallas kernels for 1% -> 3%
where the time goes in v8:
time: 190 us; the launch traced here: 187 us
  waiting for transfers between devices  61 us (32%)
  blocking collectives  60.8 us (32%)
  starting transfers between devices  44 us (23%)
  Pallas kernels  16.1 us (8%)
  local copies, waits for them, and re-layouts  4.57 us (2%)
    all_to_all x1, waiting for transfers between devices, per_device(): lax.all_to_all(pack(me, upstream, factors.transpose(0, 2, 1)), ('z', 'cor...  44.8 us
    all_to_all x1, blocking collectives, per_device(): total = lax.all_to_all(total.reshape((2 * NZ,) + part), ('zh', 'z'), 0, 0)  34.5 us
    all_to_all x1, blocking collectives, per_device(): total = lax.all_to_all(total, 'y', 0, 0)  16.4 us
    all_to_all x1, starting transfers between devices, per_device(): lax.all_to_all(pack(me, upstream, factors.transpose(0, 2, 1)), ('z', 'cor...  12.8 us
    all_to_all x1, starting transfers between devices, per_device(): base = lax.all_to_all(base, ('z', 'core'), 0, 0)  11.6 us
    all_to_all x1, blocking collectives, per_device(): total = lax.all_to_all(total, ('x0', 'y'), 0, 0)  9.97 us
    ppermute x3, starting transfers between devices, per_device(): lax.ppermute(mixing, 'y', flips(NY, k))  9.82 us
    ppermute x3, waiting for transfers between devices, per_device(): lax.ppermute(mixing, 'y', flips(NY, k))  9.78 us
  transfers between devices with their start and end apart: 9, of which 5 were waited for; matrix products, arithmetic and copies ran while one was open for 2% of the time, Pallas kernels for 3%

profile of v8, /device:TPU:24, one launch (start us, length us, event | category | flops | bytes accessed | tf_op | source)
XLA Modules:
  0.0 186.9 jit_solution(7917842983262645644)
XLA Ops:
  0.0 2.6 %pack.1 = bf16[16,272,128]{2,1,0:T(8,128)(2,1)} custom-call(s32[1]{0:T(128)} %bitcast.me, bf16[128,3328]{1,0:T(8,128)(2,1)} %upstream.1, f32[7,64,128]{2,1,0:T(8,128)} %bitcast.12), custom_call_target="tpu_custom_call" | custom-call | tf_op jit(solution)/shard_map/pack/pallas_call | solution.py:107
  2.6 12.8 %all-to-all-start.1 = ((bf16[16,272,128]{2,1,0:T(8,128)(2,1)}), bf16[16,272,128]{2,1,0:T(8,128)(2,1)S(1)}, u32[]{:S(2)}, u32[]{:S(2)}) async-start(bf16[16,272,128]{2,1,0:T(8,128)(2,1)} %pack.1), calls=%async_computation.1 | async-start | bytes 2228224 | tf_op jit(solution)/shard_map/all_to_all | solution.py:424
  15.4 0.1 broadcast_bitcast_fusion
  15.4 0.1 fusion
  15.6 1.3 copy.5
  16.9 44.8 %all-to-all-done.1 = bf16[16,272,128]{2,1,0:T(8,128)(2,1)S(1)} async-done(((bf16[16,272,128]{2,1,0:T(8,128)(2,1)}), bf16[16,272,128]{2,1,0:T(8,128)(2,1)S(1)}, u32[]{:S(2)}, u32[]{:S(2)}) %all-to-all-start.1) | async-done | bytes 1114144 | tf_op jit(solution)/shard_map/all_to_all | solution.py:424
  61.7 1.0 copy-done.1
  62.7 11.6 %all-to-all-start = ((bf16[16,208,128]{2,1,0:T(8,128)(2,1)}), bf16[16,208,128]{2,1,0:T(8,128)(2,1)S(1)}, u32[]{:S(2)}, u32[]{:S(2)}) async-start(bf16[16,208,128]{2,1,0:T(8,128)(2,1)} %bitcast.4), calls=%async_computation | async-start | bytes 1703936 | tf_op jit(solution)/shard_map/all_to_all | solution.py:428
  74.4 1.2 slice.9.mine.refs_7_.refs_13_
  75.6 3.4 %collective-permute-start.3 = (bf16[16,208,128]{2,1,0:T(8,128)(2,1)S(1)}, bf16[16,208,128]{2,1,0:T(8,128)(2,1)S(1)}, u32[]{:S(2)}, u32[]{:S(2)}) collective-permute-start(bf16[16,208,128]{2,1,0:T(8,128)(2,1)S(1)} %slice.9.mine.refs_7_.refs_13_), channel_id=1, source_target_pairs={{0,128},{128,0},{1,129},{129,1},{2,130},{130,2},{3,131},{131,3},{4... | collective-permute-start | bytes 2555912 | tf_op jit(solution)/shard_map/ppermute | solution.py:429
  79.0 1.0 slice.8.refs_0_
  80.0 2.1 %collective-permute-start.2 = (bf16[16,64,128]{2,1,0:T(8,128)(2,1)S(1)}, bf16[16,64,128]{2,1,0:T(8,128)(2,1)S(1)}, u32[]{:S(2)}, u32[]{:S(2)}) collective-permute-start(bf16[16,64,128]{2,1,0:T(8,128)(2,1)S(1)} %slice.8.refs_0_), channel_id=1, source_target_pairs={{0,3},{1,2},{2,1},{3,0},{4,7},{5,6},{6,5},{7,4},{8,11},{9,10},{10,... | collective-permute-start | bytes 786440 | tf_op jit(solution)/shard_map/ppermute | solution.py:431
  82.1 4.5 %collective-permute-start.1 = (bf16[16,64,128]{2,1,0:T(8,128)(2,1)S(1)}, bf16[16,64,128]{2,1,0:T(8,128)(2,1)S(1)}, u32[]{:S(2)}, u32[]{:S(2)}) collective-permute-start(bf16[16,64,128]{2,1,0:T(8,128)(2,1)S(1)} %slice.8.refs_0_), channel_id=1, source_target_pairs={{0,2},{1,3},{2,0},{3,1},{4,6},{5,7},{6,4},{7,5},{8,10},{9,11},{10,... | collective-permute-start | bytes 786440 | tf_op jit(solution)/shard_map/ppermute | solution.py:431
  86.6 3.2 %collective-permute-start = (bf16[16,64,128]{2,1,0:T(8,128)(2,1)S(1)}, bf16[16,64,128]{2,1,0:T(8,128)(2,1)S(1)}, u32[]{:S(2)}, u32[]{:S(2)}) collective-permute-start(bf16[16,64,128]{2,1,0:T(8,128)(2,1)S(1)} %slice.8.refs_0_), channel_id=1, source_target_pairs={{0,1},{1,0},{2,3},{3,2},{4,5},{5,4},{6,7},{7,6},{8,9},{9,8},{10,11... | collective-permute-start | bytes 786440 | tf_op jit(solution)/shard_map/ppermute | solution.py:431
  89.8 7.2 %collective-permute-done.2.refs_3_ = bf16[16,64,128]{2,1,0:T(8,128)(2,1)S(1)} collective-permute-done((bf16[16,64,128]{2,1,0:T(8,128)(2,1)S(1)}, bf16[16,64,128]{2,1,0:T(8,128)(2,1)S(1)}, u32[]{:S(2)}, u32[]{:S(2)}) %collective-permute-start.2) | collective-permute-done | bytes 262176 | tf_op jit(solution)/shard_map/ppermute | solution.py:431
  97.0 2.5 %collective-permute-done.refs_1_ = bf16[16,64,128]{2,1,0:T(8,128)(2,1)S(1)} collective-permute-done((bf16[16,64,128]{2,1,0:T(8,128)(2,1)S(1)}, bf16[16,64,128]{2,1,0:T(8,128)(2,1)S(1)}, u32[]{:S(2)}, u32[]{:S(2)}) %collective-permute-start) | collective-permute-done | bytes 262176 | tf_op jit(solution)/shard_map/ppermute | solution.py:431
  99.6 1.0 stack.1
  100.6 1.9 %collective-permute-start.4 = (bf16[4,16,64,128]{3,2,1,0:T(8,128)(2,1)}, bf16[4,16,64,128]{3,2,1,0:T(8,128)(2,1)}, u32[]{:S(2)}, u32[]{:S(2)}) collective-permute-start(bf16[4,16,64,128]{3,2,1,0:T(8,128)(2,1)} %get-tuple-element.26.near), channel_id=1, source_target_pairs={{0,8},{8,0},{1,9},{9,1},{2,10},{10,2},{3,11},{11,3},{4,12},{12,4},... | collective-permute-start | bytes 3145736 | tf_op jit(solution)/shard_map/ppermute | solution.py:433
  102.5 2.6 %collective-permute-start.5 = (bf16[8,64,128]{2,1,0:T(8,128)(2,1)S(1)}, bf16[8,64,128]{2,1,0:T(8,128)(2,1)S(1)}, u32[]{:S(2)}, u32[]{:S(2)}) collective-permute-start(bf16[8,64,128]{2,1,0:T(8,128)(2,1)S(1)} %get-tuple-element.33), channel_id=1, source_target_pairs={{0,128},{128,0},{1,129},{129,1},{2,130},{130,2},{3,131},{131,3},{4... | collective-permute-start | bytes 393224 | tf_op jit(solution)/shard_map/ppermute | solution.py:434
  105.1 5.2 %collective-permute-done.5.halves = bf16[8,64,128]{2,1,0:T(8,128)(2,1)S(1)} collective-permute-done((bf16[8,64,128]{2,1,0:T(8,128)(2,1)S(1)}, bf16[8,64,128]{2,1,0:T(8,128)(2,1)S(1)}, u32[]{:S(2)}, u32[]{:S(2)}) %collective-permute-start.5) | collective-permute-done | bytes 131104 | tf_op jit(solution)/shard_map/ppermute | solution.py:434
  110.3 2.8 %top_grad.1.refs_6_.refs_12_ = bf16[16,208,128]{2,1,0:T(8,128)(2,1)S(1)} custom-call(s32[1]{0:T(128)} %bitcast.me, bf16[4,16,64,128]{3,2,1,0:T(8,128)(2,1)} %get-tuple-element.26.near, bf16[8,64,128]{2,1,0:T(8,128)(2,1)S(1)} %collective-permute-done.5.halves, bf16[16,208,128]{2,1,0:T(8,128)(2,1)S(1)} %slice.9.mine.refs_7_.refs_13_, ...), custom_call_target="tpu_custom_call" | custom-call | tf_op jit(solution)/shard_map/top_grad/pallas_call | solution.py:202
  113.2 2.9 %expand.1 = (bf16[16,128,128]{2,1,0:T(8,128)(2,1)S(1)}, bf16[16,128,128]{2,1,0:T(8,128)(2,1)S(1)}, bf16[16,128,256]{2,1,0:T(8,128)(2,1)S(1)}, bf16[16,128,256]{2...) custom-call(s32[1]{0:T(128)} %bitcast.me, ...), custom_call_target="tpu_custom_call" | custom-call | tf_op jit(solution)/shard_map/expand/pallas_call | solution.py:254
  116.1 4.4 %chains.1 = (bf16[4,8,7,16,128]{4,3,2,1,0:T(8,128)(2,1)S(1)}, bf16[16,208,128]{2,1,0:T(8,128)(2,1)S(1)}, bf16[16,208,128]{2,1,0:T(8,128)(2,1)S(1)}, bf16[16,208,...) custom-call(s32[1]{0:T(128)} %bitcast.me, ...), custom_call_target="tpu_custom_call" | custom-call | tf_op jit(solution)/shard_map/chains/pallas_call | solution.py:355
  120.6 1.9 %collective-permute-start.6 = (bf16[4,8,7,16,128]{4,3,2,1,0:T(8,128)(2,1)S(1)}, bf16[4,8,7,16,128]{4,3,2,1,0:T(8,128)(2,1)S(1)}, u32[]{:S(2)}, u32[]{:S(2)}) collective-permute-start(bf16[4,8,7,16,128]{4,3,2,1,0:T(8,128)(2,1)S(1)} %get-tuple-element.46), channel_id=1, source_target_pairs={{0,8},{8,0},{1,9},{9,1},{2,10},{10,2},{3,11},{11,3},{4,12},{12,4},... | collective-permute-start | bytes 2752520 | tf_op jit(solution)/shard_map/ppermute | solution.py:438
  122.5 1.3 own_products.1.own
  123.8 1.2 collective-permute-done.6.got
  124.9 0.2 core_sum.1
  125.1 16.4 %all_to_all.25.parts = bf16[4,8,7,16,128]{4,3,2,1,0:T(8,128)(2,1)S(1)} all-to-all(bf16[4,8,7,16,128]{4,3,2,1,0:T(8,128)(2,1)S(1)} %core_sum.1), channel_id=1, replica_groups=mesh['x1'=2,'x0'=2,'z'=8,'core'=2,'zh'=2,'y'=4] {'y'}, dimensions={0} | all-to-all | bytes 1835008 | tf_op jit(solution)/shard_map/all_to_all | solution.py:443
  141.5 0.1 copies_of_sum.2
  141.7 34.5 %all_to_all.26.parts = bf16[16,7,16,128]{3,2,1,0:T(8,128)(2,1)S(1)} all-to-all(bf16[16,7,16,128]{3,2,1,0:T(8,128)(2,1)S(1)} %bitcast.11), channel_id=1, replica_groups=mesh['x1'=2,'x0'=2,'z'=8,'core'=2,'zh'=2,'y'=4] {'zh','z'}, dimensions={0} | all-to-all | bytes 917504 | tf_op jit(solution)/shard_map/all_to_all | solution.py:445
  176.2 10.0 %all_to_all.27.slices = bf16[8,7,16,128]{3,2,1,0:T(8,128)(2,1)S(1)} all-to-all(bf16[8,7,16,128]{3,2,1,0:T(8,128)(2,1)S(1)} %copies_of_sum.3), channel_id=1, replica_groups=mesh['x1'=2,'x0'=2,'z'=8,'core'=2,'zh'=2,'y'=4] {'x0','y'}, dimensions={0} | all-to-all | bytes 458752 | tf_op jit(solution)/shard_map/all_to_all | solution.py:447
  186.2 0.7 finish.1
  (10 shorter events, 0.1 us)
Async XLA Ops:
  0.0 15.4 %copy-start = (f32[1,26]{1,0:T(1,128)S(1)}, f32[1,26]{1,0:T(1,128)}, u32[]{:S(2)}) copy-start(f32[1,26]{1,0:T(1,128)} %param.5) | copy-start | bytes 316
  2.6 12.9 %copy-start.2 = (bf16[128,3328]{1,0:T(8,128)(2,1)S(1)}, bf16[128,3328]{1,0:T(8,128)(2,1)}, u32[]{:S(2)}) copy-start(bf16[128,3328]{1,0:T(8,128)(2,1)} %param.4) | copy-start | bytes 2555908
  2.6 59.1 %all-to-all-start.1 = ((bf16[16,272,128]{2,1,0:T(8,128)(2,1)}), bf16[16,272,128]{2,1,0:T(8,128)(2,1)S(1)}, u32[]{:S(2)}, u32[]{:S(2)}) async-start(bf16[16,272,128]{2,1,0:T(8,128)(2,1)} %pack.1), calls=%async_computation.1 | async-start | bytes 2228224 | tf_op jit(solution)/shard_map/all_to_all | solution.py:424
  61.7 1.0 copy-start.1
  62.7 50.5 %all-to-all-start = ((bf16[16,208,128]{2,1,0:T(8,128)(2,1)}), bf16[16,208,128]{2,1,0:T(8,128)(2,1)S(1)}, u32[]{:S(2)}, u32[]{:S(2)}) async-start(bf16[16,208,128]{2,1,0:T(8,128)(2,1)} %bitcast.4), calls=%async_computation | async-start | bytes 1703936 | tf_op jit(solution)/shard_map/all_to_all | solution.py:428
  75.6 24.0 %collective-permute-start.3 = (bf16[16,208,128]{2,1,0:T(8,128)(2,1)S(1)}, bf16[16,208,128]{2,1,0:T(8,128)(2,1)S(1)}, u32[]{:S(2)}, u32[]{:S(2)}) collective-permute-start(bf16[16,208,128]{2,1,0:T(8,128)(2,1)S(1)} %slice.9.mine.refs_7_.refs_13_), channel_id=1, source_target_pairs={{0,128},{128,0},{1,129},{129,1},{2,130},{130,2},{3,131},{131,3},{4... | collective-permute-start | bytes 2555912 | tf_op jit(solution)/shard_map/ppermute | solution.py:429
  80.0 17.1 %collective-permute-start.2 = (bf16[16,64,128]{2,1,0:T(8,128)(2,1)S(1)}, bf16[16,64,128]{2,1,0:T(8,128)(2,1)S(1)}, u32[]{:S(2)}, u32[]{:S(2)}) collective-permute-start(bf16[16,64,128]{2,1,0:T(8,128)(2,1)S(1)} %slice.8.refs_0_), channel_id=1, source_target_pairs={{0,3},{1,2},{2,1},{3,0},{4,7},{5,6},{6,5},{7,4},{8,11},{9,10},{10,... | collective-permute-start | bytes 786440 | tf_op jit(solution)/shard_map/ppermute | solution.py:431
  82.1 14.9 %collective-permute-start.1 = (bf16[16,64,128]{2,1,0:T(8,128)(2,1)S(1)}, bf16[16,64,128]{2,1,0:T(8,128)(2,1)S(1)}, u32[]{:S(2)}, u32[]{:S(2)}) collective-permute-start(bf16[16,64,128]{2,1,0:T(8,128)(2,1)S(1)} %slice.8.refs_0_), channel_id=1, source_target_pairs={{0,2},{1,3},{2,0},{3,1},{4,6},{5,7},{6,4},{7,5},{8,10},{9,11},{10,... | collective-permute-start | bytes 786440 | tf_op jit(solution)/shard_map/ppermute | solution.py:431
  86.6 13.0 %collective-permute-start = (bf16[16,64,128]{2,1,0:T(8,128)(2,1)S(1)}, bf16[16,64,128]{2,1,0:T(8,128)(2,1)S(1)}, u32[]{:S(2)}, u32[]{:S(2)}) collective-permute-start(bf16[16,64,128]{2,1,0:T(8,128)(2,1)S(1)} %slice.8.refs_0_), channel_id=1, source_target_pairs={{0,1},{1,0},{2,3},{3,2},{4,5},{5,4},{6,7},{7,6},{8,9},{9,8},{10,11... | collective-permute-start | bytes 786440 | tf_op jit(solution)/shard_map/ppermute | solution.py:431
  100.6 12.6 %collective-permute-start.4 = (bf16[4,16,64,128]{3,2,1,0:T(8,128)(2,1)}, bf16[4,16,64,128]{3,2,1,0:T(8,128)(2,1)}, u32[]{:S(2)}, u32[]{:S(2)}) collective-permute-start(bf16[4,16,64,128]{3,2,1,0:T(8,128)(2,1)} %get-tuple-element.26.near), channel_id=1, source_target_pairs={{0,8},{8,0},{1,9},{9,1},{2,10},{10,2},{3,11},{11,3},{4,12},{12,4},... | collective-permute-start | bytes 3145736 | tf_op jit(solution)/shard_map/ppermute | solution.py:433
  102.5 7.8 %collective-permute-start.5 = (bf16[8,64,128]{2,1,0:T(8,128)(2,1)S(1)}, bf16[8,64,128]{2,1,0:T(8,128)(2,1)S(1)}, u32[]{:S(2)}, u32[]{:S(2)}) collective-permute-start(bf16[8,64,128]{2,1,0:T(8,128)(2,1)S(1)} %get-tuple-element.33), channel_id=1, source_target_pairs={{0,128},{128,0},{1,129},{129,1},{2,130},{130,2},{3,131},{131,3},{4... | collective-permute-start | bytes 393224 | tf_op jit(solution)/shard_map/ppermute | solution.py:434
  120.6 4.4 %collective-permute-start.6 = (bf16[4,8,7,16,128]{4,3,2,1,0:T(8,128)(2,1)S(1)}, bf16[4,8,7,16,128]{4,3,2,1,0:T(8,128)(2,1)S(1)}, u32[]{:S(2)}, u32[]{:S(2)}) collective-permute-start(bf16[4,8,7,16,128]{4,3,2,1,0:T(8,128)(2,1)S(1)} %get-tuple-element.46), channel_id=1, source_target_pairs={{0,8},{8,0},{1,9},{9,1},{2,10},{10,2},{3,11},{11,3},{4,12},{12,4},... | collective-permute-start | bytes 2752520 | tf_op jit(solution)/shard_map/ppermute | solution.py:438

commit v9 on v8

--- a/solution.py
+++ b/solution.py
@@ -174,7 +174,7 @@
     return [pick.astype(F32).astype(BF) for pick in picks], keep
 
 
-def top_kernel(me, near, halves, mine, theirs, out, held, sem):
+def top_kernel(me, near, halves, mine, theirs, out, held, full, sem):
     place = Place(me)
     first_core = place.core == 0
     load = pltpu.make_async_copy(near.at[jnp.bitwise_xor(place.y, NY - 1)], held, sem)
@@ -192,10 +192,11 @@
 
     for block in range(2 * NZ):
         k, pick = block // 4, far[block % 4]
-        full = [rows(dot(held[block], own[0]), dot(held[block], own[1]))]
-        full.append(rows(dot(halves[k], pick), dot(halves[count + k], pick)))
+        full[block, :ROWS] = rows(dot(held[block], own[0]), dot(held[block], own[1]))
+        full[block, ROWS:] = rows(dot(halves[k], pick), dot(halves[count + k], pick))
+    for block in range(2 * NZ):
         both = jnp.concatenate([mine[block], theirs[block]], axis=1)
-        out[block] = dot(both, jnp.concatenate(full, axis=0)).astype(BF)
+        out[block] = dot(both, full[block]).astype(BF)
 
 
 def top_grad(me, near, halves, mine, theirs):
@@ -204,8 +205,13 @@
         in_specs=[SCALARS, pl.BlockSpec(memory_space=pl.ANY)] + [WHOLE] * 3,
         out_specs=WHOLE,
         out_shape=jax.ShapeDtypeStruct(mine.shape, BF),
-        scratch_shapes=[pltpu.VMEM(near.shape[1:], BF), pltpu.SemaphoreType.DMA],
-        compiler_params=PARAMS,
+        scratch_shapes=[
+            pltpu.VMEM(near.shape[1:], BF),
+            pltpu.VMEM((2 * NZ, 2 * ROWS, ROWS), BF),
+            pltpu.SemaphoreType.DMA,
+        ],
+        compiler_params=PARAMS,
+        cost_estimate=pl.CostEstimate(flops=10**10, bytes_accessed=10**7, transcendentals=0),
         name="top_grad",
     )(me, near, halves, mine, theirs)
 

time: 190 us -> 190 us (level)
    ppermute x1, waiting for transfers between devices: 5.22 us -> 2.36 us  [per_device(): halves = lax.ppermute(top, 'x0', flips(2))]
  transfers between devices with their start and end apart: 9 -> 9, of which waited for: 5 -> 6; matrix products, arithmetic and copies ran while one was open for 2% -> 2% of each run, Pallas kernels for 3% -> 2%
where the time goes in v9:
time: 190 us; the launch traced here: 187 us
  blocking collectives  62.1 us (33%)
  waiting for transfers between devices  59.7 us (31%)
  starting transfers between devices  44.8 us (24%)
  Pallas kernels  15.5 us (8%)
  local copies, waits for them, and re-layouts  4.57 us (2%)
    all_to_all x1, waiting for transfers between devices, per_device(): lax.all_to_all(pack(me, upstream, factors.transpose(0, 2, 1)), ('z', 'cor...  44.8 us
    all_to_all x1, blocking collectives, per_device(): total = lax.all_to_all(total.reshape((2 * NZ,) + part), ('zh', 'z'), 0, 0)  35.5 us
    all_to_all x1, blocking collectives, per_device(): total = lax.all_to_all(total, 'y', 0, 0)  16.6 us
    all_to_all x1, starting transfers between devices, per_device(): lax.all_to_all(pack(me, upstream, factors.transpose(0, 2, 1)), ('z', 'cor...  12.8 us
    all_to_all x1, starting transfers between devices, per_device(): base = lax.all_to_all(base, ('z', 'core'), 0, 0)  11.6 us
    all_to_all x1, blocking collectives, per_device(): total = lax.all_to_all(total, ('x0', 'y'), 0, 0)  9.97 us
    ppermute x3, starting transfers between devices, per_device(): lax.ppermute(mixing, 'y', flips(NY, k))  9.82 us
    ppermute x3, waiting for transfers between devices, per_device(): lax.ppermute(mixing, 'y', flips(NY, k))  9.78 us
  transfers between devices with their start and end apart: 9, of which 6 were waited for; matrix products, arithmetic and copies ran while one was open for 2% of the time, Pallas kernels for 2%

profile of v9, /device:TPU:24, one launch (start us, length us, event | category | flops | bytes accessed | tf_op | source)
XLA Modules:
  0.0 186.9 jit_solution(6409293951198742195)
XLA Ops:
  0.0 2.6 %pack.1 = bf16[16,272,128]{2,1,0:T(8,128)(2,1)} custom-call(s32[1]{0:T(128)} %bitcast.me, bf16[128,3328]{1,0:T(8,128)(2,1)} %upstream.1, f32[7,64,128]{2,1,0:T(8,128)} %bitcast.12), custom_call_target="tpu_custom_call" | custom-call | tf_op jit(solution)/shard_map/pack/pallas_call | solution.py:107
  2.6 12.8 %all-to-all-start.1 = ((bf16[16,272,128]{2,1,0:T(8,128)(2,1)}), bf16[16,272,128]{2,1,0:T(8,128)(2,1)S(1)}, u32[]{:S(2)}, u32[]{:S(2)}) async-start(bf16[16,272,128]{2,1,0:T(8,128)(2,1)} %pack.1), calls=%async_computation.1 | async-start | bytes 2228224 | tf_op jit(solution)/shard_map/all_to_all | solution.py:430
  15.4 0.1 fusion
  15.6 1.3 copy.5
  16.9 44.8 %all-to-all-done.1 = bf16[16,272,128]{2,1,0:T(8,128)(2,1)S(1)} async-done(((bf16[16,272,128]{2,1,0:T(8,128)(2,1)}), bf16[16,272,128]{2,1,0:T(8,128)(2,1)S(1)}, u32[]{:S(2)}, u32[]{:S(2)}) %all-to-all-start.1) | async-done | bytes 1114144 | tf_op jit(solution)/shard_map/all_to_all | solution.py:430
  61.7 1.0 copy-done.1
  62.7 11.6 %all-to-all-start = ((bf16[16,208,128]{2,1,0:T(8,128)(2,1)}), bf16[16,208,128]{2,1,0:T(8,128)(2,1)S(1)}, u32[]{:S(2)}, u32[]{:S(2)}) async-start(bf16[16,208,128]{2,1,0:T(8,128)(2,1)} %bitcast.4), calls=%async_computation | async-start | bytes 1703936 | tf_op jit(solution)/shard_map/all_to_all | solution.py:434
  74.4 1.2 slice.9.mine.refs_7_.refs_13_
  75.6 3.4 %collective-permute-start.3 = (bf16[16,208,128]{2,1,0:T(8,128)(2,1)S(1)}, bf16[16,208,128]{2,1,0:T(8,128)(2,1)S(1)}, u32[]{:S(2)}, u32[]{:S(2)}) collective-permute-start(bf16[16,208,128]{2,1,0:T(8,128)(2,1)S(1)} %slice.9.mine.refs_7_.refs_13_), channel_id=1, source_target_pairs={{0,128},{128,0},{1,129},{129,1},{2,130},{130,2},{3,131},{131,3},{4... | collective-permute-start | bytes 2555912 | tf_op jit(solution)/shard_map/ppermute | solution.py:435
  79.0 1.0 slice.8.refs_0_
  80.0 2.1 %collective-permute-start.2 = (bf16[16,64,128]{2,1,0:T(8,128)(2,1)S(1)}, bf16[16,64,128]{2,1,0:T(8,128)(2,1)S(1)}, u32[]{:S(2)}, u32[]{:S(2)}) collective-permute-start(bf16[16,64,128]{2,1,0:T(8,128)(2,1)S(1)} %slice.8.refs_0_), channel_id=1, source_target_pairs={{0,3},{1,2},{2,1},{3,0},{4,7},{5,6},{6,5},{7,4},{8,11},{9,10},{10,... | collective-permute-start | bytes 786440 | tf_op jit(solution)/shard_map/ppermute | solution.py:437
  82.1 4.5 %collective-permute-start.1 = (bf16[16,64,128]{2,1,0:T(8,128)(2,1)S(1)}, bf16[16,64,128]{2,1,0:T(8,128)(2,1)S(1)}, u32[]{:S(2)}, u32[]{:S(2)}) collective-permute-start(bf16[16,64,128]{2,1,0:T(8,128)(2,1)S(1)} %slice.8.refs_0_), channel_id=1, source_target_pairs={{0,2},{1,3},{2,0},{3,1},{4,6},{5,7},{6,4},{7,5},{8,10},{9,11},{10,... | collective-permute-start | bytes 786440 | tf_op jit(solution)/shard_map/ppermute | solution.py:437
  86.6 3.2 %collective-permute-start = (bf16[16,64,128]{2,1,0:T(8,128)(2,1)S(1)}, bf16[16,64,128]{2,1,0:T(8,128)(2,1)S(1)}, u32[]{:S(2)}, u32[]{:S(2)}) collective-permute-start(bf16[16,64,128]{2,1,0:T(8,128)(2,1)S(1)} %slice.8.refs_0_), channel_id=1, source_target_pairs={{0,1},{1,0},{2,3},{3,2},{4,5},{5,4},{6,7},{7,6},{8,9},{9,8},{10,11... | collective-permute-start | bytes 786440 | tf_op jit(solution)/shard_map/ppermute | solution.py:437
  89.8 7.2 %collective-permute-done.2.refs_3_ = bf16[16,64,128]{2,1,0:T(8,128)(2,1)S(1)} collective-permute-done((bf16[16,64,128]{2,1,0:T(8,128)(2,1)S(1)}, bf16[16,64,128]{2,1,0:T(8,128)(2,1)S(1)}, u32[]{:S(2)}, u32[]{:S(2)}) %collective-permute-start.2) | collective-permute-done | bytes 262176 | tf_op jit(solution)/shard_map/ppermute | solution.py:437
  97.0 2.5 %collective-permute-done.refs_1_ = bf16[16,64,128]{2,1,0:T(8,128)(2,1)S(1)} collective-permute-done((bf16[16,64,128]{2,1,0:T(8,128)(2,1)S(1)}, bf16[16,64,128]{2,1,0:T(8,128)(2,1)S(1)}, u32[]{:S(2)}, u32[]{:S(2)}) %collective-permute-start) | collective-permute-done | bytes 262176 | tf_op jit(solution)/shard_map/ppermute | solution.py:437
  99.6 1.0 stack.1
  100.6 2.5 %collective-permute-start.5 = (bf16[8,64,128]{2,1,0:T(8,128)(2,1)S(1)}, bf16[8,64,128]{2,1,0:T(8,128)(2,1)S(1)}, u32[]{:S(2)}, u32[]{:S(2)}) collective-permute-start(bf16[8,64,128]{2,1,0:T(8,128)(2,1)S(1)} %get-tuple-element.33), channel_id=1, source_target_pairs={{0,128},{128,0},{1,129},{129,1},{2,130},{130,2},{3,131},{131,3},{4... | collective-permute-start | bytes 393224 | tf_op jit(solution)/shard_map/ppermute | solution.py:440
  103.2 1.9 %collective-permute-start.4 = (bf16[4,16,64,128]{3,2,1,0:T(8,128)(2,1)}, bf16[4,16,64,128]{3,2,1,0:T(8,128)(2,1)}, u32[]{:S(2)}, u32[]{:S(2)}) collective-permute-start(bf16[4,16,64,128]{3,2,1,0:T(8,128)(2,1)} %get-tuple-element.26.near), channel_id=1, source_target_pairs={{0,8},{8,0},{1,9},{9,1},{2,10},{10,2},{3,11},{11,3},{4,12},{12,4},... | collective-permute-start | bytes 3145736 | tf_op jit(solution)/shard_map/ppermute | solution.py:439
  105.1 2.4 %collective-permute-done.5.halves = bf16[8,64,128]{2,1,0:T(8,128)(2,1)S(1)} collective-permute-done((bf16[8,64,128]{2,1,0:T(8,128)(2,1)S(1)}, bf16[8,64,128]{2,1,0:T(8,128)(2,1)S(1)}, u32[]{:S(2)}, u32[]{:S(2)}) %collective-permute-start.5) | collective-permute-done | bytes 131104 | tf_op jit(solution)/shard_map/ppermute | solution.py:440
  107.5 2.2 %top_grad.1.refs_6_.refs_12_ = bf16[16,208,128]{2,1,0:T(8,128)(2,1)S(1)} custom-call(s32[1]{0:T(128)} %bitcast.me, bf16[4,16,64,128]{3,2,1,0:T(8,128)(2,1)} %get-tuple-element.26.near, bf16[8,64,128]{2,1,0:T(8,128)(2,1)S(1)} %collective-permute-done.5.halves, bf16[16,208,128]{2,1,0:T(8,128)(2,1)S(1)} %slice.9.mine.refs_7_.refs_13_, ...), custom_call_target="tpu_custom_call" | custom-call | flops 10000000000 | bytes 10000000 | tf_op jit(solution)/shard_map/top_grad/pallas_call | solution.py:203
  109.7 1.9 %all-to-all-done._.base = bf16[16,208,128]{2,1,0:T(8,128)(2,1)S(1)} async-done(((bf16[16,208,128]{2,1,0:T(8,128)(2,1)}), bf16[16,208,128]{2,1,0:T(8,128)(2,1)S(1)}, u32[]{:S(2)}, u32[]{:S(2)}) %all-to-all-start) | async-done | bytes 852000 | tf_op jit(solution)/shard_map/all_to_all | solution.py:434
  111.6 2.9 %expand.1 = (bf16[16,128,128]{2,1,0:T(8,128)(2,1)S(1)}, bf16[16,128,128]{2,1,0:T(8,128)(2,1)S(1)}, bf16[16,128,256]{2,1,0:T(8,128)(2,1)S(1)}, bf16[16,128,256]{2...) custom-call(s32[1]{0:T(128)} %bitcast.me, ...), custom_call_target="tpu_custom_call" | custom-call | tf_op jit(solution)/shard_map/expand/pallas_call | solution.py:260
  114.5 4.4 %chains.1 = (bf16[4,8,7,16,128]{4,3,2,1,0:T(8,128)(2,1)S(1)}, bf16[16,208,128]{2,1,0:T(8,128)(2,1)S(1)}, bf16[16,208,128]{2,1,0:T(8,128)(2,1)S(1)}, bf16[16,208,...) custom-call(s32[1]{0:T(128)} %bitcast.me, ...), custom_call_target="tpu_custom_call" | custom-call | tf_op jit(solution)/shard_map/chains/pallas_call | solution.py:361
  118.9 2.7 %collective-permute-start.6 = (bf16[4,8,7,16,128]{4,3,2,1,0:T(8,128)(2,1)S(1)}, bf16[4,8,7,16,128]{4,3,2,1,0:T(8,128)(2,1)S(1)}, u32[]{:S(2)}, u32[]{:S(2)}) collective-permute-start(bf16[4,8,7,16,128]{4,3,2,1,0:T(8,128)(2,1)S(1)} %get-tuple-element.46), channel_id=1, source_target_pairs={{0,8},{8,0},{1,9},{9,1},{2,10},{10,2},{3,11},{11,3},{4,12},{12,4},... | collective-permute-start | bytes 2752520 | tf_op jit(solution)/shard_map/ppermute | solution.py:444
  121.6 1.3 own_products.1.own
  122.9 0.8 collective-permute-done.6.got
  123.7 0.2 core_sum.1
  123.9 16.6 %all_to_all.25.parts = bf16[4,8,7,16,128]{4,3,2,1,0:T(8,128)(2,1)S(1)} all-to-all(bf16[4,8,7,16,128]{4,3,2,1,0:T(8,128)(2,1)S(1)} %core_sum.1), channel_id=1, replica_groups=mesh['x1'=2,'x0'=2,'z'=8,'core'=2,'zh'=2,'y'=4] {'y'}, dimensions={0} | all-to-all | bytes 1835008 | tf_op jit(solution)/shard_map/all_to_all | solution.py:449
  140.5 0.1 copies_of_sum.2
  140.6 35.5 %all_to_all.26.parts = bf16[16,7,16,128]{3,2,1,0:T(8,128)(2,1)S(1)} all-to-all(bf16[16,7,16,128]{3,2,1,0:T(8,128)(2,1)S(1)} %bitcast.11), channel_id=1, replica_groups=mesh['x1'=2,'x0'=2,'z'=8,'core'=2,'zh'=2,'y'=4] {'zh','z'}, dimensions={0} | all-to-all | bytes 917504 | tf_op jit(solution)/shard_map/all_to_all | solution.py:451
  176.2 10.0 %all_to_all.27.slices = bf16[8,7,16,128]{3,2,1,0:T(8,128)(2,1)S(1)} all-to-all(bf16[8,7,16,128]{3,2,1,0:T(8,128)(2,1)S(1)} %copies_of_sum.3), channel_id=1, replica_groups=mesh['x1'=2,'x0'=2,'z'=8,'core'=2,'zh'=2,'y'=4] {'x0','y'}, dimensions={0} | all-to-all | bytes 458752 | tf_op jit(solution)/shard_map/all_to_all | solution.py:453
  186.2 0.7 finish.1
  (10 shorter events, 0.2 us)
Async XLA Ops:
  0.0 15.4 %copy-start = (f32[1,26]{1,0:T(1,128)S(1)}, f32[1,26]{1,0:T(1,128)}, u32[]{:S(2)}) copy-start(f32[1,26]{1,0:T(1,128)} %param.5) | copy-start | bytes 316
  2.6 12.9 %copy-start.2 = (bf16[128,3328]{1,0:T(8,128)(2,1)S(1)}, bf16[128,3328]{1,0:T(8,128)(2,1)}, u32[]{:S(2)}) copy-start(bf16[128,3328]{1,0:T(8,128)(2,1)} %param.4) | copy-start | bytes 2555908
  2.6 59.1 %all-to-all-start.1 = ((bf16[16,272,128]{2,1,0:T(8,128)(2,1)}), bf16[16,272,128]{2,1,0:T(8,128)(2,1)S(1)}, u32[]{:S(2)}, u32[]{:S(2)}) async-start(bf16[16,272,128]{2,1,0:T(8,128)(2,1)} %pack.1), calls=%async_computation.1 | async-start | bytes 2228224 | tf_op jit(solution)/shard_map/all_to_all | solution.py:430
  61.7 1.0 copy-start.1
  62.7 48.8 %all-to-all-start = ((bf16[16,208,128]{2,1,0:T(8,128)(2,1)}), bf16[16,208,128]{2,1,0:T(8,128)(2,1)S(1)}, u32[]{:S(2)}, u32[]{:S(2)}) async-start(bf16[16,208,128]{2,1,0:T(8,128)(2,1)} %bitcast.4), calls=%async_computation | async-start | bytes 1703936 | tf_op jit(solution)/shard_map/all_to_all | solution.py:434
  75.6 24.0 %collective-permute-start.3 = (bf16[16,208,128]{2,1,0:T(8,128)(2,1)S(1)}, bf16[16,208,128]{2,1,0:T(8,128)(2,1)S(1)}, u32[]{:S(2)}, u32[]{:S(2)}) collective-permute-start(bf16[16,208,128]{2,1,0:T(8,128)(2,1)S(1)} %slice.9.mine.refs_7_.refs_13_), channel_id=1, source_target_pairs={{0,128},{128,0},{1,129},{129,1},{2,130},{130,2},{3,131},{131,3},{4... | collective-permute-start | bytes 2555912 | tf_op jit(solution)/shard_map/ppermute | solution.py:435
  80.0 17.1 %collective-permute-start.2 = (bf16[16,64,128]{2,1,0:T(8,128)(2,1)S(1)}, bf16[16,64,128]{2,1,0:T(8,128)(2,1)S(1)}, u32[]{:S(2)}, u32[]{:S(2)}) collective-permute-start(bf16[16,64,128]{2,1,0:T(8,128)(2,1)S(1)} %slice.8.refs_0_), channel_id=1, source_target_pairs={{0,3},{1,2},{2,1},{3,0},{4,7},{5,6},{6,5},{7,4},{8,11},{9,10},{10,... | collective-permute-start | bytes 786440 | tf_op jit(solution)/shard_map/ppermute | solution.py:437
  82.1 14.9 %collective-permute-start.1 = (bf16[16,64,128]{2,1,0:T(8,128)(2,1)S(1)}, bf16[16,64,128]{2,1,0:T(8,128)(2,1)S(1)}, u32[]{:S(2)}, u32[]{:S(2)}) collective-permute-start(bf16[16,64,128]{2,1,0:T(8,128)(2,1)S(1)} %slice.8.refs_0_), channel_id=1, source_target_pairs={{0,2},{1,3},{2,0},{3,1},{4,6},{5,7},{6,4},{7,5},{8,10},{9,11},{10,... | collective-permute-start | bytes 786440 | tf_op jit(solution)/shard_map/ppermute | solution.py:437
  86.6 13.0 %collective-permute-start = (bf16[16,64,128]{2,1,0:T(8,128)(2,1)S(1)}, bf16[16,64,128]{2,1,0:T(8,128)(2,1)S(1)}, u32[]{:S(2)}, u32[]{:S(2)}) collective-permute-start(bf16[16,64,128]{2,1,0:T(8,128)(2,1)S(1)} %slice.8.refs_0_), channel_id=1, source_target_pairs={{0,1},{1,0},{2,3},{3,2},{4,5},{5,4},{6,7},{7,6},{8,9},{9,8},{10,11... | collective-permute-start | bytes 786440 | tf_op jit(solution)/shard_map/ppermute | solution.py:437
  100.6 6.8 %collective-permute-start.5 = (bf16[8,64,128]{2,1,0:T(8,128)(2,1)S(1)}, bf16[8,64,128]{2,1,0:T(8,128)(2,1)S(1)}, u32[]{:S(2)}, u32[]{:S(2)}) collective-permute-start(bf16[8,64,128]{2,1,0:T(8,128)(2,1)S(1)} %get-tuple-element.33), channel_id=1, source_target_pairs={{0,128},{128,0},{1,129},{129,1},{2,130},{130,2},{3,131},{131,3},{4... | collective-permute-start | bytes 393224 | tf_op jit(solution)/shard_map/ppermute | solution.py:440
  103.2 8.4 %collective-permute-start.4 = (bf16[4,16,64,128]{3,2,1,0:T(8,128)(2,1)}, bf16[4,16,64,128]{3,2,1,0:T(8,128)(2,1)}, u32[]{:S(2)}, u32[]{:S(2)}) collective-permute-start(bf16[4,16,64,128]{3,2,1,0:T(8,128)(2,1)} %get-tuple-element.26.near), channel_id=1, source_target_pairs={{0,8},{8,0},{1,9},{9,1},{2,10},{10,2},{3,11},{11,3},{4,12},{12,4},... | collective-permute-start | bytes 3145736 | tf_op jit(solution)/shard_map/ppermute | solution.py:439
  118.9 4.8 %collective-permute-start.6 = (bf16[4,8,7,16,128]{4,3,2,1,0:T(8,128)(2,1)S(1)}, bf16[4,8,7,16,128]{4,3,2,1,0:T(8,128)(2,1)S(1)}, u32[]{:S(2)}, u32[]{:S(2)}) collective-permute-start(bf16[4,8,7,16,128]{4,3,2,1,0:T(8,128)(2,1)S(1)} %get-tuple-element.46), channel_id=1, source_target_pairs={{0,8},{8,0},{1,9},{9,1},{2,10},{10,2},{3,11},{11,3},{4,12},{12,4},... | collective-permute-start | bytes 2752520 | tf_op jit(solution)/shard_map/ppermute | solution.py:444
